TPU v7x, 32 devices: a whole 2x2x4 slice. The times are simulated.
32 devices in a mesh: section: 4 (over y, x), rep: 8 (over z, core).
Axes of the slice: x: 2, y: 2, z: 4, core: 2. Of those that a mesh axis runs over, the one named last changes fastest.
Arguments:
- section_state: float32 [4, 4, 8, 196, 512], P('section', None, 'rep'), may hold values from -6 to 6
- arriving: float32 [2, 4, 8, 196, 512], P(None, None, 'rep'), may hold values from -6 to 6
- first_weight: float32 [4, 1, 9, 512, 128], P('section'), may hold values from -0.1875 to 0.1875
- second_weight: float32 [4, 1, 9, 512, 128], P('section'), may hold values from -0.1875 to 0.1875
Outputs:
- returned: float32 [4, 4, 8, 196, 512], P('section', None, 'rep')
- first_grad: float32 [4, 1, 9, 512, 128], P('section', None, None, 'rep')
- second_grad: float32 [4, 1, 9, 512, 128], P('section', None, None, 'rep')
All inputs are finite; a program needn't handle non-finite values.
Results may differ from a plain program's by a relative error of at most 0.00019.
Values sent between devices are 32-bit elements; how exact they have to be, the bound alone decides.
No kernel may reach another device: no remote copies, remote signals or barrier semaphores. Data moves between devices by JAX's collectives and lax.ppermute only.
A program may use at most 128 MiB of HBM per device.

v0:
```python
import functools
import math

import jax
import jax.numpy as jnp
from jax import lax
from jax.experimental import pallas as pl
from jax.experimental.pallas import tpu as pltpu
from jax.sharding import PartitionSpec as P

F32, BF16 = jnp.float32, jnp.bfloat16
VMEM_LIMIT = 16 * 2**20
VMEM, HBM, ANY = pltpu.VMEM, pltpu.HBM, pl.ANY


def halves(value):
    high = value.astype(BF16)
    return high, (value - high.astype(F32)).astype(BF16)


def spread(taps, value, pitch):
    rows, width = value.shape
    for b in range(3):
        moved = value if b == 1 else pltpu.roll(value, 1 if b == 0 else rows - 1, 0)
        for k, half in enumerate(halves(moved)):
            low = (3 * k + b) * width
            taps[pitch : pitch + rows, low : low + width] = half


def conv(taps, packed, rows, pitch):
    total = None
    for a in range(3):
        filters = packed[a]
        part = jnp.dot(
            taps[a * pitch : a * pitch + rows, :], jnp.concatenate([filters, filters], axis=0), preferred_element_type=F32
        )
        total = part if total is None else total + part
    width = total.shape[1] // 2
    return total[:, :width] + total[:, width:]


def turn(value, depth):
    rows, width = value.shape
    high, low = halves(jnp.concatenate([value, jnp.zeros((depth - rows, width), F32)], axis=0).T)
    return jnp.concatenate([high, high, low], axis=1)


def step_kernel(dims, k_turn, tick, last, n_after, *refs):
    side, pitch, groups, width, shares = dims
    rows, pixels = side * pitch, side * side
    depth = -(-rows // 128) * 128
    first, lead, final = tick == 0, tick == 0 and n_after == 0, last and k_turn == 0
    refs = list(refs)
    take = lambda n: [refs.pop(0) for _ in range(n)]
    (info,) = take(1)
    if first:
        (state,) = take(1)
        filters = take(2 if lead else 1)
    else:
        moved, arriving, packed, sums_in = take(4)
    others = take(groups - 1) if final else []
    take(n_after)
    (out,) = take(1)
    if first:
        (packed,) = take(1)
        if lead:
            (kept,) = take(1)
    if last:
        grads = take(shares)
    else:
        (sums,) = take(1)
    plane, taps_one, taps_two, taps_error, sems = take(5)
    if lead:
        (weights,) = take(1)
    if not first:
        (held,) = take(1)
    if last:
        (sums,) = take(1)
    if final:
        (whole,) = take(1)

    group = lax.rem(info[0] + k_turn, groups)
    channels = pl.ds(pl.multiple_of(group * width, width), width)
    if lead:
        copies = [pltpu.make_async_copy(f.at[:, channels, :], weights.at[k], sems.at[k]) for k, f in enumerate(filters)]
        copies += [pltpu.make_async_copy(f, kept.at[k], sems.at[2 + k]) for k, f in enumerate(filters)]
        for copy in copies:
            copy.start()
    if not first:
        at_end = info[1] == 1
        from_end = pltpu.make_async_copy(arriving.at[tick - 1], held, sems.at[0])

        @pl.when(at_end)
        def _():
            from_end.start()

    for taps in (taps_one, taps_two, taps_error):
        taps[0:pitch, :] = jnp.zeros((pitch, 6 * width), BF16)
        low = pitch + rows
        taps[low:, :] = jnp.zeros((taps.shape[0] - low, 6 * width), BF16)
    for member in range(4):
        for r in range(side):
            plane[member, r * pitch + side : (r + 1) * pitch, :] = jnp.zeros((pitch - side, width), F32)

    def take_whole(source):
        for member in range(4):
            for r in range(side):
                plane[member, r * pitch : r * pitch + side, :] = source[
                    member, pl.ds(r * side * groups + group, side, stride=groups), :
                ]

    if first:
        take_whole(state)
    else:

        @pl.when(at_end)
        def _():
            from_end.wait()
            take_whole(held)

        @pl.when(jnp.logical_not(at_end))
        def _():
            for member in range(4):
                for r in range(side):
                    low = member * pixels + r * side
                    plane[member, r * pitch : r * pitch + side, :] = moved[low : low + side, :]

    inside = lax.rem(lax.broadcasted_iota(jnp.int32, (rows, width), 0), pitch) < side

    def branch(value):
        gate = 1.0 / (1.0 + jnp.exp(-value))
        return value * gate, gate * (1.0 + value * (1.0 - gate))

    leaving = []

    def give(member, value):
        if final:
            for slot, other in enumerate(others):
                theirs = lax.rem(info[0] + others_turns(groups)[slot], groups)
                whole[member, pl.ds(theirs, pixels, stride=groups), :] = other[member * pixels : (member + 1) * pixels, :]
        for r in range(side):
            piece = value[r * pitch : r * pitch + side, :]
            if final:
                whole[member, pl.ds(r * side * groups + group, side, stride=groups), :] = piece
            else:
                low = member * pixels + r * side
                out[low : low + side, :] = piece
        if final:
            copy = pltpu.make_async_copy(whole.at[member], out.at[member], sems.at[1 + member])
            copy.start()
            leaving.append(copy)

    def pack(k):
        for t in range(9):
            if lead:
                tap, mirror = weights[k, t], weights[k, 8 - t]
            else:
                tap, mirror = filters[0][k, t, channels, :], filters[0][k, 8 - t, channels, :]
            a, b = divmod(t, 3)
            packed[k, a, b * width : (b + 1) * width, :] = jnp.concatenate(halves(tap.T), axis=1)
            packed[2 + k, a, b * width : (b + 1) * width, :] = jnp.concatenate(halves(mirror), axis=1)

    spread(taps_one, plane[0], pitch)
    if first:
        if lead:
            copies[1].wait()
        pack(1)
    act, slope_two = branch(conv(taps_one, packed.at[1], rows, pitch))
    x_two = jnp.where(inside, plane[1] - act, 0.0)
    spread(taps_two, x_two, pitch)
    give(1, x_two)
    change_two = jnp.where(inside, plane[3] * slope_two, 0.0)
    spread(taps_error, change_two, pitch)
    d_one = jnp.where(inside, plane[2] + conv(taps_error, packed.at[3], rows, pitch), 0.0)
    give(2, d_one)
    if first:
        if lead:
            copies[0].wait()
        pack(0)
    act, slope_one = branch(conv(taps_two, packed.at[0], rows, pitch))
    give(0, plane[0] - act)
    change_one = jnp.where(inside, d_one * slope_one, 0.0)
    spread(taps_error, change_one, pitch)
    give(3, plane[3] + conv(taps_error, packed.at[2], rows, pitch))

    for k, (change, taps) in enumerate(((change_one, taps_two), (change_two, taps_one))):
        turned = turn(change, depth)
        for a in range(3):
            high = taps[a * pitch : a * pitch + depth, : 3 * width]
            low = taps[a * pitch : a * pitch + depth, 3 * width :]
            grad = jnp.dot(turned, jnp.concatenate([high, low, high], axis=0), preferred_element_type=F32)
            for b in range(3):
                tap = grad[:, b * width : (b + 1) * width]
                sums[k, 3 * a + b] = tap if first else tap + sums_in[k, 3 * a + b]
    if last:
        part = width // shares
        for d in range(shares):
            low = pl.multiple_of(lax.rem(info[2] + d, shares) * part, part)
            grads[d][...] = sums[:, :, pl.ds(low, part), :]
    if lead:
        copies[2].wait()
        copies[3].wait()
    for copy in leaving:
        copy.wait()


def others_turns(groups):
    return sorted(range(1, groups), key=lambda k: (-min(k, groups - k), k))


def step(dims, k_turn, tick, last, info, operands, after):
    side, pitch, groups, width, shares = dims
    pixels, rows = side * side, side * pitch
    depth = -(-rows // 128) * 128
    first, lead, final = tick == 0, tick == 0 and not after, last and k_turn == 0
    in_vmem = pl.BlockSpec(memory_space=VMEM)
    anywhere = pl.BlockSpec(memory_space=ANY)

    def local(array):
        return pltpu.with_memory_space_constraint(array, VMEM)

    def far(array):
        return pltpu.with_memory_space_constraint(array, HBM)

    sums = (2, 9, width, width)
    specs, args = [pl.BlockSpec(memory_space=pltpu.SMEM)], [info]

    def give(array, where, spec):
        args.append(where(array))
        specs.append(spec)

    if first:
        state, *filters = operands
        give(state, local, in_vmem)
        for f in filters:
            give(f, far if lead else local, anywhere if lead else in_vmem)
    else:
        moved, arriving, packed, before, *others = operands
        give(moved, lambda x: x, in_vmem)
        give(arriving, far, anywhere)
        for x in (packed, before, *others):
            give(x, local, in_vmem)
    for x in after:
        give(x, lambda x: x, anywhere)

    if final:
        out_shape, out_specs = [jax.ShapeDtypeStruct((4, pixels * groups, width), F32)], [anywhere]
    else:
        out_shape, out_specs = [VMEM((4 * pixels, width), F32)], [in_vmem]
    if first:
        out_shape.append(VMEM((4, 3, 3 * width, 2 * width), BF16))
        if lead:
            out_shape.append(VMEM((2, 9, groups * width, width), F32))
    if last:
        out_shape += [VMEM((2, 9, width // shares, width), F32)] * shares
    else:
        out_shape.append(VMEM(sums, F32))
    out_specs += [in_vmem] * (len(out_shape) - 1)

    scratch = [VMEM((4, rows, width), F32)] + [VMEM((2 * pitch + depth, 6 * width), BF16)] * 3 + [pltpu.SemaphoreType.DMA((6,))]
    if lead:
        scratch.append(VMEM(sums, F32))
    if not first:
        scratch.append(VMEM((4, pixels * groups, width), F32))
    if last:
        scratch.append(VMEM(sums, F32))
    if final:
        scratch.append(VMEM((4, pixels * groups, width), F32))
    return pl.pallas_call(
        functools.partial(step_kernel, dims, k_turn, tick, last, len(after)),
        out_shape=out_shape,
        in_specs=specs,
        out_specs=out_specs,
        scratch_shapes=scratch,
        compiler_params=pltpu.CompilerParams(vmem_limit_bytes=VMEM_LIMIT),
        cost_estimate=pl.CostEstimate(
            flops=6 * 2 * 9 * 4 * rows * width * width, bytes_accessed=6 * 2**20, transcendentals=2 * rows * width
        ),
        name=f"tick_{tick}_turn_{k_turn}",
    )(*args)


def add_kernel(n, *refs):
    for k, out in enumerate(refs[n:]):
        out[...] = functools.reduce(lambda x, y: x + y, [ref[k] for ref in refs[:n]])


def on_device(section_state, arriving, first_weight, second_weight):
    _, _, _, pixels, channels = section_state.shape
    width = first_weight.shape[-1]
    groups = channels // width
    side = math.isqrt(pixels)
    pitch = -(-(side + 1) // 16) * 16
    sections, reps = lax.axis_size("section"), lax.axis_size("rep")
    shares = reps // groups
    dims = (side, pitch, groups, width, shares)
    ticks = arriving.shape[0] + 1

    state = section_state[0].reshape(4, pixels * groups, width)
    arrivals = arriving.reshape(ticks - 1, 4, pixels * groups, width)
    filters = (first_weight[0, 0], second_weight[0, 0])

    rep = lax.axis_index("rep")
    at_end = lax.axis_index("section") == sections - 1
    info = jnp.stack([rep // shares, at_end.astype(jnp.int32), rep % shares]).astype(jnp.int32)

    turns = others_turns(groups) + [0]
    down = [(s, s - 1) for s in range(1, sections)]
    moved, packed, sums, outs, totals, waiting = {}, {}, {}, {}, {}, {}

    def gather_shares(parts):
        total = parts[0]
        for d in range(1, shares):
            total = total + lax.ppermute(parts[d], "rep", [(r, r - r % shares + (r % shares + d) % shares) for r in range(reps)])
        return total

    order = sorted(((t, p) for t in range(ticks) for p in range(groups)), key=lambda i: (i[1] + 2 * i[0], -i[0]))
    for n, (tick, p) in enumerate(order):
        k, last = turns[p], tick == ticks - 1
        after = waiting.pop(n, [])
        if tick == 0:
            results = list(step(dims, k, tick, last, info, (state, *filters), after))
            if n == 0:
                filters = (results.pop(2),)
            out, packed[p], *grads = results
        else:
            others = [outs[o] for o in range(p)] if last and k == 0 else []
            out, *grads = step(dims, k, tick, last, info, (moved[p], arrivals, packed[p], sums[p], *others), after)
        waiting.setdefault(n + 1, []).append(out)
        if not last:
            sums[p] = grads[0]
            moved[p] = lax.ppermute(out, "section", down)
            continue
        outs[p] = out
        if k:
            total = gather_shares(grads)
            waiting.setdefault(min(n + 2, len(order) - 1), []).append(total)
            totals[p] = [lax.ppermute(total, "rep", [(r, (r + k * shares) % reps) for r in range(reps)])]
        else:
            totals[p] = [grads[0]] + [
                lax.ppermute(grads[d], "rep", [(r, r - r % shares + (r % shares + d) % shares) for r in range(reps)])
                for d in range(1, shares)
            ]

    terms = [x for p in range(groups) for x in totals[p]]
    part = terms[0].shape[1:]
    first_grad, second_grad = pl.pallas_call(
        functools.partial(add_kernel, len(terms)),
        out_shape=[jax.ShapeDtypeStruct(part, F32)] * 2,
        in_specs=[pl.BlockSpec(memory_space=VMEM)] * len(terms),
        out_specs=[pl.BlockSpec(memory_space=VMEM)] * 2,
        compiler_params=pltpu.CompilerParams(vmem_limit_bytes=VMEM_LIMIT),
        name="add_gradients",
    )(*terms)
    returned = outs[groups - 1].reshape(1, 4, 1, pixels, channels)
    return (returned, first_grad[None, None], second_grad[None, None])


def solution(mesh):
    return jax.shard_map(
        on_device,
        mesh=mesh,
        in_specs=(
            P("section", None, "rep", None, None),
            P(None, None, "rep", None, None),
            P("section", None, None, None, None),
            P("section", None, None, None, None),
        ),
        out_specs=(
            P("section", None, "rep", None, None),
            P("section", None, None, "rep", None),
            P("section", None, None, "rep", None),
        ),
        check_vma=False,
    )
```

profile of v0, /device:TPU:20, one launch (start us, length us, event | category | flops | bytes accessed | tf_op | source)
XLA Modules:
  0.0 155.7 jit_solution(3347148026039855703)
XLA Ops:
  0.7 0.1 pad_add_fusion.refs_0_
  0.7 1.4 copy-done
  2.1 5.6 %tick_0_turn_2.1 = (f32[784,128]{1,0:T(8,128)S(1)}, bf16[4,3,384,256]{3,2,1,0:T(8,128)(2,1)S(1)}, f32[2,9,512,128]{3,2,1,0:T(8,128)S(1)}, f32[2,9,128,128]{3,2,1,0:T(8,128)S(1)}) custom-call(s32[3]{0:T(128)S(1)} %pad_add_fusion.refs_0_, f32[4,784,128]{2,1,0:T(8,128)S(1)} %bitcast.10, f32[9,512,128]{2,1,0:T(8,128)} %bitcast.22, f32[9,512,128]{2,1,0:T(8,128)} %bitcast.23), custom_call_target="tpu_custom_call" | custom-call | flops 1585446912 | bytes 6291456 | tf_op jit(solution)/shard_map/tick_0_turn_2/pallas_call | solution.py:269
  7.7 3.3 %collective-permute-start.1 = (f32[784,128]{1,0:T(8,128)S(1)}, f32[784,128]{1,0:T(8,128)S(1)}, u32[]{:S(2)}, u32[]{:S(2)}) collective-permute-start(f32[784,128]{1,0:T(8,128)S(1)} %get-tuple-element.39.refs_3_), channel_id=1, source_target_pairs={{8,0},{16,8},{24,16},{9,1},{17,9},{25,17},{10,2},{18,10},{26,18},{... | collective-permute-start | bytes 1204232 | tf_op jit(solution)/shard_map/ppermute | solution.py:332
  11.1 3.6 %tick_0_turn_1.1 = (f32[784,128]{1,0:T(8,128)S(1)}, bf16[4,3,384,256]{3,2,1,0:T(8,128)(2,1)S(1)}, f32[2,9,128,128]{3,2,1,0:T(8,128)S(1)}) custom-call(s32[3]{0:T(128)S(1)} %pad_add_fusion.refs_0_, f32[4,784,128]{2,1,0:T(8,128)S(1)} %bitcast.11, f32[2,9,512,128]{3,2,1,0:T(8,128)S(1)} %get-tuple-element.38.refs_2_, f32[784,128]{1,0:T(8,128)S(1)} %get-tuple-element.39.refs_3_), custom_call_target="tpu_custom_call" | custom-call | flops 1585446912 | bytes 6291456 | tf_op jit(solution)/shard_map/tick_0_turn_1/pallas_call | solution.py:269
  14.7 2.4 %collective-permute-start = (f32[784,128]{1,0:T(8,128)S(1)}, f32[784,128]{1,0:T(8,128)S(1)}, u32[]{:S(2)}, u32[]{:S(2)}) collective-permute-start(f32[784,128]{1,0:T(8,128)S(1)} %get-tuple-element.40.refs_5_), channel_id=1, source_target_pairs={{8,0},{16,8},{24,16},{9,1},{17,9},{25,17},{10,2},{18,10},{26,18},{... | collective-permute-start | bytes 1204232 | tf_op jit(solution)/shard_map/ppermute | solution.py:332
  17.1 4.7 %collective-permute-done.1.refs_1_ = f32[784,128]{1,0:T(8,128)S(1)} collective-permute-done((f32[784,128]{1,0:T(8,128)S(1)}, f32[784,128]{1,0:T(8,128)S(1)}, u32[]{:S(2)}, u32[]{:S(2)}) %collective-permute-start.1) | collective-permute-done | bytes 401440 | tf_op jit(solution)/shard_map/ppermute | solution.py:332
  21.8 3.5 %tick_1_turn_2.1 = (f32[784,128]{1,0:T(8,128)S(1)}, f32[2,9,128,128]{3,2,1,0:T(8,128)S(1)}) custom-call(s32[3]{0:T(128)S(1)} %pad_add_fusion.refs_0_, f32[784,128]{1,0:T(8,128)S(1)} %collective-permute-done.1.refs_1_, f32[2,4,784,128]{3,2,1,0:T(8,128)} %bitcast.14, bf16[4,3,384,256]{3,2,1,0:T(8,128)(2,1)S(1)} %get-tuple-element.43.refs_3_, ...), custom_call_target="tpu_custom_call" | custom-call | flops 1585446912 | bytes 6291456 | tf_op jit(solution)/shard_map/tick_1_turn_2/pallas_call | solution.py:269
  25.3 4.2 %collective-permute-start.4 = (f32[784,128]{1,0:T(8,128)S(1)}, f32[784,128]{1,0:T(8,128)S(1)}, u32[]{:S(2)}, u32[]{:S(2)}) collective-permute-start(f32[784,128]{1,0:T(8,128)S(1)} %get-tuple-element.45.refs_3_), channel_id=1, source_target_pairs={{8,0},{16,8},{24,16},{9,1},{17,9},{25,17},{10,2},{18,10},{26,18},{... | collective-permute-start | bytes 1204232 | tf_op jit(solution)/shard_map/ppermute | solution.py:332
  29.6 3.6 %tick_0_turn_3.1 = (f32[784,128]{1,0:T(8,128)S(1)}, bf16[4,3,384,256]{3,2,1,0:T(8,128)(2,1)S(1)}, f32[2,9,128,128]{3,2,1,0:T(8,128)S(1)}) custom-call(s32[3]{0:T(128)S(1)} %pad_add_fusion.refs_0_, f32[4,784,128]{2,1,0:T(8,128)S(1)} %bitcast.12, f32[2,9,512,128]{3,2,1,0:T(8,128)S(1)} %get-tuple-element.38.refs_2_, f32[784,128]{1,0:T(8,128)S(1)} %get-tuple-element.45.refs_3_), custom_call_target="tpu_custom_call" | custom-call | flops 1585446912 | bytes 6291456 | tf_op jit(solution)/shard_map/tick_0_turn_3/pallas_call | solution.py:269
  33.2 0.0 collective-permute-done.refs_1_
  33.2 3.7 %tick_1_turn_1.1 = (f32[784,128]{1,0:T(8,128)S(1)}, f32[2,9,128,128]{3,2,1,0:T(8,128)S(1)}) custom-call(s32[3]{0:T(128)S(1)} %pad_add_fusion.refs_0_, f32[784,128]{1,0:T(8,128)S(1)} %collective-permute-done.refs_1_, f32[2,4,784,128]{3,2,1,0:T(8,128)} %bitcast.15, bf16[4,3,384,256]{3,2,1,0:T(8,128)(2,1)S(1)} %get-tuple-element.41.refs_3_, ...), custom_call_target="tpu_custom_call" | custom-call | flops 1585446912 | bytes 6291456 | tf_op jit(solution)/shard_map/tick_1_turn_1/pallas_call | solution.py:269
  36.9 3.6 %tick_0_turn_0.1 = (f32[784,128]{1,0:T(8,128)S(1)}, bf16[4,3,384,256]{3,2,1,0:T(8,128)(2,1)S(1)}, f32[2,9,128,128]{3,2,1,0:T(8,128)S(1)}) custom-call(s32[3]{0:T(128)S(1)} %pad_add_fusion.refs_0_, f32[4,784,128]{2,1,0:T(8,128)S(1)} %bitcast.13, f32[2,9,512,128]{3,2,1,0:T(8,128)S(1)} %get-tuple-element.38.refs_2_, f32[784,128]{1,0:T(8,128)S(1)} %get-tuple-element.47.refs_3_), custom_call_target="tpu_custom_call" | custom-call | flops 1585446912 | bytes 6291456 | tf_op jit(solution)/shard_map/tick_0_turn_0/pallas_call | solution.py:269
  40.5 0.0 collective-permute-done.4.refs_1_
  40.5 3.7 %tick_2_turn_2.1 = (f32[784,128]{1,0:T(8,128)S(1)}, f32[2,9,64,128]{3,2,1,0:T(8,128)S(1)}, f32[2,9,64,128]{3,2,1,0:T(8,128)S(1)}) custom-call(s32[3]{0:T(128)S(1)} %pad_add_fusion.refs_0_, f32[784,128]{1,0:T(8,128)S(1)} %collective-permute-done.4.refs_1_, f32[2,4,784,128]{3,2,1,0:T(8,128)} %bitcast.16, ...), custom_call_target="tpu_custom_call" | custom-call | flops 1585446912 | bytes 6291456 | tf_op jit(solution)/shard_map/tick_2_turn_2/pallas_call | solution.py:269
  44.2 0.1 collective-permute-start.5
  44.3 1.9 %collective-permute-start.6 = (f32[784,128]{1,0:T(8,128)S(1)}, f32[784,128]{1,0:T(8,128)S(1)}, u32[]{:S(2)}, u32[]{:S(2)}) collective-permute-start(f32[784,128]{1,0:T(8,128)S(1)} %get-tuple-element.46.refs_5_), channel_id=1, source_target_pairs={{8,0},{16,8},{24,16},{9,1},{17,9},{25,17},{10,2},{18,10},{26,18},{... | collective-permute-start | bytes 1204232 | tf_op jit(solution)/shard_map/ppermute | solution.py:332
  46.2 1.9 %collective-permute-start.3 = (f32[784,128]{1,0:T(8,128)S(1)}, f32[784,128]{1,0:T(8,128)S(1)}, u32[]{:S(2)}, u32[]{:S(2)}) collective-permute-start(f32[784,128]{1,0:T(8,128)S(1)} %get-tuple-element.47.refs_3_), channel_id=1, source_target_pairs={{8,0},{16,8},{24,16},{9,1},{17,9},{25,17},{10,2},{18,10},{26,18},{... | collective-permute-start | bytes 1204232 | tf_op jit(solution)/shard_map/ppermute | solution.py:332
  48.1 10.2 %collective-permute-done.6.refs_1_ = f32[784,128]{1,0:T(8,128)S(1)} collective-permute-done((f32[784,128]{1,0:T(8,128)S(1)}, f32[784,128]{1,0:T(8,128)S(1)}, u32[]{:S(2)}, u32[]{:S(2)}) %collective-permute-start.6) | collective-permute-done | bytes 401440 | tf_op jit(solution)/shard_map/ppermute | solution.py:332
  58.3 3.5 %tick_1_turn_3.1 = (f32[784,128]{1,0:T(8,128)S(1)}, f32[2,9,128,128]{3,2,1,0:T(8,128)S(1)}) custom-call(s32[3]{0:T(128)S(1)} %pad_add_fusion.refs_0_, f32[784,128]{1,0:T(8,128)S(1)} %collective-permute-done.6.refs_1_, f32[2,4,784,128]{3,2,1,0:T(8,128)} %bitcast.17, bf16[4,3,384,256]{3,2,1,0:T(8,128)(2,1)S(1)} %get-tuple-element.55.refs_3_, ...), custom_call_target="tpu_custom_call" | custom-call | flops 1585446912 | bytes 6291456 | tf_op jit(solution)/shard_map/tick_1_turn_3/pallas_call | solution.py:269
  61.8 0.0 collective-permute-done.5
  61.8 0.1 add.15.refs_5_
  61.9 4.7 %collective-permute-done.3.refs_1_ = f32[784,128]{1,0:T(8,128)S(1)} collective-permute-done((f32[784,128]{1,0:T(8,128)S(1)}, f32[784,128]{1,0:T(8,128)S(1)}, u32[]{:S(2)}, u32[]{:S(2)}) %collective-permute-start.3) | collective-permute-done | bytes 401440 | tf_op jit(solution)/shard_map/ppermute | solution.py:332
  66.6 3.9 %tick_2_turn_1.1 = (f32[784,128]{1,0:T(8,128)S(1)}, f32[2,9,64,128]{3,2,1,0:T(8,128)S(1)}, f32[2,9,64,128]{3,2,1,0:T(8,128)S(1)}) custom-call(s32[3]{0:T(128)S(1)} %pad_add_fusion.refs_0_, f32[784,128]{1,0:T(8,128)S(1)} %collective-permute-done.3.refs_1_, f32[2,4,784,128]{3,2,1,0:T(8,128)} %bitcast.18, ...), custom_call_target="tpu_custom_call" | custom-call | flops 1585446912 | bytes 6291456 | tf_op jit(solution)/shard_map/tick_2_turn_1/pallas_call | solution.py:269
  70.6 0.1 collective-permute-start.9
  70.7 2.9 %collective-permute-start.2 = (f32[784,128]{1,0:T(8,128)S(1)}, f32[784,128]{1,0:T(8,128)S(1)}, u32[]{:S(2)}, u32[]{:S(2)}) collective-permute-start(f32[784,128]{1,0:T(8,128)S(1)} %get-tuple-element.48.refs_5_), channel_id=1, source_target_pairs={{8,0},{16,8},{24,16},{9,1},{17,9},{25,17},{10,2},{18,10},{26,18},{... | collective-permute-start | bytes 1204232 | tf_op jit(solution)/shard_map/ppermute | solution.py:332
  73.6 1.9 %collective-permute-start.8 = (f32[784,128]{1,0:T(8,128)S(1)}, f32[784,128]{1,0:T(8,128)S(1)}, u32[]{:S(2)}, u32[]{:S(2)}) collective-permute-start(f32[784,128]{1,0:T(8,128)S(1)} %get-tuple-element.58.refs_6_), channel_id=1, source_target_pairs={{8,0},{16,8},{24,16},{9,1},{17,9},{25,17},{10,2},{18,10},{26,18},{... | collective-permute-start | bytes 1204232 | tf_op jit(solution)/shard_map/ppermute | solution.py:332
  75.5 9.2 %collective-permute-done.2.refs_1_ = f32[784,128]{1,0:T(8,128)S(1)} collective-permute-done((f32[784,128]{1,0:T(8,128)S(1)}, f32[784,128]{1,0:T(8,128)S(1)}, u32[]{:S(2)}, u32[]{:S(2)}) %collective-permute-start.2) | collective-permute-done | bytes 401440 | tf_op jit(solution)/shard_map/ppermute | solution.py:332
  84.6 3.5 %tick_1_turn_0.1 = (f32[784,128]{1,0:T(8,128)S(1)}, f32[2,9,128,128]{3,2,1,0:T(8,128)S(1)}) custom-call(s32[3]{0:T(128)S(1)} %pad_add_fusion.refs_0_, f32[784,128]{1,0:T(8,128)S(1)} %collective-permute-done.2.refs_1_, f32[2,4,784,128]{3,2,1,0:T(8,128)} %bitcast.19, bf16[4,3,384,256]{3,2,1,0:T(8,128)(2,1)S(1)} %get-tuple-element.49.refs_3_, ...), custom_call_target="tpu_custom_call" | custom-call | flops 1585446912 | bytes 6291456 | tf_op jit(solution)/shard_map/tick_1_turn_0/pallas_call | solution.py:269
  88.1 0.0 collective-permute-done.9
  88.2 0.1 add.16.refs_5_
  88.2 4.6 %collective-permute-done.8.refs_1_ = f32[784,128]{1,0:T(8,128)S(1)} collective-permute-done((f32[784,128]{1,0:T(8,128)S(1)}, f32[784,128]{1,0:T(8,128)S(1)}, u32[]{:S(2)}, u32[]{:S(2)}) %collective-permute-start.8) | collective-permute-done | bytes 401440 | tf_op jit(solution)/shard_map/ppermute | solution.py:332
  92.8 3.7 %tick_2_turn_3.1 = (f32[784,128]{1,0:T(8,128)S(1)}, f32[2,9,64,128]{3,2,1,0:T(8,128)S(1)}, f32[2,9,64,128]{3,2,1,0:T(8,128)S(1)}) custom-call(s32[3]{0:T(128)S(1)} %pad_add_fusion.refs_0_, f32[784,128]{1,0:T(8,128)S(1)} %collective-permute-done.8.refs_1_, f32[2,4,784,128]{3,2,1,0:T(8,128)} %bitcast.20, ...), custom_call_target="tpu_custom_call" | custom-call | flops 1585446912 | bytes 6291456 | tf_op jit(solution)/shard_map/tick_2_turn_3/pallas_call | solution.py:269
  96.5 0.1 collective-permute-start.10
  96.6 3.8 %collective-permute-start.7 = (f32[784,128]{1,0:T(8,128)S(1)}, f32[784,128]{1,0:T(8,128)S(1)}, u32[]{:S(2)}, u32[]{:S(2)}) collective-permute-start(f32[784,128]{1,0:T(8,128)S(1)} %get-tuple-element.60.refs_6_), channel_id=1, source_target_pairs={{8,0},{16,8},{24,16},{9,1},{17,9},{25,17},{10,2},{18,10},{26,18},{... | collective-permute-start | bytes 1204232 | tf_op jit(solution)/shard_map/ppermute | solution.py:332
  100.4 0.4 collective-permute-start.11
  100.8 1.6 %collective-permute-start.12 = (f32[2,9,64,128]{3,2,1,0:T(8,128)S(1)}, f32[2,9,64,128]{3,2,1,0:T(8,128)S(1)}, u32[]{:S(2)}, u32[]{:S(2)}) collective-permute-start(f32[2,9,64,128]{3,2,1,0:T(8,128)S(1)} %add.16.refs_5_), channel_id=1, source_target_pairs={{0,2},{1,3},{2,4},{3,5},{4,6},{5,7},{6,0},{7,1},{8,10},{9,11},{10,... | collective-permute-start | bytes 1769480 | tf_op jit(solution)/shard_map/ppermute | solution.py:338
  102.4 0.0 collective-permute-done.10
  102.4 0.1 add.17.refs_9_
  102.5 7.7 %collective-permute-done.7.refs_1_ = f32[784,128]{1,0:T(8,128)S(1)} collective-permute-done((f32[784,128]{1,0:T(8,128)S(1)}, f32[784,128]{1,0:T(8,128)S(1)}, u32[]{:S(2)}, u32[]{:S(2)}) %collective-permute-start.7) | collective-permute-done | bytes 401440 | tf_op jit(solution)/shard_map/ppermute | solution.py:332
  110.2 3.8 %tick_2_turn_0.1 = (f32[4,784,128]{2,1,0:T(8,128)}, f32[2,9,64,128]{3,2,1,0:T(8,128)S(1)}, f32[2,9,64,128]{3,2,1,0:T(8,128)S(1)}) custom-call(s32[3]{0:T(128)S(1)} %pad_add_fusion.refs_0_, f32[784,128]{1,0:T(8,128)S(1)} %collective-permute-done.7.refs_1_, f32[2,4,784,128]{3,2,1,0:T(8,128)} %bitcast.21, ...), custom_call_target="tpu_custom_call" | custom-call | flops 1585446912 | bytes 6291456 | tf_op jit(solution)/shard_map/tick_2_turn_0/pallas_call | solution.py:269
  113.9 0.1 collective-permute-start.14
  114.0 0.5 collective-permute-start.13
  114.5 25.3 %collective-permute-done.11.refs_0_ = f32[2,9,64,128]{3,2,1,0:T(8,128)S(1)} collective-permute-done((f32[2,9,64,128]{3,2,1,0:T(8,128)S(1)}, f32[2,9,64,128]{3,2,1,0:T(8,128)S(1)}, u32[]{:S(2)}, u32[]{:S(2)}) %collective-permute-start.11) | collective-permute-done | bytes 589856 | tf_op jit(solution)/shard_map/ppermute | solution.py:338
  139.8 14.9 %collective-permute-done.12.refs_1_ = f32[2,9,64,128]{3,2,1,0:T(8,128)S(1)} collective-permute-done((f32[2,9,64,128]{3,2,1,0:T(8,128)S(1)}, f32[2,9,64,128]{3,2,1,0:T(8,128)S(1)}, u32[]{:S(2)}, u32[]{:S(2)}) %collective-permute-start.12) | collective-permute-done | bytes 589856 | tf_op jit(solution)/shard_map/ppermute | solution.py:338
  154.7 0.0 collective-permute-done.14.refs_4_
  154.7 0.0 collective-permute-done.13.refs_2_
  154.7 1.0 add_gradients.1
  (3 shorter events, 0.0 us)
Async XLA Ops:
  0.7 1.4 copy-start
  7.7 14.1 %collective-permute-start.1 = (f32[784,128]{1,0:T(8,128)S(1)}, f32[784,128]{1,0:T(8,128)S(1)}, u32[]{:S(2)}, u32[]{:S(2)}) collective-permute-start(f32[784,128]{1,0:T(8,128)S(1)} %get-tuple-element.39.refs_3_), channel_id=1, source_target_pairs={{8,0},{16,8},{24,16},{9,1},{17,9},{25,17},{10,2},{18,10},{26,18},{... | collective-permute-start | bytes 1204232 | tf_op jit(solution)/shard_map/ppermute | solution.py:332
  14.7 18.5 %collective-permute-start = (f32[784,128]{1,0:T(8,128)S(1)}, f32[784,128]{1,0:T(8,128)S(1)}, u32[]{:S(2)}, u32[]{:S(2)}) collective-permute-start(f32[784,128]{1,0:T(8,128)S(1)} %get-tuple-element.40.refs_5_), channel_id=1, source_target_pairs={{8,0},{16,8},{24,16},{9,1},{17,9},{25,17},{10,2},{18,10},{26,18},{... | collective-permute-start | bytes 1204232 | tf_op jit(solution)/shard_map/ppermute | solution.py:332
  21.8 7.8 %copy-start.1 = (f32[1,4,1,196,512]{4,2,3,1,0:T(1,128)S(1)}, f32[1,4,1,196,512]{4,2,3,1,0:T(1,128)}, u32[]{:S(2)}) copy-start(f32[1,4,1,196,512]{4,2,3,1,0:T(1,128)} %param.4) | copy-start | bytes 4816900
  25.3 15.2 %collective-permute-start.4 = (f32[784,128]{1,0:T(8,128)S(1)}, f32[784,128]{1,0:T(8,128)S(1)}, u32[]{:S(2)}, u32[]{:S(2)}) collective-permute-start(f32[784,128]{1,0:T(8,128)S(1)} %get-tuple-element.45.refs_3_), channel_id=1, source_target_pairs={{8,0},{16,8},{24,16},{9,1},{17,9},{25,17},{10,2},{18,10},{26,18},{... | collective-permute-start | bytes 1204232 | tf_op jit(solution)/shard_map/ppermute | solution.py:332
  44.2 17.7 %collective-permute-start.5 = (f32[2,9,64,128]{3,2,1,0:T(8,128)S(1)}, f32[2,9,64,128]{3,2,1,0:T(8,128)S(1)}, u32[]{:S(2)}, u32[]{:S(2)}) collective-permute-start(f32[2,9,64,128]{3,2,1,0:T(8,128)S(1)} %get-tuple-element.54), channel_id=1, source_target_pairs={{0,1},{1,0},{2,3},{3,2},{4,5},{5,4},{6,7},{7,6},{8,9},{9,8},{10,11... | collective-permute-start | bytes 1769480 | tf_op jit(solution)/shard_map/ppermute | solution.py:314
  44.3 14.1 %collective-permute-start.6 = (f32[784,128]{1,0:T(8,128)S(1)}, f32[784,128]{1,0:T(8,128)S(1)}, u32[]{:S(2)}, u32[]{:S(2)}) collective-permute-start(f32[784,128]{1,0:T(8,128)S(1)} %get-tuple-element.46.refs_5_), channel_id=1, source_target_pairs={{8,0},{16,8},{24,16},{9,1},{17,9},{25,17},{10,2},{18,10},{26,18},{... | collective-permute-start | bytes 1204232 | tf_op jit(solution)/shard_map/ppermute | solution.py:332
  46.2 20.4 %collective-permute-start.3 = (f32[784,128]{1,0:T(8,128)S(1)}, f32[784,128]{1,0:T(8,128)S(1)}, u32[]{:S(2)}, u32[]{:S(2)}) collective-permute-start(f32[784,128]{1,0:T(8,128)S(1)} %get-tuple-element.47.refs_3_), channel_id=1, source_target_pairs={{8,0},{16,8},{24,16},{9,1},{17,9},{25,17},{10,2},{18,10},{26,18},{... | collective-permute-start | bytes 1204232 | tf_op jit(solution)/shard_map/ppermute | solution.py:332
  70.6 17.6 %collective-permute-start.9 = (f32[2,9,64,128]{3,2,1,0:T(8,128)S(1)}, f32[2,9,64,128]{3,2,1,0:T(8,128)S(1)}, u32[]{:S(2)}, u32[]{:S(2)}) collective-permute-start(f32[2,9,64,128]{3,2,1,0:T(8,128)S(1)} %get-tuple-element.64), channel_id=1, source_target_pairs={{0,1},{1,0},{2,3},{3,2},{4,5},{5,4},{6,7},{7,6},{8,9},{9,8},{10,11... | collective-permute-start | bytes 1769480 | tf_op jit(solution)/shard_map/ppermute | solution.py:314
  70.7 14.0 %collective-permute-start.2 = (f32[784,128]{1,0:T(8,128)S(1)}, f32[784,128]{1,0:T(8,128)S(1)}, u32[]{:S(2)}, u32[]{:S(2)}) collective-permute-start(f32[784,128]{1,0:T(8,128)S(1)} %get-tuple-element.48.refs_5_), channel_id=1, source_target_pairs={{8,0},{16,8},{24,16},{9,1},{17,9},{25,17},{10,2},{18,10},{26,18},{... | collective-permute-start | bytes 1204232 | tf_op jit(solution)/shard_map/ppermute | solution.py:332
  73.6 19.3 %collective-permute-start.8 = (f32[784,128]{1,0:T(8,128)S(1)}, f32[784,128]{1,0:T(8,128)S(1)}, u32[]{:S(2)}, u32[]{:S(2)}) collective-permute-start(f32[784,128]{1,0:T(8,128)S(1)} %get-tuple-element.58.refs_6_), channel_id=1, source_target_pairs={{8,0},{16,8},{24,16},{9,1},{17,9},{25,17},{10,2},{18,10},{26,18},{... | collective-permute-start | bytes 1204232 | tf_op jit(solution)/shard_map/ppermute | solution.py:332
  96.5 5.9 %collective-permute-start.10 = (f32[2,9,64,128]{3,2,1,0:T(8,128)S(1)}, f32[2,9,64,128]{3,2,1,0:T(8,128)S(1)}, u32[]{:S(2)}, u32[]{:S(2)}) collective-permute-start(f32[2,9,64,128]{3,2,1,0:T(8,128)S(1)} %get-tuple-element.67), channel_id=1, source_target_pairs={{0,1},{1,0},{2,3},{3,2},{4,5},{5,4},{6,7},{7,6},{8,9},{9,8},{10,11... | collective-permute-start | bytes 1769480 | tf_op jit(solution)/shard_map/ppermute | solution.py:314
  96.6 13.6 %collective-permute-start.7 = (f32[784,128]{1,0:T(8,128)S(1)}, f32[784,128]{1,0:T(8,128)S(1)}, u32[]{:S(2)}, u32[]{:S(2)}) collective-permute-start(f32[784,128]{1,0:T(8,128)S(1)} %get-tuple-element.60.refs_6_), channel_id=1, source_target_pairs={{8,0},{16,8},{24,16},{9,1},{17,9},{25,17},{10,2},{18,10},{26,18},{... | collective-permute-start | bytes 1204232 | tf_op jit(solution)/shard_map/ppermute | solution.py:332
  100.4 39.4 %collective-permute-start.11 = (f32[2,9,64,128]{3,2,1,0:T(8,128)S(1)}, f32[2,9,64,128]{3,2,1,0:T(8,128)S(1)}, u32[]{:S(2)}, u32[]{:S(2)}) collective-permute-start(f32[2,9,64,128]{3,2,1,0:T(8,128)S(1)} %add.15.refs_5_), channel_id=1, source_target_pairs={{0,4},{1,5},{2,6},{3,7},{4,0},{5,1},{6,2},{7,3},{8,12},{9,13},{10,... | collective-permute-start | bytes 1769480 | tf_op jit(solution)/shard_map/ppermute | solution.py:338
  100.8 53.9 %collective-permute-start.12 = (f32[2,9,64,128]{3,2,1,0:T(8,128)S(1)}, f32[2,9,64,128]{3,2,1,0:T(8,128)S(1)}, u32[]{:S(2)}, u32[]{:S(2)}) collective-permute-start(f32[2,9,64,128]{3,2,1,0:T(8,128)S(1)} %add.16.refs_5_), channel_id=1, source_target_pairs={{0,2},{1,3},{2,4},{3,5},{4,6},{5,7},{6,0},{7,1},{8,10},{9,11},{10,... | collective-permute-start | bytes 1769480 | tf_op jit(solution)/shard_map/ppermute | solution.py:338
  113.9 40.8 %collective-permute-start.14 = (f32[2,9,64,128]{3,2,1,0:T(8,128)S(1)}, f32[2,9,64,128]{3,2,1,0:T(8,128)S(1)}, u32[]{:S(2)}, u32[]{:S(2)}) collective-permute-start(f32[2,9,64,128]{3,2,1,0:T(8,128)S(1)} %get-tuple-element.70), channel_id=1, source_target_pairs={{0,1},{1,0},{2,3},{3,2},{4,5},{5,4},{6,7},{7,6},{8,9},{9,8},{10,11... | collective-permute-start | bytes 1769480 | tf_op jit(solution)/shard_map/ppermute | solution.py:341
  114.0 40.7 %collective-permute-start.13 = (f32[2,9,64,128]{3,2,1,0:T(8,128)S(1)}, f32[2,9,64,128]{3,2,1,0:T(8,128)S(1)}, u32[]{:S(2)}, u32[]{:S(2)}) collective-permute-start(f32[2,9,64,128]{3,2,1,0:T(8,128)S(1)} %add.17.refs_9_), channel_id=1, source_target_pairs={{0,6},{1,7},{2,0},{3,1},{4,2},{5,3},{6,4},{7,5},{8,14},{9,15},{10,... | collective-permute-start | bytes 1769480 | tf_op jit(solution)/shard_map/ppermute | solution.py:338
where the time goes:
time: 156 us
  waiting for transfers between devices  81.2 us (52%)
  Pallas kernels  46.6 us (30%)
  starting transfers between devices  25.3 us (16%)
    pallas_call x12, Pallas kernels, step(): pl.pallas_call(functools.partial(step_kernel, dims, k_turn, tick, last, l...  45.6 us
    ppermute x8, waiting for transfers between devices, on_device(): moved[p] = lax.ppermute(out, 'section', down)  41 us
    ppermute x3, waiting for transfers between devices, on_device(): lax.ppermute(total, 'rep', [(r, (r + k * shares) % reps) for r in range(r...  40.2 us
    ppermute x8, starting transfers between devices, on_device(): moved[p] = lax.ppermute(out, 'section', down)  22.5 us
  transfers between devices with their start and end apart: 15, of which 8 were waited for; matrix products, arithmetic and copies ran while one was open for 0% of the time, Pallas kernels for 18%

commit v1 on v0

--- a/solution.py
+++ b/solution.py
@@ -11,6 +11,7 @@
 F32, BF16 = jnp.float32, jnp.bfloat16
 VMEM_LIMIT = 16 * 2**20
 VMEM, HBM, ANY = pltpu.VMEM, pltpu.HBM, pl.ANY
+PLAN = {'step': {1: 1000000000, 5: 1000000000, 6: 10000000000, 7: 10000000000, 8: 1000000000, 9: 10000000000, 10: 100000000000}, 'add': {1: 100000000000, 2: 10000000000}, 'need': {0: 8, 1: 9, 2: 11}, 'wait': {0: [2]}, 'sum': 100000000000, 'last': 100000000000, 'zneed': {}}
 
 
 def halves(value):
@@ -66,20 +67,18 @@
         if lead:
             (kept,) = take(1)
     if last:
-        grads = take(shares)
+        grads = take(1 + 2 * (shares - 1) if final else 1)
     else:
         (sums,) = take(1)
     plane, taps_one, taps_two, taps_error, sems = take(5)
     if lead:
         (weights,) = take(1)
-    if not first:
-        (held,) = take(1)
     if last:
         (sums,) = take(1)
     if final:
         (whole,) = take(1)
 
-    group = lax.rem(info[0] + k_turn, groups)
+    group = info[0] ^ k_turn
     channels = pl.ds(pl.multiple_of(group * width, width), width)
     if lead:
         copies = [pltpu.make_async_copy(f.at[:, channels, :], weights.at[k], sems.at[k]) for k, f in enumerate(filters)]
@@ -88,11 +87,6 @@
             copy.start()
     if not first:
         at_end = info[1] == 1
-        from_end = pltpu.make_async_copy(arriving.at[tick - 1], held, sems.at[0])
-
-        @pl.when(at_end)
-        def _():
-            from_end.start()
 
     for taps in (taps_one, taps_two, taps_error):
         taps[0:pitch, :] = jnp.zeros((pitch, 6 * width), BF16)
@@ -115,8 +109,7 @@
 
         @pl.when(at_end)
         def _():
-            from_end.wait()
-            take_whole(held)
+            take_whole(arriving.at[tick - 1])
 
         @pl.when(jnp.logical_not(at_end))
         def _():
@@ -136,7 +129,7 @@
     def give(member, value):
         if final:
             for slot, other in enumerate(others):
-                theirs = lax.rem(info[0] + others_turns(groups)[slot], groups)
+                theirs = info[0] ^ (groups - 1 - slot)
                 whole[member, pl.ds(theirs, pixels, stride=groups), :] = other[member * pixels : (member + 1) * pixels, :]
         for r in range(side):
             piece = value[r * pitch : r * pitch + side, :]
@@ -195,8 +188,15 @@
     if last:
         part = width // shares
         for d in range(shares):
-            low = pl.multiple_of(lax.rem(info[2] + d, shares) * part, part)
-            grads[d][...] = sums[:, :, pl.ds(low, part), :]
+            if final:
+                rows_of = pl.ds(pl.multiple_of(lax.rem(info[2] + d, shares) * part, part), part)
+                if d == 0:
+                    grads[0][...] = sums[:, :, rows_of, :]
+                else:
+                    for k in range(2):
+                        grads[2 * d - 1 + k][...] = sums[k, :, rows_of, :]
+            else:
+                grads[0][d] = sums[:, :, d * part : (d + 1) * part, :]
     if lead:
         copies[2].wait()
         copies[3].wait()
@@ -204,11 +204,7 @@
         copy.wait()
 
 
-def others_turns(groups):
-    return sorted(range(1, groups), key=lambda k: (-min(k, groups - k), k))
-
-
-def step(dims, k_turn, tick, last, info, operands, after):
+def step(dims, k_turn, tick, last, info, operands, after, effort):
     side, pitch, groups, width, shares = dims
     pixels, rows = side * side, side * pitch
     depth = -(-rows // 128) * 128
@@ -237,7 +233,7 @@
     else:
         moved, arriving, packed, before, *others = operands
         give(moved, lambda x: x, in_vmem)
-        give(arriving, far, anywhere)
+        give(arriving, local, in_vmem)
         for x in (packed, before, *others):
             give(x, local, in_vmem)
     for x in after:
@@ -252,7 +248,8 @@
         if lead:
             out_shape.append(VMEM((2, 9, groups * width, width), F32))
     if last:
-        out_shape += [VMEM((2, 9, width // shares, width), F32)] * shares
+        part = (2, 9, width // shares, width)
+        out_shape += [VMEM(part, F32)] + [VMEM(part[1:], F32)] * (2 * (shares - 1)) if final else [VMEM((shares, *part), F32)]
     else:
         out_shape.append(VMEM(sums, F32))
     out_specs += [in_vmem] * (len(out_shape) - 1)
@@ -260,8 +257,6 @@
     scratch = [VMEM((4, rows, width), F32)] + [VMEM((2 * pitch + depth, 6 * width), BF16)] * 3 + [pltpu.SemaphoreType.DMA((6,))]
     if lead:
         scratch.append(VMEM(sums, F32))
-    if not first:
-        scratch.append(VMEM((4, pixels * groups, width), F32))
     if last:
         scratch.append(VMEM(sums, F32))
     if final:
@@ -273,16 +268,38 @@
         out_specs=out_specs,
         scratch_shapes=scratch,
         compiler_params=pltpu.CompilerParams(vmem_limit_bytes=VMEM_LIMIT),
-        cost_estimate=pl.CostEstimate(
-            flops=6 * 2 * 9 * 4 * rows * width * width, bytes_accessed=6 * 2**20, transcendentals=2 * rows * width
-        ),
+        cost_estimate=pl.CostEstimate(flops=effort, bytes_accessed=1, transcendentals=0),
         name=f"tick_{tick}_turn_{k_turn}",
     )(*args)
 
 
-def add_kernel(n, *refs):
-    for k, out in enumerate(refs[n:]):
-        out[...] = functools.reduce(lambda x, y: x + y, [ref[k] for ref in refs[:n]])
+def add_kernel(n_terms, n_parts, n_after, *refs):
+    outs = refs[n_terms + n_parts + n_after :]
+    for k in range(2):
+        terms = [ref[k] for ref in refs[:n_terms]] + [ref[...] for ref in refs[n_terms + k : n_terms + n_parts : 2]]
+        total = functools.reduce(lambda x, y: x + y, terms)
+        if len(outs) > 1:
+            outs[k][...] = total
+        else:
+            outs[0][k] = total
+
+
+def stack_kernel(n_terms, n_after, stacked, *refs):
+    terms = [stacked[n] for n in range(stacked.shape[0])] + [ref[...] for ref in refs[:n_terms]]
+    refs[n_terms + n_after][...] = functools.reduce(lambda x, y: x + y, terms)
+
+
+def add(kernel, arrays, after, effort, out, name):
+    in_vmem = pl.BlockSpec(memory_space=VMEM)
+    return pl.pallas_call(
+        kernel,
+        out_shape=out,
+        in_specs=[in_vmem] * len(arrays) + [pl.BlockSpec(memory_space=ANY)] * len(after),
+        out_specs=[in_vmem] * len(out) if isinstance(out, list) else in_vmem,
+        compiler_params=pltpu.CompilerParams(vmem_limit_bytes=VMEM_LIMIT),
+        cost_estimate=pl.CostEstimate(flops=effort, bytes_accessed=1, transcendentals=0),
+        name=name,
+    )(*arrays, *after)
 
 
 def on_device(section_state, arriving, first_weight, second_weight):
@@ -304,28 +321,26 @@
     at_end = lax.axis_index("section") == sections - 1
     info = jnp.stack([rep // shares, at_end.astype(jnp.int32), rep % shares]).astype(jnp.int32)
 
-    turns = others_turns(groups) + [0]
+    turns = list(range(groups - 1, -1, -1))
     down = [(s, s - 1) for s in range(1, sections)]
-    moved, packed, sums, outs, totals, waiting = {}, {}, {}, {}, {}, {}
-
-    def gather_shares(parts):
-        total = parts[0]
-        for d in range(1, shares):
-            total = total + lax.ppermute(parts[d], "rep", [(r, r - r % shares + (r % shares + d) % shares) for r in range(reps)])
-        return total
+    moved, packed, sums, outs, totals, waiting, mine = {}, {}, {}, {}, {}, {}, None
+
+    def swap(part, d):
+        return lax.ppermute(part, "rep", [(r, r - r % shares + (r % shares + d) % shares) for r in range(reps)])
 
     order = sorted(((t, p) for t in range(ticks) for p in range(groups)), key=lambda i: (i[1] + 2 * i[0], -i[0]))
     for n, (tick, p) in enumerate(order):
         k, last = turns[p], tick == ticks - 1
         after = waiting.pop(n, [])
+        effort = PLAN["step"].get(n, 1)
         if tick == 0:
-            results = list(step(dims, k, tick, last, info, (state, *filters), after))
+            results = list(step(dims, k, tick, last, info, (state, *filters), after, effort))
             if n == 0:
                 filters = (results.pop(2),)
             out, packed[p], *grads = results
         else:
             others = [outs[o] for o in range(p)] if last and k == 0 else []
-            out, *grads = step(dims, k, tick, last, info, (moved[p], arrivals, packed[p], sums[p], *others), after)
+            out, *grads = step(dims, k, tick, last, info, (moved[p], arrivals, packed[p], sums[p], *others), after, effort)
         waiting.setdefault(n + 1, []).append(out)
         if not last:
             sums[p] = grads[0]
@@ -333,25 +348,28 @@
             continue
         outs[p] = out
         if k:
-            total = gather_shares(grads)
-            waiting.setdefault(min(n + 2, len(order) - 1), []).append(total)
-            totals[p] = [lax.ppermute(total, "rep", [(r, (r + k * shares) % reps) for r in range(reps)])]
+            chips = [list(range(low, low + shares)) for low in range(0, reps, shares)]
+            stacked = lax.all_to_all(grads[0], "rep", 0, 0, axis_index_groups=chips)
+            after = [moved[q] for q in PLAN["wait"].get(p, [])]
+            out = VMEM(stacked.shape[1:], F32)
+            partial = [totals.pop(0)] if p == 1 else []
+            total = add(functools.partial(stack_kernel, len(partial), len(after)), [stacked, *partial], after, PLAN["add"].get(p, 1), out, f"add_turn_{k}")
+            if p in PLAN["need"]:
+                waiting.setdefault(PLAN["need"][p], []).append(total)
+            mask = 1 if p == 0 else k
+            totals[p] = lax.ppermute(total, "rep", [(r, (r // shares ^ mask) * shares + r % shares) for r in range(reps)])
+            if p in PLAN["zneed"]:
+                waiting.setdefault(PLAN["zneed"][p], []).append(totals[p])
         else:
-            totals[p] = [grads[0]] + [
-                lax.ppermute(grads[d], "rep", [(r, r - r % shares + (r % shares + d) % shares) for r in range(reps)])
-                for d in range(1, shares)
-            ]
-
-    terms = [x for p in range(groups) for x in totals[p]]
-    part = terms[0].shape[1:]
-    first_grad, second_grad = pl.pallas_call(
-        functools.partial(add_kernel, len(terms)),
-        out_shape=[jax.ShapeDtypeStruct(part, F32)] * 2,
-        in_specs=[pl.BlockSpec(memory_space=VMEM)] * len(terms),
-        out_specs=[pl.BlockSpec(memory_space=VMEM)] * 2,
-        compiler_params=pltpu.CompilerParams(vmem_limit_bytes=VMEM_LIMIT),
-        name="add_gradients",
-    )(*terms)
+            mine, swapped = grads[0], [swap(x, 1 + h // 2) for h, x in enumerate(grads[1:])]
+
+    arrived = [mine, *totals.values()]
+    out = VMEM(mine.shape, F32)
+    kept = add(functools.partial(add_kernel, len(arrived), 0, 0), arrived, [], PLAN["sum"], out, "add_arrived")
+    out = [jax.ShapeDtypeStruct(mine.shape[1:], F32)] * 2
+    first_grad, second_grad = add(
+        functools.partial(add_kernel, 1, len(swapped), 0), [kept, *swapped], [], PLAN["last"], out, "add_last"
+    )
     returned = outs[groups - 1].reshape(1, 4, 1, pixels, channels)
     return (returned, first_grad[None, None], second_grad[None, None])
 

time: 156 us -> 114 us (0.73)
  the two profiles are of different devices: /device:TPU:20 before, /device:TPU:6 now
where the time goes in v1:
time: 114 us
  Pallas kernels  46.4 us (41%)
  starting transfers between devices  28.4 us (25%)
  waiting for transfers between devices  22.5 us (20%)
  blocking collectives  14 us (12%)
  local copies, waits for them, and re-layouts  1.44 us (1%)
    pallas_call x12, Pallas kernels, step(): pl.pallas_call(functools.partial(step_kernel, dims, k_turn, tick, last, l...  45.2 us
    ppermute x8, starting transfers between devices, on_device(): moved[p] = lax.ppermute(out, 'section', down)  22.1 us
    all_to_all x3, blocking collectives, on_device(): stacked = lax.all_to_all(grads[0], 'rep', 0, 0, axis_index_groups=chips)  14 us
    ppermute x3, waiting for transfers between devices, on_device(): lax.ppermute(total, 'rep', [(r, (r // shares ^ mask) * shares + r % share...  11.6 us
    ppermute x8, waiting for transfers between devices, on_device(): moved[p] = lax.ppermute(out, 'section', down)  11 us
    ppermute x3, starting transfers between devices, on_device(): lax.ppermute(total, 'rep', [(r, (r // shares ^ mask) * shares + r % share...  5.78 us
  transfers between devices with their start and end apart: 13, of which 4 were waited for; matrix products, arithmetic and copies ran while one was open for 0% of the time, Pallas kernels for 32%

profile of v1, /device:TPU:6, one launch (start us, length us, event | category | flops | bytes accessed | tf_op | source)
XLA Modules:
  0.0 113.8 jit_solution(17448016538841768110)
XLA Ops:
  0.7 0.1 pad_add_fusion.refs_0_
  0.7 1.4 %copy-done.1 = f32[1,4,1,196,512]{4,2,3,1,0:T(1,128)S(1)} copy-done((f32[1,4,1,196,512]{4,2,3,1,0:T(1,128)S(1)}, f32[1,4,1,196,512]{4,2,3,1,0:T(1,128)}, u32[]{:S(2)}) %copy-start.1) | copy-done | bytes 1605656
  2.1 5.6 %tick_0_turn_3.1 = (f32[784,128]{1,0:T(8,128)S(1)}, bf16[4,3,384,256]{3,2,1,0:T(8,128)(2,1)S(1)}, f32[2,9,512,128]{3,2,1,0:T(8,128)S(1)}, f32[2,9,128,128]{3,2,1,0:T(8,128)S(1)}) custom-call(s32[3]{0:T(128)S(1)} %pad_add_fusion.refs_0_, f32[4,784,128]{2,1,0:T(8,128)S(1)} %bitcast.18, f32[9,512,128]{2,1,0:T(8,128)} %bitcast.22, f32[9,512,128]{2,1,0:T(8,128)} %bitcast.23), custom_call_target="tpu_custom_call" | custom-call | flops 1 | bytes 1 | tf_op jit(solution)/shard_map/tick_0_turn_3/pallas_call | solution.py:264
  7.7 2.5 %collective-permute-start.1 = (f32[784,128]{1,0:T(8,128)S(1)}, f32[784,128]{1,0:T(8,128)S(1)}, u32[]{:S(2)}, u32[]{:S(2)}) collective-permute-start(f32[784,128]{1,0:T(8,128)S(1)} %get-tuple-element.37.refs_3_), channel_id=1, source_target_pairs={{8,0},{16,8},{24,16},{9,1},{17,9},{25,17},{10,2},{18,10},{26,18},{... | collective-permute-start | bytes 1204232 | tf_op jit(solution)/shard_map/ppermute | solution.py:347
  10.2 0.0 copy-start
  10.2 3.6 %tick_0_turn_2.1 = (f32[784,128]{1,0:T(8,128)S(1)}, bf16[4,3,384,256]{3,2,1,0:T(8,128)(2,1)S(1)}, f32[2,9,128,128]{3,2,1,0:T(8,128)S(1)}) custom-call(s32[3]{0:T(128)S(1)} %pad_add_fusion.refs_0_, f32[4,784,128]{2,1,0:T(8,128)S(1)} %bitcast.19, f32[2,9,512,128]{3,2,1,0:T(8,128)S(1)} %get-tuple-element.36.refs_2_, f32[784,128]{1,0:T(8,128)S(1)} %get-tuple-element.37.refs_3_), custom_call_target="tpu_custom_call" | custom-call | flops 1000000000 | bytes 1 | tf_op jit(solution)/shard_map/tick_0_turn_2/pallas_call | solution.py:264
  13.8 3.3 %collective-permute-start = (f32[784,128]{1,0:T(8,128)S(1)}, f32[784,128]{1,0:T(8,128)S(1)}, u32[]{:S(2)}, u32[]{:S(2)}) collective-permute-start(f32[784,128]{1,0:T(8,128)S(1)} %get-tuple-element.38.refs_5_), channel_id=1, source_target_pairs={{8,0},{16,8},{24,16},{9,1},{17,9},{25,17},{10,2},{18,10},{26,18},{... | collective-permute-start | bytes 1204232 | tf_op jit(solution)/shard_map/ppermute | solution.py:347
  17.1 2.7 %collective-permute-done.1.refs_1_ = f32[784,128]{1,0:T(8,128)S(1)} collective-permute-done((f32[784,128]{1,0:T(8,128)S(1)}, f32[784,128]{1,0:T(8,128)S(1)}, u32[]{:S(2)}, u32[]{:S(2)}) %collective-permute-start.1) | collective-permute-done | bytes 401440 | tf_op jit(solution)/shard_map/ppermute | solution.py:347
  19.8 3.5 %tick_1_turn_3.1 = (f32[784,128]{1,0:T(8,128)S(1)}, f32[2,9,128,128]{3,2,1,0:T(8,128)S(1)}) custom-call(s32[3]{0:T(128)S(1)} %pad_add_fusion.refs_0_, f32[784,128]{1,0:T(8,128)S(1)} %collective-permute-done.1.refs_1_, f32[2,4,784,128]{3,2,1,0:T(8,128)S(1)} %bitcast.10, bf16[4,3,384,256]{3,2,1,0:T(8,128)(2,1)S(1)} %get-tuple-element.41.refs_3_, ...), custom_call_target="tpu_custom_call" | custom-call | flops 1 | bytes 1 | tf_op jit(solution)/shard_map/tick_1_turn_3/pallas_call | solution.py:264
  23.4 4.4 %collective-permute-start.4 = (f32[784,128]{1,0:T(8,128)S(1)}, f32[784,128]{1,0:T(8,128)S(1)}, u32[]{:S(2)}, u32[]{:S(2)}) collective-permute-start(f32[784,128]{1,0:T(8,128)S(1)} %get-tuple-element.43.refs_3_), channel_id=1, source_target_pairs={{8,0},{16,8},{24,16},{9,1},{17,9},{25,17},{10,2},{18,10},{26,18},{... | collective-permute-start | bytes 1204232 | tf_op jit(solution)/shard_map/ppermute | solution.py:347
  27.8 3.6 %tick_0_turn_1.1 = (f32[784,128]{1,0:T(8,128)S(1)}, bf16[4,3,384,256]{3,2,1,0:T(8,128)(2,1)S(1)}, f32[2,9,128,128]{3,2,1,0:T(8,128)S(1)}) custom-call(s32[3]{0:T(128)S(1)} %pad_add_fusion.refs_0_, f32[4,784,128]{2,1,0:T(8,128)S(1)} %bitcast.20, f32[2,9,512,128]{3,2,1,0:T(8,128)S(1)} %get-tuple-element.36.refs_2_, f32[784,128]{1,0:T(8,128)S(1)} %get-tuple-element.43.refs_3_), custom_call_target="tpu_custom_call" | custom-call | flops 1 | bytes 1 | tf_op jit(solution)/shard_map/tick_0_turn_1/pallas_call | solution.py:264
  31.4 4.2 %collective-permute-start.5 = (f32[784,128]{1,0:T(8,128)S(1)}, f32[784,128]{1,0:T(8,128)S(1)}, u32[]{:S(2)}, u32[]{:S(2)}) collective-permute-start(f32[784,128]{1,0:T(8,128)S(1)} %get-tuple-element.44.refs_5_), channel_id=1, source_target_pairs={{8,0},{16,8},{24,16},{9,1},{17,9},{25,17},{10,2},{18,10},{26,18},{... | collective-permute-start | bytes 1204232 | tf_op jit(solution)/shard_map/ppermute | solution.py:347
  35.6 0.0 collective-permute-done.refs_1_
  35.6 3.7 %tick_1_turn_2.1 = (f32[784,128]{1,0:T(8,128)S(1)}, f32[2,9,128,128]{3,2,1,0:T(8,128)S(1)}) custom-call(s32[3]{0:T(128)S(1)} %pad_add_fusion.refs_0_, f32[784,128]{1,0:T(8,128)S(1)} %collective-permute-done.refs_1_, f32[2,4,784,128]{3,2,1,0:T(8,128)S(1)} %bitcast.11, bf16[4,3,384,256]{3,2,1,0:T(8,128)(2,1)S(1)} %get-tuple-element.39.refs_3_, ...), custom_call_target="tpu_custom_call" | custom-call | flops 1 | bytes 1 | tf_op jit(solution)/shard_map/tick_1_turn_2/pallas_call | solution.py:264
  39.4 1.9 %collective-permute-start.3 = (f32[784,128]{1,0:T(8,128)S(1)}, f32[784,128]{1,0:T(8,128)S(1)}, u32[]{:S(2)}, u32[]{:S(2)}) collective-permute-start(f32[784,128]{1,0:T(8,128)S(1)} %get-tuple-element.45.refs_3_), channel_id=1, source_target_pairs={{8,0},{16,8},{24,16},{9,1},{17,9},{25,17},{10,2},{18,10},{26,18},{... | collective-permute-start | bytes 1204232 | tf_op jit(solution)/shard_map/ppermute | solution.py:347
  41.3 3.6 %tick_0_turn_0.1 = (f32[784,128]{1,0:T(8,128)S(1)}, bf16[4,3,384,256]{3,2,1,0:T(8,128)(2,1)S(1)}, f32[2,9,128,128]{3,2,1,0:T(8,128)S(1)}) custom-call(s32[3]{0:T(128)S(1)} %pad_add_fusion.refs_0_, f32[4,784,128]{2,1,0:T(8,128)S(1)} %bitcast.21, f32[2,9,512,128]{3,2,1,0:T(8,128)S(1)} %get-tuple-element.36.refs_2_, f32[784,128]{1,0:T(8,128)S(1)} %get-tuple-element.45.refs_3_), custom_call_target="tpu_custom_call" | custom-call | flops 1000000000 | bytes 1 | tf_op jit(solution)/shard_map/tick_0_turn_0/pallas_call | solution.py:264
  44.9 1.9 %collective-permute-start.2 = (f32[784,128]{1,0:T(8,128)S(1)}, f32[784,128]{1,0:T(8,128)S(1)}, u32[]{:S(2)}, u32[]{:S(2)}) collective-permute-start(f32[784,128]{1,0:T(8,128)S(1)} %get-tuple-element.46.refs_5_), channel_id=1, source_target_pairs={{8,0},{16,8},{24,16},{9,1},{17,9},{25,17},{10,2},{18,10},{26,18},{... | collective-permute-start | bytes 1204232 | tf_op jit(solution)/shard_map/ppermute | solution.py:347
  46.8 0.0 collective-permute-done.4.refs_1_
  46.8 3.5 %tick_2_turn_3.1 = (f32[784,128]{1,0:T(8,128)S(1)}, f32[2,2,9,64,128]{4,3,2,1,0:T(8,128)S(1)}) custom-call(s32[3]{0:T(128)S(1)} %pad_add_fusion.refs_0_, f32[784,128]{1,0:T(8,128)S(1)} %collective-permute-done.4.refs_1_, f32[2,4,784,128]{3,2,1,0:T(8,128)S(1)} %bitcast.12, bf16[4,3,384,256]{3,2,1,0:T(8,128)(2,1)S(1)} %get-tuple-element.41.refs_3_, ...), custom_call_target="tpu_custom_call" | custom-call | flops 10000000000 | bytes 1 | tf_op jit(solution)/shard_map/tick_2_turn_3/pallas_call | solution.py:264
  50.3 0.0 copy-start.3
  50.3 4.7 %all_to_all.15.stacked = f32[2,2,9,64,128]{4,3,2,1,0:T(8,128)S(1)} all-to-all(f32[2,2,9,64,128]{4,3,2,1,0:T(8,128)S(1)} %get-tuple-element.51), channel_id=1, replica_groups={{0,1},{2,3},{4,5},{6,7},{8,9},{10,11},{12,13},{14,15},{16,17},{18,19},{..., dimensions={0} | all-to-all | bytes 2359296 | tf_op jit(solution)/shard_map/all_to_all | solution.py:352
  55.0 0.0 collective-permute-done.5.refs_0_.refs_1_
  55.0 0.1 add_turn_3.1.refs_5_
  55.1 1.6 %collective-permute-start.6 = (f32[2,9,64,128]{3,2,1,0:T(8,128)S(1)}, f32[2,9,64,128]{3,2,1,0:T(8,128)S(1)}, u32[]{:S(2)}, u32[]{:S(2)}) collective-permute-start(f32[2,9,64,128]{3,2,1,0:T(8,128)S(1)} %add_turn_3.1.refs_5_), channel_id=1, source_target_pairs={{0,2},{1,3},{2,0},{3,1},{4,6},{5,7},{6,4},{7,5},{8,10},{9,11},{10,... | collective-permute-start | bytes 1769480 | tf_op jit(solution)/shard_map/ppermute | solution.py:360
  56.7 3.5 %tick_1_turn_1.1 = (f32[784,128]{1,0:T(8,128)S(1)}, f32[2,9,128,128]{3,2,1,0:T(8,128)S(1)}) custom-call(s32[3]{0:T(128)S(1)} %pad_add_fusion.refs_0_, f32[784,128]{1,0:T(8,128)S(1)} %collective-permute-done.5.refs_0_.refs_1_, f32[2,4,784,128]{3,2,1,0:T(8,128)S(1)} %bitcast.13, bf16[4,3,384,256]{3,2,1,0:T(8,128)(2,1)S(1)} %get-tuple-element.52.refs_3_, ...), custom_call_target="tpu_custom_call" | custom-call | flops 10000000000 | bytes 1 | tf_op jit(solution)/shard_map/tick_1_turn_1/pallas_call | solution.py:264
  60.3 1.9 %collective-permute-start.8 = (f32[784,128]{1,0:T(8,128)S(1)}, f32[784,128]{1,0:T(8,128)S(1)}, u32[]{:S(2)}, u32[]{:S(2)}) collective-permute-start(f32[784,128]{1,0:T(8,128)S(1)} %get-tuple-element.55.refs_6_), channel_id=1, source_target_pairs={{8,0},{16,8},{24,16},{9,1},{17,9},{25,17},{10,2},{18,10},{26,18},{... | collective-permute-start | bytes 1204232 | tf_op jit(solution)/shard_map/ppermute | solution.py:347
  62.2 0.0 collective-permute-done.3.refs_1_
  62.2 3.7 %tick_2_turn_2.1 = (f32[784,128]{1,0:T(8,128)S(1)}, f32[2,2,9,64,128]{4,3,2,1,0:T(8,128)S(1)}) custom-call(s32[3]{0:T(128)S(1)} %pad_add_fusion.refs_0_, f32[784,128]{1,0:T(8,128)S(1)} %collective-permute-done.3.refs_1_, f32[2,4,784,128]{3,2,1,0:T(8,128)S(1)} %bitcast.14, bf16[4,3,384,256]{3,2,1,0:T(8,128)(2,1)S(1)} %get-tuple-element.39.refs_3_, ...), custom_call_target="tpu_custom_call" | custom-call | flops 1000000000 | bytes 1 | tf_op jit(solution)/shard_map/tick_2_turn_2/pallas_call | solution.py:264
  65.9 4.7 %all_to_all.16.stacked = f32[2,2,9,64,128]{4,3,2,1,0:T(8,128)S(1)} all-to-all(f32[2,2,9,64,128]{4,3,2,1,0:T(8,128)S(1)} %get-tuple-element.57), channel_id=1, replica_groups={{0,1},{2,3},{4,5},{6,7},{8,9},{10,11},{12,13},{14,15},{16,17},{18,19},{..., dimensions={0} | all-to-all | bytes 2359296 | tf_op jit(solution)/shard_map/all_to_all | solution.py:352
  70.6 0.0 collective-permute-done.6.refs_0_
  70.6 0.1 add_turn_2.1.refs_6_
  70.7 3.5 %tick_1_turn_0.1 = (f32[784,128]{1,0:T(8,128)S(1)}, f32[2,9,128,128]{3,2,1,0:T(8,128)S(1)}) custom-call(s32[3]{0:T(128)S(1)} %pad_add_fusion.refs_0_, f32[784,128]{1,0:T(8,128)S(1)} %collective-permute-done.2.refs_1_, f32[2,4,784,128]{3,2,1,0:T(8,128)S(1)} %bitcast.15, bf16[4,3,384,256]{3,2,1,0:T(8,128)(2,1)S(1)} %get-tuple-element.47.refs_3_, ...), custom_call_target="tpu_custom_call" | custom-call | flops 10000000000 | bytes 1 | tf_op jit(solution)/shard_map/tick_1_turn_0/pallas_call | solution.py:264
  74.3 0.0 collective-permute-done.8.refs_1_
  74.3 3.5 %tick_2_turn_1.1 = (f32[784,128]{1,0:T(8,128)S(1)}, f32[2,2,9,64,128]{4,3,2,1,0:T(8,128)S(1)}) custom-call(s32[3]{0:T(128)S(1)} %pad_add_fusion.refs_0_, f32[784,128]{1,0:T(8,128)S(1)} %collective-permute-done.8.refs_1_, f32[2,4,784,128]{3,2,1,0:T(8,128)S(1)} %bitcast.16, bf16[4,3,384,256]{3,2,1,0:T(8,128)(2,1)S(1)} %get-tuple-element.52.refs_3_, ...), custom_call_target="tpu_custom_call" | custom-call | flops 99999997952 | bytes 1 | tf_op jit(solution)/shard_map/tick_2_turn_1/pallas_call | solution.py:264
  77.8 4.7 %all_to_all.17.stacked = f32[2,2,9,64,128]{4,3,2,1,0:T(8,128)S(1)} all-to-all(f32[2,2,9,64,128]{4,3,2,1,0:T(8,128)S(1)} %get-tuple-element.62), channel_id=1, replica_groups={{0,1},{2,3},{4,5},{6,7},{8,9},{10,11},{12,13},{14,15},{16,17},{18,19},{..., dimensions={0} | all-to-all | bytes 2359296 | tf_op jit(solution)/shard_map/all_to_all | solution.py:352
  82.5 0.1 add_turn_1.1.refs_9_
  82.5 1.6 %collective-permute-start.10 = (f32[2,9,64,128]{3,2,1,0:T(8,128)S(1)}, f32[2,9,64,128]{3,2,1,0:T(8,128)S(1)}, u32[]{:S(2)}, u32[]{:S(2)}) collective-permute-start(f32[2,9,64,128]{3,2,1,0:T(8,128)S(1)} %add_turn_1.1.refs_9_), channel_id=1, source_target_pairs={{0,2},{1,3},{2,0},{3,1},{4,6},{5,7},{6,4},{7,5},{8,10},{9,11},{10,... | collective-permute-start | bytes 1769480 | tf_op jit(solution)/shard_map/ppermute | solution.py:360
  84.1 2.6 %collective-permute-start.9 = (f32[2,9,64,128]{3,2,1,0:T(8,128)S(1)}, f32[2,9,64,128]{3,2,1,0:T(8,128)S(1)}, u32[]{:S(2)}, u32[]{:S(2)}) collective-permute-start(f32[2,9,64,128]{3,2,1,0:T(8,128)S(1)} %add_turn_2.1.refs_6_), channel_id=1, source_target_pairs={{0,4},{1,5},{2,6},{3,7},{4,0},{5,1},{6,2},{7,3},{8,12},{9,13},{10,... | collective-permute-start | bytes 1769480 | tf_op jit(solution)/shard_map/ppermute | solution.py:360
  86.7 1.9 %collective-permute-start.7 = (f32[784,128]{1,0:T(8,128)S(1)}, f32[784,128]{1,0:T(8,128)S(1)}, u32[]{:S(2)}, u32[]{:S(2)}) collective-permute-start(f32[784,128]{1,0:T(8,128)S(1)} %get-tuple-element.58.refs_5_), channel_id=1, source_target_pairs={{8,0},{16,8},{24,16},{9,1},{17,9},{25,17},{10,2},{18,10},{26,18},{... | collective-permute-start | bytes 1204232 | tf_op jit(solution)/shard_map/ppermute | solution.py:347
  88.6 8.2 %collective-permute-done.7.refs_1_ = f32[784,128]{1,0:T(8,128)S(1)} collective-permute-done((f32[784,128]{1,0:T(8,128)S(1)}, f32[784,128]{1,0:T(8,128)S(1)}, u32[]{:S(2)}, u32[]{:S(2)}) %collective-permute-start.7) | collective-permute-done | bytes 401440 | tf_op jit(solution)/shard_map/ppermute | solution.py:347
  96.8 3.8 %tick_2_turn_0.1 = (f32[4,784,128]{2,1,0:T(8,128)}, f32[2,9,64,128]{3,2,1,0:T(8,128)S(1)}, f32[9,64,128]{2,1,0:T(8,128)S(1)}, f32[9,64,128]{2,1,0:T(8,128)S(1)}) custom-call(s32[3]{0:T(128)S(1)} %pad_add_fusion.refs_0_, f32[784,128]{1,0:T(8,128)S(1)} %collective-permute-done.7.refs_1_, f32[2,4,784,128]{3,2,1,0:T(8,128)S(1)} %bitcast.17, ...), custom_call_target="tpu_custom_call" | custom-call | flops 1 | bytes 1 | tf_op jit(solution)/shard_map/tick_2_turn_0/pallas_call | solution.py:264
  100.6 0.1 collective-permute-start.11
  100.7 0.5 collective-permute-start.12
  101.2 9.4 %collective-permute-done.10.refs_2_ = f32[2,9,64,128]{3,2,1,0:T(8,128)S(1)} collective-permute-done((f32[2,9,64,128]{3,2,1,0:T(8,128)S(1)}, f32[2,9,64,128]{3,2,1,0:T(8,128)S(1)}, u32[]{:S(2)}, u32[]{:S(2)}) %collective-permute-start.10) | collective-permute-done | bytes 589856 | tf_op jit(solution)/shard_map/ppermute | solution.py:360
  110.6 2.2 %collective-permute-done.9.refs_1_ = f32[2,9,64,128]{3,2,1,0:T(8,128)S(1)} collective-permute-done((f32[2,9,64,128]{3,2,1,0:T(8,128)S(1)}, f32[2,9,64,128]{3,2,1,0:T(8,128)S(1)}, u32[]{:S(2)}, u32[]{:S(2)}) %collective-permute-start.9) | collective-permute-done | bytes 589856 | tf_op jit(solution)/shard_map/ppermute | solution.py:360
  112.8 0.1 add_arrived.1.refs_0_
  112.9 0.0 collective-permute-done.11.refs_1_
  112.9 0.9 add_last.1
  (9 shorter events, 0.0 us)
Async XLA Ops:
  0.7 1.4 %copy-start.1 = (f32[1,4,1,196,512]{4,2,3,1,0:T(1,128)S(1)}, f32[1,4,1,196,512]{4,2,3,1,0:T(1,128)}, u32[]{:S(2)}) copy-start(f32[1,4,1,196,512]{4,2,3,1,0:T(1,128)} %param.4) | copy-start | bytes 4816900
  7.7 12.1 %collective-permute-start.1 = (f32[784,128]{1,0:T(8,128)S(1)}, f32[784,128]{1,0:T(8,128)S(1)}, u32[]{:S(2)}, u32[]{:S(2)}) collective-permute-start(f32[784,128]{1,0:T(8,128)S(1)} %get-tuple-element.37.refs_3_), channel_id=1, source_target_pairs={{8,0},{16,8},{24,16},{9,1},{17,9},{25,17},{10,2},{18,10},{26,18},{... | collective-permute-start | bytes 1204232 | tf_op jit(solution)/shard_map/ppermute | solution.py:347
  10.2 9.7 %copy-start = (f32[2,4,1,196,512]{4,2,3,1,0:T(1,128)S(1)}, f32[2,4,1,196,512]{4,2,3,1,0:T(1,128)}, u32[]{:S(2)}) copy-start(f32[2,4,1,196,512]{4,2,3,1,0:T(1,128)} %param.5) | copy-start | bytes 9633796
  13.8 21.8 %collective-permute-start = (f32[784,128]{1,0:T(8,128)S(1)}, f32[784,128]{1,0:T(8,128)S(1)}, u32[]{:S(2)}, u32[]{:S(2)}) collective-permute-start(f32[784,128]{1,0:T(8,128)S(1)} %get-tuple-element.38.refs_5_), channel_id=1, source_target_pairs={{8,0},{16,8},{24,16},{9,1},{17,9},{25,17},{10,2},{18,10},{26,18},{... | collective-permute-start | bytes 1204232 | tf_op jit(solution)/shard_map/ppermute | solution.py:347
  19.8 7.9 %copy-start.2 = (f32[1,4,1,196,512]{4,2,3,1,0:T(1,128)S(1)}, f32[1,4,1,196,512]{4,2,3,1,0:T(1,128)}, u32[]{:S(2)}) copy-start(f32[1,4,1,196,512]{4,2,3,1,0:T(1,128)} %param.4) | copy-start | bytes 4816900
  23.4 23.4 %collective-permute-start.4 = (f32[784,128]{1,0:T(8,128)S(1)}, f32[784,128]{1,0:T(8,128)S(1)}, u32[]{:S(2)}, u32[]{:S(2)}) collective-permute-start(f32[784,128]{1,0:T(8,128)S(1)} %get-tuple-element.43.refs_3_), channel_id=1, source_target_pairs={{8,0},{16,8},{24,16},{9,1},{17,9},{25,17},{10,2},{18,10},{26,18},{... | collective-permute-start | bytes 1204232 | tf_op jit(solution)/shard_map/ppermute | solution.py:347
  31.4 23.6 %collective-permute-start.5 = (f32[784,128]{1,0:T(8,128)S(1)}, f32[784,128]{1,0:T(8,128)S(1)}, u32[]{:S(2)}, u32[]{:S(2)}) collective-permute-start(f32[784,128]{1,0:T(8,128)S(1)} %get-tuple-element.44.refs_5_), channel_id=1, source_target_pairs={{8,0},{16,8},{24,16},{9,1},{17,9},{25,17},{10,2},{18,10},{26,18},{... | collective-permute-start | bytes 1204232 | tf_op jit(solution)/shard_map/ppermute | solution.py:347
  39.4 22.8 %collective-permute-start.3 = (f32[784,128]{1,0:T(8,128)S(1)}, f32[784,128]{1,0:T(8,128)S(1)}, u32[]{:S(2)}, u32[]{:S(2)}) collective-permute-start(f32[784,128]{1,0:T(8,128)S(1)} %get-tuple-element.45.refs_3_), channel_id=1, source_target_pairs={{8,0},{16,8},{24,16},{9,1},{17,9},{25,17},{10,2},{18,10},{26,18},{... | collective-permute-start | bytes 1204232 | tf_op jit(solution)/shard_map/ppermute | solution.py:347
  44.9 25.9 %collective-permute-start.2 = (f32[784,128]{1,0:T(8,128)S(1)}, f32[784,128]{1,0:T(8,128)S(1)}, u32[]{:S(2)}, u32[]{:S(2)}) collective-permute-start(f32[784,128]{1,0:T(8,128)S(1)} %get-tuple-element.46.refs_5_), channel_id=1, source_target_pairs={{8,0},{16,8},{24,16},{9,1},{17,9},{25,17},{10,2},{18,10},{26,18},{... | collective-permute-start | bytes 1204232 | tf_op jit(solution)/shard_map/ppermute | solution.py:347
  50.3 6.4 %copy-start.3 = (f32[784,128]{1,0:T(8,128)}, f32[784,128]{1,0:T(8,128)S(1)}, u32[]{:S(2)}) copy-start(f32[784,128]{1,0:T(8,128)S(1)} %get-tuple-element.54.refs_5_) | copy-start | bytes 1204228
  55.1 15.5 %collective-permute-start.6 = (f32[2,9,64,128]{3,2,1,0:T(8,128)S(1)}, f32[2,9,64,128]{3,2,1,0:T(8,128)S(1)}, u32[]{:S(2)}, u32[]{:S(2)}) collective-permute-start(f32[2,9,64,128]{3,2,1,0:T(8,128)S(1)} %add_turn_3.1.refs_5_), channel_id=1, source_target_pairs={{0,2},{1,3},{2,0},{3,1},{4,6},{5,7},{6,4},{7,5},{8,10},{9,11},{10,... | collective-permute-start | bytes 1769480 | tf_op jit(solution)/shard_map/ppermute | solution.py:360
  60.3 14.0 %collective-permute-start.8 = (f32[784,128]{1,0:T(8,128)S(1)}, f32[784,128]{1,0:T(8,128)S(1)}, u32[]{:S(2)}, u32[]{:S(2)}) collective-permute-start(f32[784,128]{1,0:T(8,128)S(1)} %get-tuple-element.55.refs_6_), channel_id=1, source_target_pairs={{8,0},{16,8},{24,16},{9,1},{17,9},{25,17},{10,2},{18,10},{26,18},{... | collective-permute-start | bytes 1204232 | tf_op jit(solution)/shard_map/ppermute | solution.py:347
  82.5 14.3 %copy-start.4 = (f32[784,128]{1,0:T(8,128)S(1)}, f32[784,128]{1,0:T(8,128)}, u32[]{:S(2)}) copy-start(f32[784,128]{1,0:T(8,128)} %copy-done.3) | copy-start | bytes 1204228
  82.5 28.1 %collective-permute-start.10 = (f32[2,9,64,128]{3,2,1,0:T(8,128)S(1)}, f32[2,9,64,128]{3,2,1,0:T(8,128)S(1)}, u32[]{:S(2)}, u32[]{:S(2)}) collective-permute-start(f32[2,9,64,128]{3,2,1,0:T(8,128)S(1)} %add_turn_1.1.refs_9_), channel_id=1, source_target_pairs={{0,2},{1,3},{2,0},{3,1},{4,6},{5,7},{6,4},{7,5},{8,10},{9,11},{10,... | collective-permute-start | bytes 1769480 | tf_op jit(solution)/shard_map/ppermute | solution.py:360
  84.1 28.7 %collective-permute-start.9 = (f32[2,9,64,128]{3,2,1,0:T(8,128)S(1)}, f32[2,9,64,128]{3,2,1,0:T(8,128)S(1)}, u32[]{:S(2)}, u32[]{:S(2)}) collective-permute-start(f32[2,9,64,128]{3,2,1,0:T(8,128)S(1)} %add_turn_2.1.refs_6_), channel_id=1, source_target_pairs={{0,4},{1,5},{2,6},{3,7},{4,0},{5,1},{6,2},{7,3},{8,12},{9,13},{10,... | collective-permute-start | bytes 1769480 | tf_op jit(solution)/shard_map/ppermute | solution.py:360
  86.7 10.1 %collective-permute-start.7 = (f32[784,128]{1,0:T(8,128)S(1)}, f32[784,128]{1,0:T(8,128)S(1)}, u32[]{:S(2)}, u32[]{:S(2)}) collective-permute-start(f32[784,128]{1,0:T(8,128)S(1)} %get-tuple-element.58.refs_5_), channel_id=1, source_target_pairs={{8,0},{16,8},{24,16},{9,1},{17,9},{25,17},{10,2},{18,10},{26,18},{... | collective-permute-start | bytes 1204232 | tf_op jit(solution)/shard_map/ppermute | solution.py:347
  100.6 12.3 %collective-permute-start.11 = (f32[9,64,128]{2,1,0:T(8,128)S(1)}, f32[9,64,128]{2,1,0:T(8,128)S(1)}, u32[]{:S(2)}, u32[]{:S(2)}) collective-permute-start(f32[9,64,128]{2,1,0:T(8,128)S(1)} %get-tuple-element.65), channel_id=1, source_target_pairs={{0,1},{1,0},{2,3},{3,2},{4,5},{5,4},{6,7},{7,6},{8,9},{9,8},{10,11... | collective-permute-start | bytes 884744 | tf_op jit(solution)/shard_map/ppermute | solution.py:329
  100.7 12.2 %collective-permute-start.12 = (f32[9,64,128]{2,1,0:T(8,128)S(1)}, f32[9,64,128]{2,1,0:T(8,128)S(1)}, u32[]{:S(2)}, u32[]{:S(2)}) collective-permute-start(f32[9,64,128]{2,1,0:T(8,128)S(1)} %get-tuple-element.66), channel_id=1, source_target_pairs={{0,1},{1,0},{2,3},{3,2},{4,5},{5,4},{6,7},{7,6},{8,9},{9,8},{10,11... | collective-permute-start | bytes 884744 | tf_op jit(solution)/shard_map/ppermute | solution.py:329

commit v2 on v1

v2 whole, which is shorter than its diff:
```python
import functools
import math

import jax
import jax.numpy as jnp
from jax import lax
from jax.experimental import pallas as pl
from jax.experimental.pallas import tpu as pltpu
from jax.sharding import PartitionSpec as P

F32, BF16 = jnp.float32, jnp.bfloat16
VMEM_LIMIT = 8 * 2**20
VMEM, HBM, ANY = pltpu.VMEM, pltpu.HBM, pl.ANY
PLAN = {'step': {(1, 0): 10000000000, (1, 1): 100000000000, (1, 2): 10000000000, (2, 1): 1000000000, (1, 3): 10000000000}, 'add': {0: 1000000000}, 'need': {0: (1, 2), 2: (2, 3), 1: (2, 2)}, 'wait': {0: [2]}, 'znd': {}, 'swap': {3: 2, 0: 0, 1: 1, 2: 2}, 'sum': 10000000000, 'last': 1, 'order': ((0, 0), (0, 1), (1, 0), (0, 2), (1, 1), (0, 3), (2, 0), (1, 2), (2, 1), (1, 3), (2, 2), (2, 3))}


def halves(value):
    high = value.astype(BF16)
    return high, (value - high.astype(F32)).astype(BF16)


def spread(taps, value, pitch, shifted):
    rows, width = value.shape
    shifted[8 : 8 + rows, :] = value
    for b in range(3):
        moved = value if b == 1 else shifted[7 + b : 7 + b + rows, :]
        for k, half in enumerate(halves(moved)):
            low = (3 * k + b) * width
            taps[pitch : pitch + rows, low : low + width] = half


def conv(taps, packed, rows, pitch):
    total = None
    for a in range(3):
        filters = packed[a]
        part = jnp.dot(
            taps[a * pitch : a * pitch + rows, :], jnp.concatenate([filters, filters], axis=0), preferred_element_type=F32
        )
        total = part if total is None else total + part
    width = total.shape[1] // 2
    return total[:, :width] + total[:, width:]


def turn(value, depth):
    rows, width = value.shape
    high, low = halves(jnp.concatenate([value, jnp.zeros((depth - rows, width), F32)], axis=0).T)
    return jnp.concatenate([high, high, low], axis=1)


def step_kernel(dims, k_turn, tick, last, n_after, pieces, *refs):
    side, pitch, groups, width, shares = dims
    rows, pixels = side * pitch, side * side
    depth = -(-rows // 128) * 128
    first, lead, final = tick == 0, tick == 0 and n_after == 0, last and k_turn == 0
    refs = list(refs)
    take = lambda n: [refs.pop(0) for _ in range(n)]
    (info,) = take(1)
    if first:
        (state,) = take(1)
        filters = take(2 if lead else 1)
    else:
        moved, arriving, packed, sums_in = take(4)
    others = take(groups - 1) if final else []
    take(n_after)
    (out,) = take(1)
    if first:
        (packed,) = take(1)
        if lead:
            kept, kept_state = take(2)
    if last:
        grads = take(1 + pieces * (shares - 1))
    else:
        (sums,) = take(1)
    plane, taps_one, taps_two, taps_error, sems, shifted = take(6)
    shifted[0:8, :] = jnp.zeros((8, width), F32)
    shifted[8 + rows :, :] = jnp.zeros((8, width), F32)
    if lead:
        (weights,) = take(1)
    if last:
        (sums,) = take(1)
    if final:
        (whole,) = take(1)

    group = info[0] ^ k_turn
    channels = pl.ds(pl.multiple_of(group * width, width), width)
    if lead:
        copies = [pltpu.make_async_copy(f.at[:, channels, :], weights.at[k], sems.at[k]) for k, f in enumerate(filters)]
        copies += [pltpu.make_async_copy(f, kept.at[k], sems.at[2 + k]) for k, f in enumerate(filters)]
        from_state = pltpu.make_async_copy(state, kept_state, sems.at[4])
        from_state.start()
        for copy in copies:
            copy.start()
    if not first:
        at_end = info[1] == 1
    for taps in (taps_one, taps_two, taps_error):
        taps[0:pitch, :] = jnp.zeros((pitch, 6 * width), BF16)
        low = pitch + rows
        taps[low:, :] = jnp.zeros((taps.shape[0] - low, 6 * width), BF16)
    for member in range(4):
        for r in range(side):
            plane[member, r * pitch + side : (r + 1) * pitch, :] = jnp.zeros((pitch - side, width), F32)

    if lead:
        from_state.wait()
        state = kept_state
    for member in range(4):
        for r in range(side):
            low = member * pixels + r * side
            strided = pl.ds(r * side * groups + group, side, stride=groups)
            if first:
                row = state[member, strided, :]
            else:
                row = jnp.where(at_end, arriving[tick - 1, member, strided, :], moved[low : low + side, :])
            plane[member, r * pitch : r * pitch + side, :] = row

    inside = lax.rem(lax.broadcasted_iota(jnp.int32, (rows, width), 0), pitch) < side

    def branch(value):
        gate = 1.0 / (1.0 + jnp.exp(-value))
        return value * gate, gate * (1.0 + value * (1.0 - gate))

    leaving = []

    def give(member, value):
        if final:
            for slot, other in enumerate(others):
                theirs = info[0] ^ (groups - 1 - slot)
                whole[member, pl.ds(theirs, pixels, stride=groups), :] = other[member * pixels : (member + 1) * pixels, :]
        for r in range(side):
            piece = value[r * pitch : r * pitch + side, :]
            if final:
                whole[member, pl.ds(r * side * groups + group, side, stride=groups), :] = piece
            else:
                low = member * pixels + r * side
                out[low : low + side, :] = piece
        if final:
            copy = pltpu.make_async_copy(whole.at[member], out.at[member], sems.at[1 + member])
            copy.start()
            leaving.append(copy)

    def pack(k):
        for t in range(9):
            if lead:
                tap, mirror = weights[k, t], weights[k, 8 - t]
            else:
                tap, mirror = filters[0][k, t, channels, :], filters[0][k, 8 - t, channels, :]
            a, b = divmod(t, 3)
            packed[k, a, b * width : (b + 1) * width, :] = jnp.concatenate(halves(tap.T), axis=1)
            packed[2 + k, a, b * width : (b + 1) * width, :] = jnp.concatenate(halves(mirror), axis=1)

    def filter_grads(k, change, taps):
        turned = turn(change, depth)
        for a in range(3):
            high = taps[a * pitch : a * pitch + depth, : 3 * width]
            low = taps[a * pitch : a * pitch + depth, 3 * width :]
            grad = jnp.dot(turned, jnp.concatenate([high, low, high], axis=0), preferred_element_type=F32)
            for b in range(3):
                tap = grad[:, b * width : (b + 1) * width]
                sums[k, 3 * a + b] = tap if first else tap + sums_in[k, 3 * a + b]

    spread(taps_one, plane[0], pitch, shifted)
    if first:
        if lead:
            copies[1].wait()
        pack(1)
    act, slope_two = branch(conv(taps_one, packed.at[1], rows, pitch))
    x_two = jnp.where(inside, plane[1] - act, 0.0)
    spread(taps_two, x_two, pitch, shifted)
    give(1, x_two)
    change_two = jnp.where(inside, plane[3] * slope_two, 0.0)
    spread(taps_error, change_two, pitch, shifted)
    if first:
        if lead:
            copies[0].wait()
        pack(0)
    raw_one = conv(taps_two, packed.at[0], rows, pitch)
    raw_error = conv(taps_error, packed.at[3], rows, pitch)
    act, slope_one = branch(raw_one)
    give(0, plane[0] - act)
    d_one = jnp.where(inside, plane[2] + raw_error, 0.0)
    give(2, d_one)
    filter_grads(1, change_two, taps_one)
    change_one = jnp.where(inside, d_one * slope_one, 0.0)
    spread(taps_error, change_one, pitch, shifted)
    give(3, plane[3] + conv(taps_error, packed.at[2], rows, pitch))

    filter_grads(0, change_one, taps_two)
    if last:
        part = width // shares
        for d in range(shares):
            rows_of = pl.ds(pl.multiple_of(lax.rem(info[2] + d, shares) * part, part), part)
            if pieces == 0:
                grads[0][d] = sums[:, :, d * part : (d + 1) * part, :]
            elif d == 0 or pieces == 1:
                grads[d][...] = sums[:, :, rows_of, :]
            else:
                for k in range(2):
                    grads[2 * d - 1 + k][...] = sums[k, :, rows_of, :]
    if lead:
        copies[2].wait()
        copies[3].wait()
    for copy in leaving:
        copy.wait()


def step(dims, k_turn, tick, last, info, operands, after, effort, pieces):
    side, pitch, groups, width, shares = dims
    pixels, rows = side * side, side * pitch
    depth = -(-rows // 128) * 128
    first, lead, final = tick == 0, tick == 0 and not after, last and k_turn == 0
    in_vmem = pl.BlockSpec(memory_space=VMEM)
    anywhere = pl.BlockSpec(memory_space=ANY)

    def local(array):
        return pltpu.with_memory_space_constraint(array, VMEM)

    def far(array):
        return pltpu.with_memory_space_constraint(array, HBM)

    sums = (2, 9, width, width)
    specs, args = [pl.BlockSpec(memory_space=pltpu.SMEM)], [info]

    def give(array, where, spec):
        args.append(where(array))
        specs.append(spec)

    if first:
        state, *filters = operands
        give(state, far if lead else local, anywhere if lead else in_vmem)
        for f in filters:
            give(f, far if lead else local, anywhere if lead else in_vmem)
    else:
        moved, arriving, packed, before, *others = operands
        give(moved, lambda x: x, in_vmem)
        give(arriving, local, in_vmem)
        for x in (packed, before, *others):
            give(x, local, in_vmem)
    for x in after:
        give(x, lambda x: x, anywhere)

    if final:
        out_shape, out_specs = [jax.ShapeDtypeStruct((4, pixels * groups, width), F32)], [anywhere]
    else:
        out_shape, out_specs = [VMEM((4 * pixels, width), F32)], [in_vmem]
    if first:
        out_shape.append(VMEM((4, 3, 3 * width, 2 * width), BF16))
        if lead:
            out_shape += [VMEM((2, 9, groups * width, width), F32), VMEM((4, pixels * groups, width), F32)]
    if last:
        part = (2, 9, width // shares, width)
        if pieces == 0:
            out_shape.append(VMEM((shares, *part), F32))
        else:
            out_shape += [VMEM(part, F32)] + [VMEM(part if pieces == 1 else part[1:], F32)] * (pieces * (shares - 1))
    else:
        out_shape.append(VMEM(sums, F32))
    out_specs += [in_vmem] * (len(out_shape) - 1)

    scratch = [VMEM((4, rows, width), F32)] + [VMEM((2 * pitch + depth, 6 * width), BF16)] * 3 + [pltpu.SemaphoreType.DMA((6,)), VMEM((rows + 16, width), F32)]
    if lead:
        scratch.append(VMEM(sums, F32))
    if last:
        scratch.append(VMEM(sums, F32))
    if final:
        scratch.append(VMEM((4, pixels * groups, width), F32))
    return pl.pallas_call(
        functools.partial(step_kernel, dims, k_turn, tick, last, len(after), pieces),
        out_shape=out_shape,
        in_specs=specs,
        out_specs=out_specs,
        scratch_shapes=scratch,
        compiler_params=pltpu.CompilerParams(vmem_limit_bytes=VMEM_LIMIT),
        cost_estimate=pl.CostEstimate(flops=effort, bytes_accessed=1, transcendentals=0),
        name=f"tick_{tick}_turn_{k_turn}",
    )(*args)


def add_kernel(stacked, n_terms, n_parts, n_after, *refs):
    outs = refs[n_terms + n_parts + n_after :]
    for k in range(2):
        terms = [refs[0][n, k] for n in range(refs[0].shape[0])] if stacked else [refs[0][k]]
        terms += [ref[k] for ref in refs[1:n_terms]] + [ref[...] for ref in refs[n_terms + k : n_terms + n_parts : 2]]
        total = functools.reduce(lambda x, y: x + y, terms)
        if len(outs) > 1:
            outs[k][...] = total
        else:
            outs[0][k] = total


def add(stacked, terms, parts, after, effort, out, name):
    in_vmem = pl.BlockSpec(memory_space=VMEM)
    return pl.pallas_call(
        functools.partial(add_kernel, stacked, len(terms), len(parts), len(after)),
        out_shape=out,
        in_specs=[in_vmem] * (len(terms) + len(parts)) + [pl.BlockSpec(memory_space=ANY)] * len(after),
        out_specs=[in_vmem] * len(out) if isinstance(out, list) else in_vmem,
        compiler_params=pltpu.CompilerParams(vmem_limit_bytes=VMEM_LIMIT),
        cost_estimate=pl.CostEstimate(flops=effort, bytes_accessed=1, transcendentals=0),
        name=name,
    )(*terms, *parts, *after)


def on_device(section_state, arriving, first_weight, second_weight):
    _, _, _, pixels, channels = section_state.shape
    width = first_weight.shape[-1]
    groups = channels // width
    side = math.isqrt(pixels)
    pitch = -(-(side + 1) // 16) * 16
    sections, reps = lax.axis_size("section"), lax.axis_size("rep")
    shares = reps // groups
    dims = (side, pitch, groups, width, shares)
    ticks = arriving.shape[0] + 1

    state = section_state[0].reshape(4, pixels * groups, width)
    arrivals = arriving.reshape(ticks - 1, 4, pixels * groups, width)
    filters = (first_weight[0, 0], second_weight[0, 0])

    rep = lax.axis_index("rep")
    at_end = lax.axis_index("section") == sections - 1
    info = jnp.stack([rep // shares, at_end.astype(jnp.int32), rep % shares]).astype(jnp.int32)

    turns = list(range(groups - 1, -1, -1))
    down = [(s, s - 1) for s in range(1, sections)]
    moved, packed, sums, outs, totals, waiting, mine = {}, {}, {}, {}, {}, {}, None

    def swap(part, d):
        return lax.ppermute(part, "rep", [(r, r - r % shares + (r % shares + d) % shares) for r in range(reps)])

    order = PLAN["order"] or sorted(((t, p) for t in range(ticks) for p in range(groups)), key=lambda i: (i[1] + 2 * i[0], -i[0]))
    part = (2, 9, width // shares, width)
    previous = None
    for item in order:
        tick, p = item
        k, last = turns[p], tick == ticks - 1
        after = waiting.pop(item, []) + ([] if previous is None else [previous])
        effort, pieces = PLAN["step"].get(item, 1), PLAN["swap"].get(p, 2)
        if tick == 0:
            results = list(step(dims, k, tick, last, info, (state, *filters), after, effort, pieces))
            if previous is None:
                filters, state = (results.pop(2),), results.pop(2)
            out, packed[p], *grads = results
        else:
            others = [outs[o] for o in range(p)] if last and k == 0 else []
            out, *grads = step(dims, k, tick, last, info, (moved[p], arrivals, packed[p], sums[p], *others), after, effort, pieces)
        previous = out
        if not last:
            sums[p] = grads[0]
            moved[p] = lax.ppermute(out, "section", down)
            continue
        outs[p] = out
        terms, parts = [grads[0]], []
        if pieces == 0:
            chips = [list(range(low, low + shares)) for low in range(0, reps, shares)]
            terms = [lax.all_to_all(grads[0], "rep", 0, 0, axis_index_groups=chips)]
        else:
            parts = [swap(x, 1 + h // pieces) for h, x in enumerate(grads[1:])]
            if pieces == 1:
                terms, parts = terms + parts, []
        if k == 0:
            mine, swapped = terms[0], parts
            break
        if p == 1:
            terms.append(totals.pop(0))
        after = [moved[q] for q in PLAN["wait"].get(p, [])]
        total = add(pieces == 0, terms, parts, after, PLAN["add"].get(p, 1), VMEM(part, F32), f"add_turn_{k}")
        if p in PLAN["need"]:
            waiting.setdefault(PLAN["need"][p], []).append(total)
        mask = 1 if p == 0 else k
        totals[p] = lax.ppermute(total, "rep", [(r, (r // shares ^ mask) * shares + r % shares) for r in range(reps)])
        if p in PLAN["znd"]:
            waiting.setdefault(PLAN["znd"][p], []).append(totals[p])

    kept = add(False, [mine, *totals.values()], [], [], PLAN["sum"], VMEM(part, F32), "add_arrived")
    out = [jax.ShapeDtypeStruct(part[1:], F32)] * 2
    first_grad, second_grad = add(False, [kept], swapped, [], PLAN["last"], out, "add_last")
    returned = outs[groups - 1].reshape(1, 4, 1, pixels, channels)
    return (returned, first_grad[None, None], second_grad[None, None])


def solution(mesh):
    return jax.shard_map(
        on_device,
        mesh=mesh,
        in_specs=(
            P("section", None, "rep", None, None),
            P(None, None, "rep", None, None),
            P("section", None, None, None, None),
            P("section", None, None, None, None),
        ),
        out_specs=(
            P("section", None, "rep", None, None),
            P("section", None, None, "rep", None),
            P("section", None, None, "rep", None),
        ),
        check_vma=False,
    )
```

time: 114 us -> 106 us (0.930)
  the two profiles are of different devices: /device:TPU:6 before, /device:TPU:0 now
where the time goes in v2:
time: 106 us
  Pallas kernels  42.9 us (40%)
  waiting for transfers between devices  39.5 us (37%)
  starting transfers between devices  18.1 us (17%)
  blocking collectives  4.68 us (4%)
    pallas_call x12, Pallas kernels, step(): pl.pallas_call(functools.partial(step_kernel, dims, k_turn, tick, last, l...  41.7 us
    ppermute x8, waiting for transfers between devices, on_device(): moved[p] = lax.ppermute(out, 'section', down)  32 us
    ppermute x8, starting transfers between devices, on_device(): moved[p] = lax.ppermute(out, 'section', down)  10.7 us
    ppermute x3, waiting for transfers between devices, on_device(): lax.ppermute(total, 'rep', [(r, (r // shares ^ mask) * shares + r % share...  7.42 us
    ppermute x3, starting transfers between devices, on_device(): lax.ppermute(total, 'rep', [(r, (r // shares ^ mask) * shares + r % share...  6.19 us
    all_to_all x1, blocking collectives, on_device(): terms = [lax.all_to_all(grads[0], 'rep', 0, 0, axis_index_groups=chips)]  4.68 us
  transfers between devices with their start and end apart: 16, of which 8 were waited for; matrix products, arithmetic and copies ran while one was open for 0% of the time, Pallas kernels for 31%

profile of v2, /device:TPU:0, one launch (start us, length us, event | category | flops | bytes accessed | tf_op | source)
XLA Modules:
  0.0 106.2 jit_solution(8634841681921541938)
XLA Ops:
  0.7 0.1 pad_add_fusion.refs_0_
  0.7 5.2 %tick_0_turn_3.1 = (f32[784,128]{1,0:T(8,128)S(1)}, bf16[4,3,384,256]{3,2,1,0:T(8,128)(2,1)S(1)}, f32[2,9,512,128]{3,2,1,0:T(8,128)S(1)}, f32[4,784,128]{2,1,0:T(8,128)S(1)}, f32[2,9,128,128]{3,2,1,0:T(8,128)S(1)}) custom-call(s32[3]{0:T(128)S(1)} %pad_add_fusion.refs_0_, f32[4,784,128]{2,1,0:T(8,128)} %bitcast.20, f32[9,512,128]{2,1,0:T(8,128)} %bitcast.18, ...), custom_call_target="tpu_custom_call" | custom-call | flops 1 | bytes 1 | tf_op jit(solution)/shard_map/tick_0_turn_3/pallas_call | solution.py:266
  6.0 1.3 %collective-permute-start.1 = (f32[784,128]{1,0:T(8,128)S(1)}, f32[784,128]{1,0:T(8,128)S(1)}, u32[]{:S(2)}, u32[]{:S(2)}) collective-permute-start(f32[784,128]{1,0:T(8,128)S(1)} %get-tuple-element.42.refs_3_), channel_id=1, source_target_pairs={{8,0},{16,8},{24,16},{9,1},{17,9},{25,17},{10,2},{18,10},{26,18},{... | collective-permute-start | bytes 1204232 | tf_op jit(solution)/shard_map/ppermute | solution.py:348
  7.3 0.0 copy-start
  7.3 3.3 %tick_0_turn_2.1 = (f32[784,128]{1,0:T(8,128)S(1)}, bf16[4,3,384,256]{3,2,1,0:T(8,128)(2,1)S(1)}, f32[2,9,128,128]{3,2,1,0:T(8,128)S(1)}) custom-call(s32[3]{0:T(128)S(1)} %pad_add_fusion.refs_0_, f32[4,784,128]{2,1,0:T(8,128)S(1)} %get-tuple-element.40.refs_1_, f32[2,9,512,128]{3,2,1,0:T(8,128)S(1)} %get-tuple-element.41.refs_2_, ...), custom_call_target="tpu_custom_call" | custom-call | flops 1 | bytes 1 | tf_op jit(solution)/shard_map/tick_0_turn_2/pallas_call | solution.py:266
  10.6 1.3 %collective-permute-start = (f32[784,128]{1,0:T(8,128)S(1)}, f32[784,128]{1,0:T(8,128)S(1)}, u32[]{:S(2)}, u32[]{:S(2)}) collective-permute-start(f32[784,128]{1,0:T(8,128)S(1)} %get-tuple-element.43.refs_5_), channel_id=1, source_target_pairs={{8,0},{16,8},{24,16},{9,1},{17,9},{25,17},{10,2},{18,10},{26,18},{... | collective-permute-start | bytes 1204232 | tf_op jit(solution)/shard_map/ppermute | solution.py:348
  11.9 9.0 %collective-permute-done.1.refs_1_ = f32[784,128]{1,0:T(8,128)S(1)} collective-permute-done((f32[784,128]{1,0:T(8,128)S(1)}, f32[784,128]{1,0:T(8,128)S(1)}, u32[]{:S(2)}, u32[]{:S(2)}) %collective-permute-start.1) | collective-permute-done | bytes 401440 | tf_op jit(solution)/shard_map/ppermute | solution.py:348
  20.9 3.2 %tick_1_turn_3.1 = (f32[784,128]{1,0:T(8,128)S(1)}, f32[2,9,128,128]{3,2,1,0:T(8,128)S(1)}) custom-call(s32[3]{0:T(128)S(1)} %pad_add_fusion.refs_0_, f32[784,128]{1,0:T(8,128)S(1)} %collective-permute-done.1.refs_1_, f32[2,4,784,128]{3,2,1,0:T(8,128)S(1)} %bitcast.10, bf16[4,3,384,256]{3,2,1,0:T(8,128)(2,1)S(1)} %get-tuple-element.46.refs_3_, ...), custom_call_target="tpu_custom_call" | custom-call | flops 10000000000 | bytes 1 | tf_op jit(solution)/shard_map/tick_1_turn_3/pallas_call | solution.py:266
  24.2 1.3 %collective-permute-start.5 = (f32[784,128]{1,0:T(8,128)S(1)}, f32[784,128]{1,0:T(8,128)S(1)}, u32[]{:S(2)}, u32[]{:S(2)}) collective-permute-start(f32[784,128]{1,0:T(8,128)S(1)} %get-tuple-element.48.refs_3_), channel_id=1, source_target_pairs={{8,0},{16,8},{24,16},{9,1},{17,9},{25,17},{10,2},{18,10},{26,18},{... | collective-permute-start | bytes 1204232 | tf_op jit(solution)/shard_map/ppermute | solution.py:348
  25.5 3.3 %tick_0_turn_1.1 = (f32[784,128]{1,0:T(8,128)S(1)}, bf16[4,3,384,256]{3,2,1,0:T(8,128)(2,1)S(1)}, f32[2,9,128,128]{3,2,1,0:T(8,128)S(1)}) custom-call(s32[3]{0:T(128)S(1)} %pad_add_fusion.refs_0_, f32[4,784,128]{2,1,0:T(8,128)S(1)} %get-tuple-element.40.refs_1_, f32[2,9,512,128]{3,2,1,0:T(8,128)S(1)} %get-tuple-element.41.refs_2_, ...), custom_call_target="tpu_custom_call" | custom-call | flops 1 | bytes 1 | tf_op jit(solution)/shard_map/tick_0_turn_1/pallas_call | solution.py:266
  28.8 1.5 %collective-permute-start.4 = (f32[784,128]{1,0:T(8,128)S(1)}, f32[784,128]{1,0:T(8,128)S(1)}, u32[]{:S(2)}, u32[]{:S(2)}) collective-permute-start(f32[784,128]{1,0:T(8,128)S(1)} %get-tuple-element.49.refs_5_), channel_id=1, source_target_pairs={{8,0},{16,8},{24,16},{9,1},{17,9},{25,17},{10,2},{18,10},{26,18},{... | collective-permute-start | bytes 1204232 | tf_op jit(solution)/shard_map/ppermute | solution.py:348
  30.3 0.0 collective-permute-done.refs_1_
  30.3 3.2 %tick_1_turn_2.1 = (f32[784,128]{1,0:T(8,128)S(1)}, f32[2,9,128,128]{3,2,1,0:T(8,128)S(1)}) custom-call(s32[3]{0:T(128)S(1)} %pad_add_fusion.refs_0_, f32[784,128]{1,0:T(8,128)S(1)} %collective-permute-done.refs_1_, f32[2,4,784,128]{3,2,1,0:T(8,128)S(1)} %bitcast.11, bf16[4,3,384,256]{3,2,1,0:T(8,128)(2,1)S(1)} %get-tuple-element.44.refs_3_, ...), custom_call_target="tpu_custom_call" | custom-call | flops 99999997952 | bytes 1 | tf_op jit(solution)/shard_map/tick_1_turn_2/pallas_call | solution.py:266
  33.5 3.3 %tick_0_turn_0.1 = (f32[784,128]{1,0:T(8,128)S(1)}, bf16[4,3,384,256]{3,2,1,0:T(8,128)(2,1)S(1)}, f32[2,9,128,128]{3,2,1,0:T(8,128)S(1)}) custom-call(s32[3]{0:T(128)S(1)} %pad_add_fusion.refs_0_, f32[4,784,128]{2,1,0:T(8,128)S(1)} %get-tuple-element.40.refs_1_, f32[2,9,512,128]{3,2,1,0:T(8,128)S(1)} %get-tuple-element.41.refs_2_, ...), custom_call_target="tpu_custom_call" | custom-call | flops 1 | bytes 1 | tf_op jit(solution)/shard_map/tick_0_turn_0/pallas_call | solution.py:266
  36.8 1.3 %collective-permute-start.3 = (f32[784,128]{1,0:T(8,128)S(1)}, f32[784,128]{1,0:T(8,128)S(1)}, u32[]{:S(2)}, u32[]{:S(2)}) collective-permute-start(f32[784,128]{1,0:T(8,128)S(1)} %get-tuple-element.50.refs_3_), channel_id=1, source_target_pairs={{8,0},{16,8},{24,16},{9,1},{17,9},{25,17},{10,2},{18,10},{26,18},{... | collective-permute-start | bytes 1204232 | tf_op jit(solution)/shard_map/ppermute | solution.py:348
  38.1 1.3 %collective-permute-start.2 = (f32[784,128]{1,0:T(8,128)S(1)}, f32[784,128]{1,0:T(8,128)S(1)}, u32[]{:S(2)}, u32[]{:S(2)}) collective-permute-start(f32[784,128]{1,0:T(8,128)S(1)} %get-tuple-element.51.refs_5_), channel_id=1, source_target_pairs={{8,0},{16,8},{24,16},{9,1},{17,9},{25,17},{10,2},{18,10},{26,18},{... | collective-permute-start | bytes 1204232 | tf_op jit(solution)/shard_map/ppermute | solution.py:348
  39.4 0.0 collective-permute-done.5.refs_1_
  39.4 3.2 %tick_2_turn_3.1 = (f32[784,128]{1,0:T(8,128)S(1)}, f32[2,2,9,64,128]{4,3,2,1,0:T(8,128)S(1)}) custom-call(s32[3]{0:T(128)S(1)} %pad_add_fusion.refs_0_, f32[784,128]{1,0:T(8,128)S(1)} %collective-permute-done.5.refs_1_, f32[2,4,784,128]{3,2,1,0:T(8,128)S(1)} %bitcast.12, bf16[4,3,384,256]{3,2,1,0:T(8,128)(2,1)S(1)} %get-tuple-element.46.refs_3_, ...), custom_call_target="tpu_custom_call" | custom-call | flops 1 | bytes 1 | tf_op jit(solution)/shard_map/tick_2_turn_3/pallas_call | solution.py:266
  42.6 4.7 %all_to_all.5.refs_0_ = f32[2,2,9,64,128]{4,3,2,1,0:T(8,128)S(1)} all-to-all(f32[2,2,9,64,128]{4,3,2,1,0:T(8,128)S(1)} %get-tuple-element.58), channel_id=1, replica_groups={{0,1},{2,3},{4,5},{6,7},{8,9},{10,11},{12,13},{14,15},{16,17},{18,19},{..., dimensions={0} | all-to-all | bytes 2359296 | tf_op jit(solution)/shard_map/all_to_all | solution.py:354
  47.3 0.5 collective-permute-done.4.refs_1_
  47.8 0.1 add_turn_3.1.refs_5_
  47.9 1.7 %collective-permute-start.9 = (f32[2,9,64,128]{3,2,1,0:T(8,128)S(1)}, f32[2,9,64,128]{3,2,1,0:T(8,128)S(1)}, u32[]{:S(2)}, u32[]{:S(2)}) collective-permute-start(f32[2,9,64,128]{3,2,1,0:T(8,128)S(1)} %add_turn_3.1.refs_5_), channel_id=1, source_target_pairs={{0,2},{1,3},{2,0},{3,1},{4,6},{5,7},{6,4},{7,5},{8,10},{9,11},{10,... | collective-permute-start | bytes 1769480 | tf_op jit(solution)/shard_map/ppermute | solution.py:369
  49.6 3.2 %tick_1_turn_1.1 = (f32[784,128]{1,0:T(8,128)S(1)}, f32[2,9,128,128]{3,2,1,0:T(8,128)S(1)}) custom-call(s32[3]{0:T(128)S(1)} %pad_add_fusion.refs_0_, f32[784,128]{1,0:T(8,128)S(1)} %collective-permute-done.4.refs_1_, f32[2,4,784,128]{3,2,1,0:T(8,128)S(1)} %bitcast.13, bf16[4,3,384,256]{3,2,1,0:T(8,128)(2,1)S(1)} %get-tuple-element.55.refs_3_, ...), custom_call_target="tpu_custom_call" | custom-call | flops 10000000000 | bytes 1 | tf_op jit(solution)/shard_map/tick_1_turn_1/pallas_call | solution.py:266
  52.8 1.5 %collective-permute-start.7 = (f32[784,128]{1,0:T(8,128)S(1)}, f32[784,128]{1,0:T(8,128)S(1)}, u32[]{:S(2)}, u32[]{:S(2)}) collective-permute-start(f32[784,128]{1,0:T(8,128)S(1)} %get-tuple-element.60.refs_5_), channel_id=1, source_target_pairs={{8,0},{16,8},{24,16},{9,1},{17,9},{25,17},{10,2},{18,10},{26,18},{... | collective-permute-start | bytes 1204232 | tf_op jit(solution)/shard_map/ppermute | solution.py:348
  54.3 2.1 %collective-permute-done.3.refs_1_ = f32[784,128]{1,0:T(8,128)S(1)} collective-permute-done((f32[784,128]{1,0:T(8,128)S(1)}, f32[784,128]{1,0:T(8,128)S(1)}, u32[]{:S(2)}, u32[]{:S(2)}) %collective-permute-start.3) | collective-permute-done | bytes 401440 | tf_op jit(solution)/shard_map/ppermute | solution.py:348
  56.4 3.4 %tick_2_turn_2.1 = (f32[784,128]{1,0:T(8,128)S(1)}, f32[2,9,64,128]{3,2,1,0:T(8,128)S(1)}, f32[2,9,64,128]{3,2,1,0:T(8,128)S(1)}) custom-call(s32[3]{0:T(128)S(1)} %pad_add_fusion.refs_0_, f32[784,128]{1,0:T(8,128)S(1)} %collective-permute-done.3.refs_1_, f32[2,4,784,128]{3,2,1,0:T(8,128)S(1)} %bitcast.14, ...), custom_call_target="tpu_custom_call" | custom-call | flops 1000000000 | bytes 1 | tf_op jit(solution)/shard_map/tick_2_turn_2/pallas_call | solution.py:266
  59.9 0.1 collective-permute-start.8
  59.9 5.1 %collective-permute-done.2.refs_1_ = f32[784,128]{1,0:T(8,128)S(1)} collective-permute-done((f32[784,128]{1,0:T(8,128)S(1)}, f32[784,128]{1,0:T(8,128)S(1)}, u32[]{:S(2)}, u32[]{:S(2)}) %collective-permute-start.2) | collective-permute-done | bytes 401440 | tf_op jit(solution)/shard_map/ppermute | solution.py:348
  65.0 3.2 %tick_1_turn_0.1 = (f32[784,128]{1,0:T(8,128)S(1)}, f32[2,9,128,128]{3,2,1,0:T(8,128)S(1)}) custom-call(s32[3]{0:T(128)S(1)} %pad_add_fusion.refs_0_, f32[784,128]{1,0:T(8,128)S(1)} %collective-permute-done.2.refs_1_, f32[2,4,784,128]{3,2,1,0:T(8,128)S(1)} %bitcast.15, bf16[4,3,384,256]{3,2,1,0:T(8,128)(2,1)S(1)} %get-tuple-element.52.refs_3_, ...), custom_call_target="tpu_custom_call" | custom-call | flops 10000000000 | bytes 1 | tf_op jit(solution)/shard_map/tick_1_turn_0/pallas_call | solution.py:266
  68.2 0.0 collective-permute-done.8.refs_1_
  68.3 0.0 collective-permute-done.9.refs_2_
  68.3 0.1 add_turn_2.1.refs_5_
  68.4 3.3 %collective-permute-done.7.refs_1_ = f32[784,128]{1,0:T(8,128)S(1)} collective-permute-done((f32[784,128]{1,0:T(8,128)S(1)}, f32[784,128]{1,0:T(8,128)S(1)}, u32[]{:S(2)}, u32[]{:S(2)}) %collective-permute-start.7) | collective-permute-done | bytes 401440 | tf_op jit(solution)/shard_map/ppermute | solution.py:348
  71.7 3.4 %tick_2_turn_1.1 = (f32[784,128]{1,0:T(8,128)S(1)}, f32[2,9,64,128]{3,2,1,0:T(8,128)S(1)}, f32[9,64,128]{2,1,0:T(8,128)S(1)}, f32[9,64,128]{2,1,0:T(8,128)S(1)}) custom-call(s32[3]{0:T(128)S(1)} %pad_add_fusion.refs_0_, f32[784,128]{1,0:T(8,128)S(1)} %collective-permute-done.7.refs_1_, f32[2,4,784,128]{3,2,1,0:T(8,128)S(1)} %bitcast.16, ...), custom_call_target="tpu_custom_call" | custom-call | flops 1 | bytes 1 | tf_op jit(solution)/shard_map/tick_2_turn_1/pallas_call | solution.py:266
  75.1 0.1 collective-permute-start.10
  75.2 0.5 collective-permute-start.11
  75.7 2.8 %collective-permute-start.12 = (f32[2,9,64,128]{3,2,1,0:T(8,128)S(1)}, f32[2,9,64,128]{3,2,1,0:T(8,128)S(1)}, u32[]{:S(2)}, u32[]{:S(2)}) collective-permute-start(f32[2,9,64,128]{3,2,1,0:T(8,128)S(1)} %add_turn_2.1.refs_5_), channel_id=1, source_target_pairs={{0,4},{1,5},{2,6},{3,7},{4,0},{5,1},{6,2},{7,3},{8,12},{9,13},{10,... | collective-permute-start | bytes 1769480 | tf_op jit(solution)/shard_map/ppermute | solution.py:369
  78.5 0.1 add_turn_1.1.refs_8_
  78.6 1.6 %collective-permute-start.13 = (f32[2,9,64,128]{3,2,1,0:T(8,128)S(1)}, f32[2,9,64,128]{3,2,1,0:T(8,128)S(1)}, u32[]{:S(2)}, u32[]{:S(2)}) collective-permute-start(f32[2,9,64,128]{3,2,1,0:T(8,128)S(1)} %add_turn_1.1.refs_8_), channel_id=1, source_target_pairs={{0,2},{1,3},{2,0},{3,1},{4,6},{5,7},{6,4},{7,5},{8,10},{9,11},{10,... | collective-permute-start | bytes 1769480 | tf_op jit(solution)/shard_map/ppermute | solution.py:369
  80.2 1.3 %collective-permute-start.6 = (f32[784,128]{1,0:T(8,128)S(1)}, f32[784,128]{1,0:T(8,128)S(1)}, u32[]{:S(2)}, u32[]{:S(2)}) collective-permute-start(f32[784,128]{1,0:T(8,128)S(1)} %get-tuple-element.62.refs_6_), channel_id=1, source_target_pairs={{8,0},{16,8},{24,16},{9,1},{17,9},{25,17},{10,2},{18,10},{26,18},{... | collective-permute-start | bytes 1204232 | tf_op jit(solution)/shard_map/ppermute | solution.py:348
  81.5 12.0 %collective-permute-done.6.refs_1_ = f32[784,128]{1,0:T(8,128)S(1)} collective-permute-done((f32[784,128]{1,0:T(8,128)S(1)}, f32[784,128]{1,0:T(8,128)S(1)}, u32[]{:S(2)}, u32[]{:S(2)}) %collective-permute-start.6) | collective-permute-done | bytes 401440 | tf_op jit(solution)/shard_map/ppermute | solution.py:348
  93.5 3.7 %tick_2_turn_0.1 = (f32[4,784,128]{2,1,0:T(8,128)}, f32[2,9,64,128]{3,2,1,0:T(8,128)S(1)}, f32[9,64,128]{2,1,0:T(8,128)S(1)}, f32[9,64,128]{2,1,0:T(8,128)S(1)}) custom-call(s32[3]{0:T(128)S(1)} %pad_add_fusion.refs_0_, f32[784,128]{1,0:T(8,128)S(1)} %collective-permute-done.6.refs_1_, f32[2,4,784,128]{3,2,1,0:T(8,128)S(1)} %bitcast.17, ...), custom_call_target="tpu_custom_call" | custom-call | flops 1 | bytes 1 | tf_op jit(solution)/shard_map/tick_2_turn_0/pallas_call | solution.py:266
  97.2 0.1 collective-permute-start.14
  97.2 0.5 collective-permute-start.15
  97.7 7.1 %collective-permute-done.12.refs_1_ = f32[2,9,64,128]{3,2,1,0:T(8,128)S(1)} collective-permute-done((f32[2,9,64,128]{3,2,1,0:T(8,128)S(1)}, f32[2,9,64,128]{3,2,1,0:T(8,128)S(1)}, u32[]{:S(2)}, u32[]{:S(2)}) %collective-permute-start.12) | collective-permute-done | bytes 589856 | tf_op jit(solution)/shard_map/ppermute | solution.py:369
  104.8 0.3 collective-permute-done.13.refs_2_
  105.2 0.1 add_arrived.1.refs_0_
  105.3 0.9 add_last.1
  (5 shorter events, 0.0 us)
Async XLA Ops:
  6.0 15.0 %collective-permute-start.1 = (f32[784,128]{1,0:T(8,128)S(1)}, f32[784,128]{1,0:T(8,128)S(1)}, u32[]{:S(2)}, u32[]{:S(2)}) collective-permute-start(f32[784,128]{1,0:T(8,128)S(1)} %get-tuple-element.42.refs_3_), channel_id=1, source_target_pairs={{8,0},{16,8},{24,16},{9,1},{17,9},{25,17},{10,2},{18,10},{26,18},{... | collective-permute-start | bytes 1204232 | tf_op jit(solution)/shard_map/ppermute | solution.py:348
  7.3 13.7 %copy-start = (f32[2,4,1,196,512]{4,2,3,1,0:T(1,128)S(1)}, f32[2,4,1,196,512]{4,2,3,1,0:T(1,128)}, u32[]{:S(2)}) copy-start(f32[2,4,1,196,512]{4,2,3,1,0:T(1,128)} %param.5) | copy-start | bytes 9633796
  10.6 19.7 %collective-permute-start = (f32[784,128]{1,0:T(8,128)S(1)}, f32[784,128]{1,0:T(8,128)S(1)}, u32[]{:S(2)}, u32[]{:S(2)}) collective-permute-start(f32[784,128]{1,0:T(8,128)S(1)} %get-tuple-element.43.refs_5_), channel_id=1, source_target_pairs={{8,0},{16,8},{24,16},{9,1},{17,9},{25,17},{10,2},{18,10},{26,18},{... | collective-permute-start | bytes 1204232 | tf_op jit(solution)/shard_map/ppermute | solution.py:348
  24.2 15.2 %collective-permute-start.5 = (f32[784,128]{1,0:T(8,128)S(1)}, f32[784,128]{1,0:T(8,128)S(1)}, u32[]{:S(2)}, u32[]{:S(2)}) collective-permute-start(f32[784,128]{1,0:T(8,128)S(1)} %get-tuple-element.48.refs_3_), channel_id=1, source_target_pairs={{8,0},{16,8},{24,16},{9,1},{17,9},{25,17},{10,2},{18,10},{26,18},{... | collective-permute-start | bytes 1204232 | tf_op jit(solution)/shard_map/ppermute | solution.py:348
  28.8 19.0 %collective-permute-start.4 = (f32[784,128]{1,0:T(8,128)S(1)}, f32[784,128]{1,0:T(8,128)S(1)}, u32[]{:S(2)}, u32[]{:S(2)}) collective-permute-start(f32[784,128]{1,0:T(8,128)S(1)} %get-tuple-element.49.refs_5_), channel_id=1, source_target_pairs={{8,0},{16,8},{24,16},{9,1},{17,9},{25,17},{10,2},{18,10},{26,18},{... | collective-permute-start | bytes 1204232 | tf_op jit(solution)/shard_map/ppermute | solution.py:348
  36.8 19.6 %collective-permute-start.3 = (f32[784,128]{1,0:T(8,128)S(1)}, f32[784,128]{1,0:T(8,128)S(1)}, u32[]{:S(2)}, u32[]{:S(2)}) collective-permute-start(f32[784,128]{1,0:T(8,128)S(1)} %get-tuple-element.50.refs_3_), channel_id=1, source_target_pairs={{8,0},{16,8},{24,16},{9,1},{17,9},{25,17},{10,2},{18,10},{26,18},{... | collective-permute-start | bytes 1204232 | tf_op jit(solution)/shard_map/ppermute | solution.py:348
  38.1 26.9 %collective-permute-start.2 = (f32[784,128]{1,0:T(8,128)S(1)}, f32[784,128]{1,0:T(8,128)S(1)}, u32[]{:S(2)}, u32[]{:S(2)}) collective-permute-start(f32[784,128]{1,0:T(8,128)S(1)} %get-tuple-element.51.refs_5_), channel_id=1, source_target_pairs={{8,0},{16,8},{24,16},{9,1},{17,9},{25,17},{10,2},{18,10},{26,18},{... | collective-permute-start | bytes 1204232 | tf_op jit(solution)/shard_map/ppermute | solution.py:348
  47.9 20.4 %collective-permute-start.9 = (f32[2,9,64,128]{3,2,1,0:T(8,128)S(1)}, f32[2,9,64,128]{3,2,1,0:T(8,128)S(1)}, u32[]{:S(2)}, u32[]{:S(2)}) collective-permute-start(f32[2,9,64,128]{3,2,1,0:T(8,128)S(1)} %add_turn_3.1.refs_5_), channel_id=1, source_target_pairs={{0,2},{1,3},{2,0},{3,1},{4,6},{5,7},{6,4},{7,5},{8,10},{9,11},{10,... | collective-permute-start | bytes 1769480 | tf_op jit(solution)/shard_map/ppermute | solution.py:369
  52.8 18.9 %collective-permute-start.7 = (f32[784,128]{1,0:T(8,128)S(1)}, f32[784,128]{1,0:T(8,128)S(1)}, u32[]{:S(2)}, u32[]{:S(2)}) collective-permute-start(f32[784,128]{1,0:T(8,128)S(1)} %get-tuple-element.60.refs_5_), channel_id=1, source_target_pairs={{8,0},{16,8},{24,16},{9,1},{17,9},{25,17},{10,2},{18,10},{26,18},{... | collective-permute-start | bytes 1204232 | tf_op jit(solution)/shard_map/ppermute | solution.py:348
  59.9 8.4 %collective-permute-start.8 = (f32[2,9,64,128]{3,2,1,0:T(8,128)S(1)}, f32[2,9,64,128]{3,2,1,0:T(8,128)S(1)}, u32[]{:S(2)}, u32[]{:S(2)}) collective-permute-start(f32[2,9,64,128]{3,2,1,0:T(8,128)S(1)} %get-tuple-element.66), channel_id=1, source_target_pairs={{0,1},{1,0},{2,3},{3,2},{4,5},{5,4},{6,7},{7,6},{8,9},{9,8},{10,11... | collective-permute-start | bytes 1769480 | tf_op jit(solution)/shard_map/ppermute | solution.py:327
  75.1 3.4 %collective-permute-start.10 = (f32[9,64,128]{2,1,0:T(8,128)S(1)}, f32[9,64,128]{2,1,0:T(8,128)S(1)}, u32[]{:S(2)}, u32[]{:S(2)}) collective-permute-start(f32[9,64,128]{2,1,0:T(8,128)S(1)} %get-tuple-element.69), channel_id=1, source_target_pairs={{0,1},{1,0},{2,3},{3,2},{4,5},{5,4},{6,7},{7,6},{8,9},{9,8},{10,11... | collective-permute-start | bytes 884744 | tf_op jit(solution)/shard_map/ppermute | solution.py:327
  75.2 3.3 %collective-permute-start.11 = (f32[9,64,128]{2,1,0:T(8,128)S(1)}, f32[9,64,128]{2,1,0:T(8,128)S(1)}, u32[]{:S(2)}, u32[]{:S(2)}) collective-permute-start(f32[9,64,128]{2,1,0:T(8,128)S(1)} %get-tuple-element.70), channel_id=1, source_target_pairs={{0,1},{1,0},{2,3},{3,2},{4,5},{5,4},{6,7},{7,6},{8,9},{9,8},{10,11... | collective-permute-start | bytes 884744 | tf_op jit(solution)/shard_map/ppermute | solution.py:327
  75.7 29.2 %collective-permute-start.12 = (f32[2,9,64,128]{3,2,1,0:T(8,128)S(1)}, f32[2,9,64,128]{3,2,1,0:T(8,128)S(1)}, u32[]{:S(2)}, u32[]{:S(2)}) collective-permute-start(f32[2,9,64,128]{3,2,1,0:T(8,128)S(1)} %add_turn_2.1.refs_5_), channel_id=1, source_target_pairs={{0,4},{1,5},{2,6},{3,7},{4,0},{5,1},{6,2},{7,3},{8,12},{9,13},{10,... | collective-permute-start | bytes 1769480 | tf_op jit(solution)/shard_map/ppermute | solution.py:369
  78.6 26.6 %collective-permute-start.13 = (f32[2,9,64,128]{3,2,1,0:T(8,128)S(1)}, f32[2,9,64,128]{3,2,1,0:T(8,128)S(1)}, u32[]{:S(2)}, u32[]{:S(2)}) collective-permute-start(f32[2,9,64,128]{3,2,1,0:T(8,128)S(1)} %add_turn_1.1.refs_8_), channel_id=1, source_target_pairs={{0,2},{1,3},{2,0},{3,1},{4,6},{5,7},{6,4},{7,5},{8,10},{9,11},{10,... | collective-permute-start | bytes 1769480 | tf_op jit(solution)/shard_map/ppermute | solution.py:369
  80.2 13.3 %collective-permute-start.6 = (f32[784,128]{1,0:T(8,128)S(1)}, f32[784,128]{1,0:T(8,128)S(1)}, u32[]{:S(2)}, u32[]{:S(2)}) collective-permute-start(f32[784,128]{1,0:T(8,128)S(1)} %get-tuple-element.62.refs_6_), channel_id=1, source_target_pairs={{8,0},{16,8},{24,16},{9,1},{17,9},{25,17},{10,2},{18,10},{26,18},{... | collective-permute-start | bytes 1204232 | tf_op jit(solution)/shard_map/ppermute | solution.py:348
  97.2 8.1 %collective-permute-start.14 = (f32[9,64,128]{2,1,0:T(8,128)S(1)}, f32[9,64,128]{2,1,0:T(8,128)S(1)}, u32[]{:S(2)}, u32[]{:S(2)}) collective-permute-start(f32[9,64,128]{2,1,0:T(8,128)S(1)} %get-tuple-element.73), channel_id=1, source_target_pairs={{0,1},{1,0},{2,3},{3,2},{4,5},{5,4},{6,7},{7,6},{8,9},{9,8},{10,11... | collective-permute-start | bytes 884744 | tf_op jit(solution)/shard_map/ppermute | solution.py:327
  97.2 8.0 %collective-permute-start.15 = (f32[9,64,128]{2,1,0:T(8,128)S(1)}, f32[9,64,128]{2,1,0:T(8,128)S(1)}, u32[]{:S(2)}, u32[]{:S(2)}) collective-permute-start(f32[9,64,128]{2,1,0:T(8,128)S(1)} %get-tuple-element.74), channel_id=1, source_target_pairs={{0,1},{1,0},{2,3},{3,2},{4,5},{5,4},{6,7},{7,6},{8,9},{9,8},{10,11... | collective-permute-start | bytes 884744 | tf_op jit(solution)/shard_map/ppermute | solution.py:327

commit v3 on v2

--- a/solution.py
+++ b/solution.py
@@ -11,7 +11,7 @@
 F32, BF16 = jnp.float32, jnp.bfloat16
 VMEM_LIMIT = 8 * 2**20
 VMEM, HBM, ANY = pltpu.VMEM, pltpu.HBM, pl.ANY
-PLAN = {'step': {(1, 0): 10000000000, (1, 1): 100000000000, (1, 2): 10000000000, (2, 1): 1000000000, (1, 3): 10000000000}, 'add': {0: 1000000000}, 'need': {0: (1, 2), 2: (2, 3), 1: (2, 2)}, 'wait': {0: [2]}, 'znd': {}, 'swap': {3: 2, 0: 0, 1: 1, 2: 2}, 'sum': 10000000000, 'last': 1, 'order': ((0, 0), (0, 1), (1, 0), (0, 2), (1, 1), (0, 3), (2, 0), (1, 2), (2, 1), (1, 3), (2, 2), (2, 3))}
+PLAN = {'step': {(0, 0): 10000000000, (0, 2): 1000000000, (0, 3): 1000000000, (2, 1): 1000000000, (1, 2): 100000000000}, 'add': {1: 100000000000, 2: 1000000000, 3: 1000000000}, 'need': {0: (2, 1), 1: (2, 2), 2: (2, 3)}, 'wait': {}, 'znd': {}, 'swap': {3: 2, 0: 2, 1: 1, 2: 2}, 'sum': 1, 'last': 1, 'order': ((0, 0), (0, 2), (0, 1), (1, 0), (1, 1), (0, 3), (2, 0), (2, 1), (1, 2), (1, 3), (2, 2), (2, 3))}
 
 
 def halves(value):
@@ -287,6 +287,12 @@
             outs[0][k] = total
 
 
+def arrived_kernel(info, mine, beside, relayed, far, out):
+    outer = jnp.logical_or(info[0] == 0, info[0] == 3)
+    for k in range(2):
+        out[k] = mine[k] + beside[k] + relayed[k] + jnp.where(outer, far[k], 0.0)
+
+
 def add(stacked, terms, parts, after, effort, out, name):
     in_vmem = pl.BlockSpec(memory_space=VMEM)
     return pl.pallas_call(
@@ -325,6 +331,9 @@
 
     def swap(part, d):
         return lax.ppermute(part, "rep", [(r, r - r % shares + (r % shares + d) % shares) for r in range(reps)])
+
+    def between(total, keepers):
+        return lax.ppermute(total, "rep", [(a * shares + n, b * shares + n) for a, b in keepers for n in range(shares)])
 
     order = PLAN["order"] or sorted(((t, p) for t in range(ticks) for p in range(groups)), key=lambda i: (i[1] + 2 * i[0], -i[0]))
     part = (2, 9, width // shares, width)
@@ -360,17 +369,33 @@
             mine, swapped = terms[0], parts
             break
         if p == 1:
-            terms.append(totals.pop(0))
+            terms.append(totals[0])
         after = [moved[q] for q in PLAN["wait"].get(p, [])]
-        total = add(pieces == 0, terms, parts, after, PLAN["add"].get(p, 1), VMEM(part, F32), f"add_turn_{k}")
+        own_total = add(pieces == 0, terms, parts, after, PLAN["add"].get(p, 1), VMEM(part, F32), f"add_turn_{k}")
         if p in PLAN["need"]:
-            waiting.setdefault(PLAN["need"][p], []).append(total)
-        mask = 1 if p == 0 else k
-        totals[p] = lax.ppermute(total, "rep", [(r, (r // shares ^ mask) * shares + r % shares) for r in range(reps)])
-        if p in PLAN["znd"]:
-            waiting.setdefault(PLAN["znd"][p], []).append(totals[p])
-
-    kept = add(False, [mine, *totals.values()], [], [], PLAN["sum"], VMEM(part, F32), "add_arrived")
+            waiting.setdefault(PLAN["need"][p], []).append(own_total)
+        if p == 0:
+            first_total = own_total
+            totals[0] = between(own_total, [(0, 1), (3, 2)])
+        elif p == 1:
+            totals[1] = between(own_total, [(0, 1), (3, 2), (1, 3), (2, 0)])
+            relay = add(False, [first_total, totals[1]], [], [], PLAN["add"].get(3, 1), VMEM(part, F32), "add_relay")
+            if 3 in PLAN["need"]:
+                waiting.setdefault(PLAN["need"][3], []).append(relay)
+            totals[3] = between(relay, [(1, 2), (2, 1)])
+        else:
+            totals[2] = between(own_total, [(0, 1), (1, 0), (2, 3), (3, 2)])
+
+    in_vmem = pl.BlockSpec(memory_space=VMEM)
+    kept = pl.pallas_call(
+        arrived_kernel,
+        out_shape=VMEM(part, F32),
+        in_specs=[pl.BlockSpec(memory_space=pltpu.SMEM)] + [in_vmem] * 4,
+        out_specs=in_vmem,
+        compiler_params=pltpu.CompilerParams(vmem_limit_bytes=VMEM_LIMIT),
+        cost_estimate=pl.CostEstimate(flops=PLAN["sum"], bytes_accessed=1, transcendentals=0),
+        name="add_arrived",
+    )(info, mine, totals[2], totals[3], totals[1])
     out = [jax.ShapeDtypeStruct(part[1:], F32)] * 2
     first_grad, second_grad = add(False, [kept], swapped, [], PLAN["last"], out, "add_last")
     returned = outs[groups - 1].reshape(1, 4, 1, pixels, channels)

time: 106 us -> 99.4 us (0.938)
  the two profiles are of different devices: /device:TPU:0 before, /device:TPU:20 now
where the time goes in v3:
time: 99.4 us; the launch traced here: 99 us
  Pallas kernels  44.6 us (45%)
  starting transfers between devices  31.3 us (31%)
  waiting for transfers between devices  22 us (22%)
    pallas_call x12, Pallas kernels, step(): pl.pallas_call(functools.partial(step_kernel, dims, k_turn, tick, last, l...  42.7 us
    ppermute x8, starting transfers between devices, on_device(): moved[p] = lax.ppermute(out, 'section', down)  24.3 us
    ppermute x8, waiting for transfers between devices, on_device(): moved[p] = lax.ppermute(out, 'section', down)  15.8 us
    ppermute x4, waiting for transfers between devices, between(): lax.ppermute(total, 'rep', [(a * shares + n, b * shares + n) for a, b in...  6.25 us
    ppermute x4, starting transfers between devices, between(): lax.ppermute(total, 'rep', [(a * shares + n, b * shares + n) for a, b in...  5.13 us
  transfers between devices with their start and end apart: 19, of which 8 were waited for; matrix products, arithmetic and copies ran while one was open for 0% of the time, Pallas kernels for 39%

profile of v3, /device:TPU:20, one launch (start us, length us, event | category | flops | bytes accessed | tf_op | source)
XLA Modules:
  0.0 99.0 jit_solution(12995116505595226274)
XLA Ops:
  0.7 0.1 pad_add_fusion.refs_0_.info
  0.7 5.2 %tick_0_turn_3.1 = (f32[784,128]{1,0:T(8,128)S(1)}, bf16[4,3,384,256]{3,2,1,0:T(8,128)(2,1)S(1)}, f32[2,9,512,128]{3,2,1,0:T(8,128)S(1)}, f32[4,784,128]{2,1,0:T(8,128)S(1)}, f32[2,9,128,128]{3,2,1,0:T(8,128)S(1)}) custom-call(s32[3]{0:T(128)S(1)} %pad_add_fusion.refs_0_.info, f32[4,784,128]{2,1,0:T(8,128)} %bitcast.20, f32[9,512,128]{2,1,0:T(8,128)} %bitcast.18, ...), custom_call_target="tpu_custom_call" | custom-call | flops 10000000000 | bytes 1 | tf_op jit(solution)/shard_map/tick_0_turn_3/pallas_call | solution.py:266
  6.0 3.3 %collective-permute-start.1 = (f32[784,128]{1,0:T(8,128)S(1)}, f32[784,128]{1,0:T(8,128)S(1)}, u32[]{:S(2)}, u32[]{:S(2)}) collective-permute-start(f32[784,128]{1,0:T(8,128)S(1)} %get-tuple-element.44.refs_3_), channel_id=1, source_target_pairs={{8,0},{16,8},{24,16},{9,1},{17,9},{25,17},{10,2},{18,10},{26,18},{... | collective-permute-start | bytes 1204232 | tf_op jit(solution)/shard_map/ppermute | solution.py:357
  9.3 3.3 %tick_0_turn_1.1 = (f32[784,128]{1,0:T(8,128)S(1)}, bf16[4,3,384,256]{3,2,1,0:T(8,128)(2,1)S(1)}, f32[2,9,128,128]{3,2,1,0:T(8,128)S(1)}) custom-call(s32[3]{0:T(128)S(1)} %pad_add_fusion.refs_0_.info, f32[4,784,128]{2,1,0:T(8,128)S(1)} %get-tuple-element.42.refs_1_, f32[2,9,512,128]{3,2,1,0:T(8,128)S(1)} %get-tuple-element.43.refs_2_, ...), custom_call_target="tpu_custom_call" | custom-call | flops 1000000000 | bytes 1 | tf_op jit(solution)/shard_map/tick_0_turn_1/pallas_call | solution.py:266
  12.6 0.0 copy-start
  12.7 3.3 %tick_0_turn_2.1 = (f32[784,128]{1,0:T(8,128)S(1)}, bf16[4,3,384,256]{3,2,1,0:T(8,128)(2,1)S(1)}, f32[2,9,128,128]{3,2,1,0:T(8,128)S(1)}) custom-call(s32[3]{0:T(128)S(1)} %pad_add_fusion.refs_0_.info, f32[4,784,128]{2,1,0:T(8,128)S(1)} %get-tuple-element.42.refs_1_, f32[2,9,512,128]{3,2,1,0:T(8,128)S(1)} %get-tuple-element.43.refs_2_, ...), custom_call_target="tpu_custom_call" | custom-call | flops 1 | bytes 1 | tf_op jit(solution)/shard_map/tick_0_turn_2/pallas_call | solution.py:266
  16.0 2.4 %collective-permute-start = (f32[784,128]{1,0:T(8,128)S(1)}, f32[784,128]{1,0:T(8,128)S(1)}, u32[]{:S(2)}, u32[]{:S(2)}) collective-permute-start(f32[784,128]{1,0:T(8,128)S(1)} %get-tuple-element.46.refs_5_), channel_id=1, source_target_pairs={{8,0},{16,8},{24,16},{9,1},{17,9},{25,17},{10,2},{18,10},{26,18},{... | collective-permute-start | bytes 1204232 | tf_op jit(solution)/shard_map/ppermute | solution.py:357
  18.4 0.5 collective-permute-done.1.refs_1_
  18.9 3.2 %tick_1_turn_3.1 = (f32[784,128]{1,0:T(8,128)S(1)}, f32[2,9,128,128]{3,2,1,0:T(8,128)S(1)}) custom-call(s32[3]{0:T(128)S(1)} %pad_add_fusion.refs_0_.info, f32[784,128]{1,0:T(8,128)S(1)} %collective-permute-done.1.refs_1_, f32[2,4,784,128]{3,2,1,0:T(8,128)S(1)} %bitcast.10, bf16[4,3,384,256]{3,2,1,0:T(8,128)(2,1)S(1)} %get-tuple-element.49.refs_3_, ...), custom_call_target="tpu_custom_call" | custom-call | flops 1 | bytes 1 | tf_op jit(solution)/shard_map/tick_1_turn_3/pallas_call | solution.py:266
  22.1 4.4 %collective-permute-start.5 = (f32[784,128]{1,0:T(8,128)S(1)}, f32[784,128]{1,0:T(8,128)S(1)}, u32[]{:S(2)}, u32[]{:S(2)}) collective-permute-start(f32[784,128]{1,0:T(8,128)S(1)} %get-tuple-element.51.refs_5_), channel_id=1, source_target_pairs={{8,0},{16,8},{24,16},{9,1},{17,9},{25,17},{10,2},{18,10},{26,18},{... | collective-permute-start | bytes 1204232 | tf_op jit(solution)/shard_map/ppermute | solution.py:357
  26.6 3.5 %collective-permute-done.refs_1_ = f32[784,128]{1,0:T(8,128)S(1)} collective-permute-done((f32[784,128]{1,0:T(8,128)S(1)}, f32[784,128]{1,0:T(8,128)S(1)}, u32[]{:S(2)}, u32[]{:S(2)}) %collective-permute-start) | collective-permute-done | bytes 401440 | tf_op jit(solution)/shard_map/ppermute | solution.py:357
  30.1 3.2 %tick_1_turn_2.1 = (f32[784,128]{1,0:T(8,128)S(1)}, f32[2,9,128,128]{3,2,1,0:T(8,128)S(1)}) custom-call(s32[3]{0:T(128)S(1)} %pad_add_fusion.refs_0_.info, f32[784,128]{1,0:T(8,128)S(1)} %collective-permute-done.refs_1_, f32[2,4,784,128]{3,2,1,0:T(8,128)S(1)} %bitcast.11, bf16[4,3,384,256]{3,2,1,0:T(8,128)(2,1)S(1)} %get-tuple-element.47.refs_3_, ...), custom_call_target="tpu_custom_call" | custom-call | flops 1 | bytes 1 | tf_op jit(solution)/shard_map/tick_1_turn_2/pallas_call | solution.py:266
  33.3 3.0 %collective-permute-start.4 = (f32[784,128]{1,0:T(8,128)S(1)}, f32[784,128]{1,0:T(8,128)S(1)}, u32[]{:S(2)}, u32[]{:S(2)}) collective-permute-start(f32[784,128]{1,0:T(8,128)S(1)} %get-tuple-element.52.refs_3_), channel_id=1, source_target_pairs={{8,0},{16,8},{24,16},{9,1},{17,9},{25,17},{10,2},{18,10},{26,18},{... | collective-permute-start | bytes 1204232 | tf_op jit(solution)/shard_map/ppermute | solution.py:357
  36.4 1.9 %collective-permute-start.3 = (f32[784,128]{1,0:T(8,128)S(1)}, f32[784,128]{1,0:T(8,128)S(1)}, u32[]{:S(2)}, u32[]{:S(2)}) collective-permute-start(f32[784,128]{1,0:T(8,128)S(1)} %get-tuple-element.45.refs_3_), channel_id=1, source_target_pairs={{8,0},{16,8},{24,16},{9,1},{17,9},{25,17},{10,2},{18,10},{26,18},{... | collective-permute-start | bytes 1204232 | tf_op jit(solution)/shard_map/ppermute | solution.py:357
  38.3 3.6 %tick_0_turn_0.1 = (f32[784,128]{1,0:T(8,128)}, bf16[4,3,384,256]{3,2,1,0:T(8,128)(2,1)S(1)}, f32[2,9,128,128]{3,2,1,0:T(8,128)S(1)}) custom-call(s32[3]{0:T(128)S(1)} %pad_add_fusion.refs_0_.info, f32[4,784,128]{2,1,0:T(8,128)S(1)} %get-tuple-element.42.refs_1_, f32[2,9,512,128]{3,2,1,0:T(8,128)S(1)} %get-tuple-element.43.refs_2_, ...), custom_call_target="tpu_custom_call" | custom-call | flops 1000000000 | bytes 1 | tf_op jit(solution)/shard_map/tick_0_turn_0/pallas_call | solution.py:266
  41.9 3.4 %tick_2_turn_3.1 = (f32[784,128]{1,0:T(8,128)S(1)}, f32[2,9,64,128]{3,2,1,0:T(8,128)S(1)}, f32[9,64,128]{2,1,0:T(8,128)S(1)}, f32[9,64,128]{2,1,0:T(8,128)S(1)}) custom-call(s32[3]{0:T(128)S(1)} %pad_add_fusion.refs_0_.info, f32[784,128]{1,0:T(8,128)S(1)} %collective-permute-done.5.refs_1_, f32[2,4,784,128]{3,2,1,0:T(8,128)S(1)} %bitcast.12, ...), custom_call_target="tpu_custom_call" | custom-call | flops 1 | bytes 1 | tf_op jit(solution)/shard_map/tick_2_turn_3/pallas_call | solution.py:266
  45.3 0.1 collective-permute-start.6
  45.4 0.5 collective-permute-start.7
  45.9 1.9 %collective-permute-start.2 = (f32[784,128]{1,0:T(8,128)}, f32[784,128]{1,0:T(8,128)}, u32[]{:S(2)}, u32[]{:S(2)}) collective-permute-start(f32[784,128]{1,0:T(8,128)} %get-tuple-element.53.refs_5_), channel_id=1, source_target_pairs={{8,0},{16,8},{24,16},{9,1},{17,9},{25,17},{10,2},{18,10},{26,18},{... | collective-permute-start | bytes 1204232 | tf_op jit(solution)/shard_map/ppermute | solution.py:357
  47.8 0.1 add_turn_3.1.refs_5_.refs_0_
  47.9 1.3 %collective-permute-start.11 = (f32[2,9,64,128]{3,2,1,0:T(8,128)S(1)}, f32[2,9,64,128]{3,2,1,0:T(8,128)S(1)}, u32[]{:S(2)}, u32[]{:S(2)}) collective-permute-start(f32[2,9,64,128]{3,2,1,0:T(8,128)S(1)} %add_turn_3.1.refs_5_.refs_0_), channel_id=1, source_target_pairs={{0,2},{1,3},{6,4},{7,5},{8,10},{9,11},{14,12},{15,13},{16,18},{17,... | collective-permute-start | bytes 1769480 | tf_op jit(solution)/shard_map/ppermute | solution.py:336
  49.2 3.4 %tick_2_turn_2.1 = (f32[784,128]{1,0:T(8,128)S(1)}, f32[2,9,64,128]{3,2,1,0:T(8,128)S(1)}, f32[2,9,64,128]{3,2,1,0:T(8,128)S(1)}) custom-call(s32[3]{0:T(128)S(1)} %pad_add_fusion.refs_0_.info, f32[784,128]{1,0:T(8,128)S(1)} %collective-permute-done.4.refs_1_, f32[2,4,784,128]{3,2,1,0:T(8,128)S(1)} %bitcast.13, ...), custom_call_target="tpu_custom_call" | custom-call | flops 1000000000 | bytes 1 | tf_op jit(solution)/shard_map/tick_2_turn_2/pallas_call | solution.py:266
  52.6 0.2 collective-permute-start.10
  52.8 3.3 %collective-permute-done.3.refs_1_ = f32[784,128]{1,0:T(8,128)S(1)} collective-permute-done((f32[784,128]{1,0:T(8,128)S(1)}, f32[784,128]{1,0:T(8,128)S(1)}, u32[]{:S(2)}, u32[]{:S(2)}) %collective-permute-start.3) | collective-permute-done | bytes 401440 | tf_op jit(solution)/shard_map/ppermute | solution.py:357
  56.0 3.2 %tick_1_turn_1.1 = (f32[784,128]{1,0:T(8,128)S(1)}, f32[2,9,128,128]{3,2,1,0:T(8,128)S(1)}) custom-call(s32[3]{0:T(128)S(1)} %pad_add_fusion.refs_0_.info, f32[784,128]{1,0:T(8,128)S(1)} %collective-permute-done.3.refs_1_, f32[2,4,784,128]{3,2,1,0:T(8,128)S(1)} %bitcast.14, bf16[4,3,384,256]{3,2,1,0:T(8,128)(2,1)S(1)} %get-tuple-element.56.refs_3_, ...), custom_call_target="tpu_custom_call" | custom-call | flops 99999997952 | bytes 1 | tf_op jit(solution)/shard_map/tick_1_turn_1/pallas_call | solution.py:266
  59.3 3.9 %collective-permute-start.9 = (f32[784,128]{1,0:T(8,128)S(1)}, f32[784,128]{1,0:T(8,128)S(1)}, u32[]{:S(2)}, u32[]{:S(2)}) collective-permute-start(f32[784,128]{1,0:T(8,128)S(1)} %get-tuple-element.65.refs_5_), channel_id=1, source_target_pairs={{8,0},{16,8},{24,16},{9,1},{17,9},{25,17},{10,2},{18,10},{26,18},{... | collective-permute-start | bytes 1204232 | tf_op jit(solution)/shard_map/ppermute | solution.py:357
  63.2 1.9 %collective-permute-done.11.refs_2_ = f32[2,9,64,128]{3,2,1,0:T(8,128)S(1)} collective-permute-done((f32[2,9,64,128]{3,2,1,0:T(8,128)S(1)}, f32[2,9,64,128]{3,2,1,0:T(8,128)S(1)}, u32[]{:S(2)}, u32[]{:S(2)}) %collective-permute-start.11) | collective-permute-done | bytes 589856 | tf_op jit(solution)/shard_map/ppermute | solution.py:336
  65.1 0.1 add_turn_2.1.refs_5_
  65.2 0.3 collective-permute-start.15
  65.5 0.0 collective-permute-done.2.refs_1_
  65.5 3.7 %tick_1_turn_0.1 = (f32[784,128]{1,0:T(8,128)S(1)}, f32[2,9,128,128]{3,2,1,0:T(8,128)S(1)}) custom-call(s32[3]{0:T(128)S(1)} %pad_add_fusion.refs_0_.info, f32[784,128]{1,0:T(8,128)} %collective-permute-done.2.refs_1_, f32[2,4,784,128]{3,2,1,0:T(8,128)S(1)} %bitcast.15, bf16[4,3,384,256]{3,2,1,0:T(8,128)(2,1)S(1)} %get-tuple-element.54.refs_3_, ...), custom_call_target="tpu_custom_call" | custom-call | flops 1 | bytes 1 | tf_op jit(solution)/shard_map/tick_1_turn_0/pallas_call | solution.py:266
  69.2 2.4 %collective-permute-done.9.refs_1_ = f32[784,128]{1,0:T(8,128)S(1)} collective-permute-done((f32[784,128]{1,0:T(8,128)S(1)}, f32[784,128]{1,0:T(8,128)S(1)}, u32[]{:S(2)}, u32[]{:S(2)}) %collective-permute-start.9) | collective-permute-done | bytes 401440 | tf_op jit(solution)/shard_map/ppermute | solution.py:357
  71.6 3.4 %tick_2_turn_1.1 = (f32[784,128]{1,0:T(8,128)S(1)}, f32[2,9,64,128]{3,2,1,0:T(8,128)S(1)}, f32[9,64,128]{2,1,0:T(8,128)S(1)}, f32[9,64,128]{2,1,0:T(8,128)S(1)}) custom-call(s32[3]{0:T(128)S(1)} %pad_add_fusion.refs_0_.info, f32[784,128]{1,0:T(8,128)S(1)} %collective-permute-done.9.refs_1_, f32[2,4,784,128]{3,2,1,0:T(8,128)S(1)} %bitcast.16, ...), custom_call_target="tpu_custom_call" | custom-call | flops 1 | bytes 1 | tf_op jit(solution)/shard_map/tick_2_turn_1/pallas_call | solution.py:266
  75.0 0.1 collective-permute-start.12
  75.1 0.5 collective-permute-start.13
  75.6 3.3 %collective-permute-start.8 = (f32[784,128]{1,0:T(8,128)S(1)}, f32[784,128]{1,0:T(8,128)S(1)}, u32[]{:S(2)}, u32[]{:S(2)}) collective-permute-start(f32[784,128]{1,0:T(8,128)S(1)} %get-tuple-element.66.refs_6_), channel_id=1, source_target_pairs={{8,0},{16,8},{24,16},{9,1},{17,9},{25,17},{10,2},{18,10},{26,18},{... | collective-permute-start | bytes 1204232 | tf_op jit(solution)/shard_map/ppermute | solution.py:357
  79.0 0.1 add_turn_1.1.refs_8_
  79.1 1.6 %collective-permute-start.14 = (f32[2,9,64,128]{3,2,1,0:T(8,128)S(1)}, f32[2,9,64,128]{3,2,1,0:T(8,128)S(1)}, u32[]{:S(2)}, u32[]{:S(2)}) collective-permute-start(f32[2,9,64,128]{3,2,1,0:T(8,128)S(1)} %add_turn_1.1.refs_8_), channel_id=1, source_target_pairs={{0,2},{1,3},{2,0},{3,1},{4,6},{5,7},{6,4},{7,5},{8,10},{9,11},{10,... | collective-permute-start | bytes 1769480 | tf_op jit(solution)/shard_map/ppermute | solution.py:336
  80.7 0.1 add_relay.1
  80.8 1.9 %collective-permute-start.16 = (f32[2,9,64,128]{3,2,1,0:T(8,128)S(1)}, f32[2,9,64,128]{3,2,1,0:T(8,128)S(1)}, u32[]{:S(2)}, u32[]{:S(2)}) collective-permute-start(f32[2,9,64,128]{3,2,1,0:T(8,128)S(1)} %add_relay.1), channel_id=1, source_target_pairs={{2,4},{3,5},{4,2},{5,3},{10,12},{11,13},{12,10},{13,11},{18,20},{1... | collective-permute-start | bytes 1769480 | tf_op jit(solution)/shard_map/ppermute | solution.py:336
  82.7 6.1 %collective-permute-done.8.refs_1_ = f32[784,128]{1,0:T(8,128)S(1)} collective-permute-done((f32[784,128]{1,0:T(8,128)S(1)}, f32[784,128]{1,0:T(8,128)S(1)}, u32[]{:S(2)}, u32[]{:S(2)}) %collective-permute-start.8) | collective-permute-done | bytes 401440 | tf_op jit(solution)/shard_map/ppermute | solution.py:357
  88.8 3.7 %tick_2_turn_0.1 = (f32[4,784,128]{2,1,0:T(8,128)}, f32[2,9,64,128]{3,2,1,0:T(8,128)S(1)}, f32[9,64,128]{2,1,0:T(8,128)S(1)}, f32[9,64,128]{2,1,0:T(8,128)S(1)}) custom-call(s32[3]{0:T(128)S(1)} %pad_add_fusion.refs_0_.info, f32[784,128]{1,0:T(8,128)S(1)} %collective-permute-done.8.refs_1_, f32[2,4,784,128]{3,2,1,0:T(8,128)S(1)} %bitcast.17, ...), custom_call_target="tpu_custom_call" | custom-call | flops 1 | bytes 1 | tf_op jit(solution)/shard_map/tick_2_turn_0/pallas_call | solution.py:266
  92.5 0.1 collective-permute-start.17
  92.6 0.5 collective-permute-start.18
  93.1 1.1 %collective-permute-done.14.beside = f32[2,9,64,128]{3,2,1,0:T(8,128)S(1)} collective-permute-done((f32[2,9,64,128]{3,2,1,0:T(8,128)S(1)}, f32[2,9,64,128]{3,2,1,0:T(8,128)S(1)}, u32[]{:S(2)}, u32[]{:S(2)}) %collective-permute-start.14) | collective-permute-done | bytes 589856 | tf_op jit(solution)/shard_map/ppermute | solution.py:336
  94.2 3.3 %collective-permute-done.16.relayed = f32[2,9,64,128]{3,2,1,0:T(8,128)S(1)} collective-permute-done((f32[2,9,64,128]{3,2,1,0:T(8,128)S(1)}, f32[2,9,64,128]{3,2,1,0:T(8,128)S(1)}, u32[]{:S(2)}, u32[]{:S(2)}) %collective-permute-start.16) | collective-permute-done | bytes 589856 | tf_op jit(solution)/shard_map/ppermute | solution.py:336
  97.4 0.7 add_arrived.1.refs_0_
  98.2 0.9 add_last.1
  (15 shorter events, 0.0 us)
Async XLA Ops:
  6.0 12.9 %collective-permute-start.1 = (f32[784,128]{1,0:T(8,128)S(1)}, f32[784,128]{1,0:T(8,128)S(1)}, u32[]{:S(2)}, u32[]{:S(2)}) collective-permute-start(f32[784,128]{1,0:T(8,128)S(1)} %get-tuple-element.44.refs_3_), channel_id=1, source_target_pairs={{8,0},{16,8},{24,16},{9,1},{17,9},{25,17},{10,2},{18,10},{26,18},{... | collective-permute-start | bytes 1204232 | tf_op jit(solution)/shard_map/ppermute | solution.py:357
  12.6 6.3 %copy-start = (f32[2,4,1,196,512]{4,2,3,1,0:T(1,128)S(1)}, f32[2,4,1,196,512]{4,2,3,1,0:T(1,128)}, u32[]{:S(2)}) copy-start(f32[2,4,1,196,512]{4,2,3,1,0:T(1,128)} %param.5) | copy-start | bytes 9633796
  16.0 14.1 %collective-permute-start = (f32[784,128]{1,0:T(8,128)S(1)}, f32[784,128]{1,0:T(8,128)S(1)}, u32[]{:S(2)}, u32[]{:S(2)}) collective-permute-start(f32[784,128]{1,0:T(8,128)S(1)} %get-tuple-element.46.refs_5_), channel_id=1, source_target_pairs={{8,0},{16,8},{24,16},{9,1},{17,9},{25,17},{10,2},{18,10},{26,18},{... | collective-permute-start | bytes 1204232 | tf_op jit(solution)/shard_map/ppermute | solution.py:357
  22.1 19.7 %collective-permute-start.5 = (f32[784,128]{1,0:T(8,128)S(1)}, f32[784,128]{1,0:T(8,128)S(1)}, u32[]{:S(2)}, u32[]{:S(2)}) collective-permute-start(f32[784,128]{1,0:T(8,128)S(1)} %get-tuple-element.51.refs_5_), channel_id=1, source_target_pairs={{8,0},{16,8},{24,16},{9,1},{17,9},{25,17},{10,2},{18,10},{26,18},{... | collective-permute-start | bytes 1204232 | tf_op jit(solution)/shard_map/ppermute | solution.py:357
  33.3 15.9 %collective-permute-start.4 = (f32[784,128]{1,0:T(8,128)S(1)}, f32[784,128]{1,0:T(8,128)S(1)}, u32[]{:S(2)}, u32[]{:S(2)}) collective-permute-start(f32[784,128]{1,0:T(8,128)S(1)} %get-tuple-element.52.refs_3_), channel_id=1, source_target_pairs={{8,0},{16,8},{24,16},{9,1},{17,9},{25,17},{10,2},{18,10},{26,18},{... | collective-permute-start | bytes 1204232 | tf_op jit(solution)/shard_map/ppermute | solution.py:357
  36.4 19.7 %collective-permute-start.3 = (f32[784,128]{1,0:T(8,128)S(1)}, f32[784,128]{1,0:T(8,128)S(1)}, u32[]{:S(2)}, u32[]{:S(2)}) collective-permute-start(f32[784,128]{1,0:T(8,128)S(1)} %get-tuple-element.45.refs_3_), channel_id=1, source_target_pairs={{8,0},{16,8},{24,16},{9,1},{17,9},{25,17},{10,2},{18,10},{26,18},{... | collective-permute-start | bytes 1204232 | tf_op jit(solution)/shard_map/ppermute | solution.py:357
  45.3 7.3 %copy-start.1 = (f32[784,128]{1,0:T(8,128)}, f32[784,128]{1,0:T(8,128)S(1)}, u32[]{:S(2)}) copy-start(f32[784,128]{1,0:T(8,128)S(1)} %get-tuple-element.63.refs_6_.refs_5_) | copy-start | bytes 1204228
  45.3 2.5 %collective-permute-start.6 = (f32[9,64,128]{2,1,0:T(8,128)S(1)}, f32[9,64,128]{2,1,0:T(8,128)S(1)}, u32[]{:S(2)}, u32[]{:S(2)}) collective-permute-start(f32[9,64,128]{2,1,0:T(8,128)S(1)} %get-tuple-element.61), channel_id=1, source_target_pairs={{0,1},{1,0},{2,3},{3,2},{4,5},{5,4},{6,7},{7,6},{8,9},{9,8},{10,11... | collective-permute-start | bytes 884744 | tf_op jit(solution)/shard_map/ppermute | solution.py:333
  45.4 2.4 %collective-permute-start.7 = (f32[9,64,128]{2,1,0:T(8,128)S(1)}, f32[9,64,128]{2,1,0:T(8,128)S(1)}, u32[]{:S(2)}, u32[]{:S(2)}) collective-permute-start(f32[9,64,128]{2,1,0:T(8,128)S(1)} %get-tuple-element.62), channel_id=1, source_target_pairs={{0,1},{1,0},{2,3},{3,2},{4,5},{5,4},{6,7},{7,6},{8,9},{9,8},{10,11... | collective-permute-start | bytes 884744 | tf_op jit(solution)/shard_map/ppermute | solution.py:333
  45.9 19.6 %collective-permute-start.2 = (f32[784,128]{1,0:T(8,128)}, f32[784,128]{1,0:T(8,128)}, u32[]{:S(2)}, u32[]{:S(2)}) collective-permute-start(f32[784,128]{1,0:T(8,128)} %get-tuple-element.53.refs_5_), channel_id=1, source_target_pairs={{8,0},{16,8},{24,16},{9,1},{17,9},{25,17},{10,2},{18,10},{26,18},{... | collective-permute-start | bytes 1204232 | tf_op jit(solution)/shard_map/ppermute | solution.py:357
  47.9 17.2 %collective-permute-start.11 = (f32[2,9,64,128]{3,2,1,0:T(8,128)S(1)}, f32[2,9,64,128]{3,2,1,0:T(8,128)S(1)}, u32[]{:S(2)}, u32[]{:S(2)}) collective-permute-start(f32[2,9,64,128]{3,2,1,0:T(8,128)S(1)} %add_turn_3.1.refs_5_.refs_0_), channel_id=1, source_target_pairs={{0,2},{1,3},{6,4},{7,5},{8,10},{9,11},{14,12},{15,13},{16,18},{17,... | collective-permute-start | bytes 1769480 | tf_op jit(solution)/shard_map/ppermute | solution.py:336
  52.6 10.6 %collective-permute-start.10 = (f32[2,9,64,128]{3,2,1,0:T(8,128)S(1)}, f32[2,9,64,128]{3,2,1,0:T(8,128)S(1)}, u32[]{:S(2)}, u32[]{:S(2)}) collective-permute-start(f32[2,9,64,128]{3,2,1,0:T(8,128)S(1)} %get-tuple-element.70), channel_id=1, source_target_pairs={{0,1},{1,0},{2,3},{3,2},{4,5},{5,4},{6,7},{7,6},{8,9},{9,8},{10,11... | collective-permute-start | bytes 1769480 | tf_op jit(solution)/shard_map/ppermute | solution.py:333
  59.3 12.4 %collective-permute-start.9 = (f32[784,128]{1,0:T(8,128)S(1)}, f32[784,128]{1,0:T(8,128)S(1)}, u32[]{:S(2)}, u32[]{:S(2)}) collective-permute-start(f32[784,128]{1,0:T(8,128)S(1)} %get-tuple-element.65.refs_5_), channel_id=1, source_target_pairs={{8,0},{16,8},{24,16},{9,1},{17,9},{25,17},{10,2},{18,10},{26,18},{... | collective-permute-start | bytes 1204232 | tf_op jit(solution)/shard_map/ppermute | solution.py:357
  65.2 15.5 %collective-permute-start.15 = (f32[2,9,64,128]{3,2,1,0:T(8,128)S(1)}, f32[2,9,64,128]{3,2,1,0:T(8,128)S(1)}, u32[]{:S(2)}, u32[]{:S(2)}) collective-permute-start(f32[2,9,64,128]{3,2,1,0:T(8,128)S(1)} %add_turn_2.1.refs_5_), channel_id=1, source_target_pairs={{0,2},{1,3},{6,4},{7,5},{2,6},{3,7},{4,0},{5,1},{8,10},{9,11},{14,... | collective-permute-start | bytes 1769480 | tf_op jit(solution)/shard_map/ppermute | solution.py:336
  75.0 3.9 %collective-permute-start.12 = (f32[9,64,128]{2,1,0:T(8,128)S(1)}, f32[9,64,128]{2,1,0:T(8,128)S(1)}, u32[]{:S(2)}, u32[]{:S(2)}) collective-permute-start(f32[9,64,128]{2,1,0:T(8,128)S(1)} %get-tuple-element.73), channel_id=1, source_target_pairs={{0,1},{1,0},{2,3},{3,2},{4,5},{5,4},{6,7},{7,6},{8,9},{9,8},{10,11... | collective-permute-start | bytes 884744 | tf_op jit(solution)/shard_map/ppermute | solution.py:333
  75.1 3.8 %collective-permute-start.13 = (f32[9,64,128]{2,1,0:T(8,128)S(1)}, f32[9,64,128]{2,1,0:T(8,128)S(1)}, u32[]{:S(2)}, u32[]{:S(2)}) collective-permute-start(f32[9,64,128]{2,1,0:T(8,128)S(1)} %get-tuple-element.74), channel_id=1, source_target_pairs={{0,1},{1,0},{2,3},{3,2},{4,5},{5,4},{6,7},{7,6},{8,9},{9,8},{10,11... | collective-permute-start | bytes 884744 | tf_op jit(solution)/shard_map/ppermute | solution.py:333
  75.6 13.2 %collective-permute-start.8 = (f32[784,128]{1,0:T(8,128)S(1)}, f32[784,128]{1,0:T(8,128)S(1)}, u32[]{:S(2)}, u32[]{:S(2)}) collective-permute-start(f32[784,128]{1,0:T(8,128)S(1)} %get-tuple-element.66.refs_6_), channel_id=1, source_target_pairs={{8,0},{16,8},{24,16},{9,1},{17,9},{25,17},{10,2},{18,10},{26,18},{... | collective-permute-start | bytes 1204232 | tf_op jit(solution)/shard_map/ppermute | solution.py:357
  79.1 9.7 %copy-start.2 = (f32[784,128]{1,0:T(8,128)S(1)}, f32[784,128]{1,0:T(8,128)}, u32[]{:S(2)}) copy-start(f32[784,128]{1,0:T(8,128)} %copy-done.1) | copy-start | bytes 1204228
  79.1 15.1 %collective-permute-start.14 = (f32[2,9,64,128]{3,2,1,0:T(8,128)S(1)}, f32[2,9,64,128]{3,2,1,0:T(8,128)S(1)}, u32[]{:S(2)}, u32[]{:S(2)}) collective-permute-start(f32[2,9,64,128]{3,2,1,0:T(8,128)S(1)} %add_turn_1.1.refs_8_), channel_id=1, source_target_pairs={{0,2},{1,3},{2,0},{3,1},{4,6},{5,7},{6,4},{7,5},{8,10},{9,11},{10,... | collective-permute-start | bytes 1769480 | tf_op jit(solution)/shard_map/ppermute | solution.py:336
  80.8 16.6 %collective-permute-start.16 = (f32[2,9,64,128]{3,2,1,0:T(8,128)S(1)}, f32[2,9,64,128]{3,2,1,0:T(8,128)S(1)}, u32[]{:S(2)}, u32[]{:S(2)}) collective-permute-start(f32[2,9,64,128]{3,2,1,0:T(8,128)S(1)} %add_relay.1), channel_id=1, source_target_pairs={{2,4},{3,5},{4,2},{5,3},{10,12},{11,13},{12,10},{13,11},{18,20},{1... | collective-permute-start | bytes 1769480 | tf_op jit(solution)/shard_map/ppermute | solution.py:336
  92.5 5.7 %collective-permute-start.17 = (f32[9,64,128]{2,1,0:T(8,128)S(1)}, f32[9,64,128]{2,1,0:T(8,128)S(1)}, u32[]{:S(2)}, u32[]{:S(2)}) collective-permute-start(f32[9,64,128]{2,1,0:T(8,128)S(1)} %get-tuple-element.77), channel_id=1, source_target_pairs={{0,1},{1,0},{2,3},{3,2},{4,5},{5,4},{6,7},{7,6},{8,9},{9,8},{10,11... | collective-permute-start | bytes 884744 | tf_op jit(solution)/shard_map/ppermute | solution.py:333
  92.6 5.6 %collective-permute-start.18 = (f32[9,64,128]{2,1,0:T(8,128)S(1)}, f32[9,64,128]{2,1,0:T(8,128)S(1)}, u32[]{:S(2)}, u32[]{:S(2)}) collective-permute-start(f32[9,64,128]{2,1,0:T(8,128)S(1)} %get-tuple-element.78), channel_id=1, source_target_pairs={{0,1},{1,0},{2,3},{3,2},{4,5},{5,4},{6,7},{7,6},{8,9},{9,8},{10,11... | collective-permute-start | bytes 884744 | tf_op jit(solution)/shard_map/ppermute | solution.py:333

commit v4 on v3

--- a/solution.py
+++ b/solution.py
@@ -88,8 +88,8 @@
         copies += [pltpu.make_async_copy(f, kept.at[k], sems.at[2 + k]) for k, f in enumerate(filters)]
         from_state = pltpu.make_async_copy(state, kept_state, sems.at[4])
         from_state.start()
-        for copy in copies:
-            copy.start()
+        copies[1].start()
+        copies[0].start()
     if not first:
         at_end = info[1] == 1
     for taps in (taps_one, taps_two, taps_error):
@@ -162,6 +162,9 @@
     if first:
         if lead:
             copies[1].wait()
+            copies[0].wait()
+            copies[2].start()
+            copies[3].start()
         pack(1)
     act, slope_two = branch(conv(taps_one, packed.at[1], rows, pitch))
     x_two = jnp.where(inside, plane[1] - act, 0.0)
@@ -170,8 +173,6 @@
     change_two = jnp.where(inside, plane[3] * slope_two, 0.0)
     spread(taps_error, change_two, pitch, shifted)
     if first:
-        if lead:
-            copies[0].wait()
         pack(0)
     raw_one = conv(taps_two, packed.at[0], rows, pitch)
     raw_error = conv(taps_error, packed.at[3], rows, pitch)
@@ -287,10 +288,11 @@
             outs[0][k] = total
 
 
-def arrived_kernel(info, mine, beside, relayed, far, out):
+def last_kernel(info, mine, beside, relayed, far, *refs):
     outer = jnp.logical_or(info[0] == 0, info[0] == 3)
-    for k in range(2):
-        out[k] = mine[k] + beside[k] + relayed[k] + jnp.where(outer, far[k], 0.0)
+    for k, out in enumerate(refs[-2:]):
+        total = mine[k] + beside[k] + relayed[k] + jnp.where(outer, far[k], 0.0)
+        out[...] = functools.reduce(lambda x, y: x + y, [ref[...] for ref in refs[k:-2:2]], total)
 
 
 def add(stacked, terms, parts, after, effort, out, name):
@@ -387,17 +389,16 @@
             totals[2] = between(own_total, [(0, 1), (1, 0), (2, 3), (3, 2)])
 
     in_vmem = pl.BlockSpec(memory_space=VMEM)
-    kept = pl.pallas_call(
-        arrived_kernel,
-        out_shape=VMEM(part, F32),
-        in_specs=[pl.BlockSpec(memory_space=pltpu.SMEM)] + [in_vmem] * 4,
-        out_specs=in_vmem,
+    terms = [mine, totals[2], totals[3], totals[1], *swapped]
+    first_grad, second_grad = pl.pallas_call(
+        last_kernel,
+        out_shape=[jax.ShapeDtypeStruct(part[1:], F32)] * 2,
+        in_specs=[pl.BlockSpec(memory_space=pltpu.SMEM)] + [in_vmem] * len(terms),
+        out_specs=[in_vmem] * 2,
         compiler_params=pltpu.CompilerParams(vmem_limit_bytes=VMEM_LIMIT),
-        cost_estimate=pl.CostEstimate(flops=PLAN["sum"], bytes_accessed=1, transcendentals=0),
-        name="add_arrived",
-    )(info, mine, totals[2], totals[3], totals[1])
-    out = [jax.ShapeDtypeStruct(part[1:], F32)] * 2
-    first_grad, second_grad = add(False, [kept], swapped, [], PLAN["last"], out, "add_last")
+        cost_estimate=pl.CostEstimate(flops=PLAN["last"], bytes_accessed=1, transcendentals=0),
+        name="add_last",
+    )(info, *terms)
     returned = outs[groups - 1].reshape(1, 4, 1, pixels, channels)
     return (returned, first_grad[None, None], second_grad[None, None])
 

time: 99.4 us -> 99.1 us (level)
    ppermute x4, waiting for transfers between devices: 6.25 us -> 4.76 us  [between(): lax.ppermute(total, 'rep', [(a * shares + n, b * shares + n) for a, b in...]
    ppermute x7, waiting for transfers between devices: 0.02 us -> 1.51 us  [swap(): lax.ppermute(part, 'rep', [(r, r - r % shares + (r % shares + d) % shares...]
  transfers between devices with their start and end apart: 19 -> 19, of which waited for: 8 -> 9; matrix products, arithmetic and copies ran while one was open for 0% -> 0% of each run, Pallas kernels for 39% -> 38%
where the time goes in v4:
time: 99.1 us; the launch traced here: 98.7 us
  Pallas kernels  44.3 us (45%)
  starting transfers between devices  31.3 us (32%)
  waiting for transfers between devices  22 us (22%)
    pallas_call x12, Pallas kernels, step(): pl.pallas_call(functools.partial(step_kernel, dims, k_turn, tick, last, l...  42.5 us
    ppermute x8, starting transfers between devices, on_device(): moved[p] = lax.ppermute(out, 'section', down)  24.3 us
    ppermute x8, waiting for transfers between devices, on_device(): moved[p] = lax.ppermute(out, 'section', down)  15.7 us
    ppermute x4, starting transfers between devices, between(): lax.ppermute(total, 'rep', [(a * shares + n, b * shares + n) for a, b in...  5.14 us
    ppermute x4, waiting for transfers between devices, between(): lax.ppermute(total, 'rep', [(a * shares + n, b * shares + n) for a, b in...  4.76 us
  transfers between devices with their start and end apart: 19, of which 9 were waited for; matrix products, arithmetic and copies ran while one was open for 0% of the time, Pallas kernels for 38%

profile of v4, /device:TPU:20, one launch (start us, length us, event | category | flops | bytes accessed | tf_op | source)
XLA Modules:
  0.0 98.7 jit_solution(16017143454203785265)
XLA Ops:
  0.7 0.1 pad_add_fusion.refs_0_.info
  0.7 5.0 %tick_0_turn_3.1 = (f32[784,128]{1,0:T(8,128)S(1)}, bf16[4,3,384,256]{3,2,1,0:T(8,128)(2,1)S(1)}, f32[2,9,512,128]{3,2,1,0:T(8,128)S(1)}, f32[4,784,128]{2,1,0:T(8,128)S(1)}, f32[2,9,128,128]{3,2,1,0:T(8,128)S(1)}) custom-call(s32[3]{0:T(128)S(1)} %pad_add_fusion.refs_0_.info, f32[4,784,128]{2,1,0:T(8,128)} %bitcast.20, f32[9,512,128]{2,1,0:T(8,128)} %bitcast.18, ...), custom_call_target="tpu_custom_call" | custom-call | flops 10000000000 | bytes 1 | tf_op jit(solution)/shard_map/tick_0_turn_3/pallas_call | solution.py:267
  5.7 3.3 %collective-permute-start.1 = (f32[784,128]{1,0:T(8,128)S(1)}, f32[784,128]{1,0:T(8,128)S(1)}, u32[]{:S(2)}, u32[]{:S(2)}) collective-permute-start(f32[784,128]{1,0:T(8,128)S(1)} %get-tuple-element.44.refs_3_), channel_id=1, source_target_pairs={{8,0},{16,8},{24,16},{9,1},{17,9},{25,17},{10,2},{18,10},{26,18},{... | collective-permute-start | bytes 1204232 | tf_op jit(solution)/shard_map/ppermute | solution.py:359
  9.1 3.3 %tick_0_turn_1.1 = (f32[784,128]{1,0:T(8,128)S(1)}, bf16[4,3,384,256]{3,2,1,0:T(8,128)(2,1)S(1)}, f32[2,9,128,128]{3,2,1,0:T(8,128)S(1)}) custom-call(s32[3]{0:T(128)S(1)} %pad_add_fusion.refs_0_.info, f32[4,784,128]{2,1,0:T(8,128)S(1)} %get-tuple-element.42.refs_1_, f32[2,9,512,128]{3,2,1,0:T(8,128)S(1)} %get-tuple-element.43.refs_2_, ...), custom_call_target="tpu_custom_call" | custom-call | flops 1000000000 | bytes 1 | tf_op jit(solution)/shard_map/tick_0_turn_1/pallas_call | solution.py:267
  12.4 0.0 copy-start
  12.4 3.3 %tick_0_turn_2.1 = (f32[784,128]{1,0:T(8,128)S(1)}, bf16[4,3,384,256]{3,2,1,0:T(8,128)(2,1)S(1)}, f32[2,9,128,128]{3,2,1,0:T(8,128)S(1)}) custom-call(s32[3]{0:T(128)S(1)} %pad_add_fusion.refs_0_.info, f32[4,784,128]{2,1,0:T(8,128)S(1)} %get-tuple-element.42.refs_1_, f32[2,9,512,128]{3,2,1,0:T(8,128)S(1)} %get-tuple-element.43.refs_2_, ...), custom_call_target="tpu_custom_call" | custom-call | flops 1 | bytes 1 | tf_op jit(solution)/shard_map/tick_0_turn_2/pallas_call | solution.py:267
  15.7 2.4 %collective-permute-start = (f32[784,128]{1,0:T(8,128)S(1)}, f32[784,128]{1,0:T(8,128)S(1)}, u32[]{:S(2)}, u32[]{:S(2)}) collective-permute-start(f32[784,128]{1,0:T(8,128)S(1)} %get-tuple-element.46.refs_5_), channel_id=1, source_target_pairs={{8,0},{16,8},{24,16},{9,1},{17,9},{25,17},{10,2},{18,10},{26,18},{... | collective-permute-start | bytes 1204232 | tf_op jit(solution)/shard_map/ppermute | solution.py:359
  18.2 0.5 collective-permute-done.1.refs_1_
  18.7 3.2 %tick_1_turn_3.1 = (f32[784,128]{1,0:T(8,128)S(1)}, f32[2,9,128,128]{3,2,1,0:T(8,128)S(1)}) custom-call(s32[3]{0:T(128)S(1)} %pad_add_fusion.refs_0_.info, f32[784,128]{1,0:T(8,128)S(1)} %collective-permute-done.1.refs_1_, f32[2,4,784,128]{3,2,1,0:T(8,128)S(1)} %bitcast.10, bf16[4,3,384,256]{3,2,1,0:T(8,128)(2,1)S(1)} %get-tuple-element.49.refs_3_, ...), custom_call_target="tpu_custom_call" | custom-call | flops 1 | bytes 1 | tf_op jit(solution)/shard_map/tick_1_turn_3/pallas_call | solution.py:267
  21.9 4.4 %collective-permute-start.5 = (f32[784,128]{1,0:T(8,128)S(1)}, f32[784,128]{1,0:T(8,128)S(1)}, u32[]{:S(2)}, u32[]{:S(2)}) collective-permute-start(f32[784,128]{1,0:T(8,128)S(1)} %get-tuple-element.51.refs_5_), channel_id=1, source_target_pairs={{8,0},{16,8},{24,16},{9,1},{17,9},{25,17},{10,2},{18,10},{26,18},{... | collective-permute-start | bytes 1204232 | tf_op jit(solution)/shard_map/ppermute | solution.py:359
  26.3 3.5 %collective-permute-done.refs_1_ = f32[784,128]{1,0:T(8,128)S(1)} collective-permute-done((f32[784,128]{1,0:T(8,128)S(1)}, f32[784,128]{1,0:T(8,128)S(1)}, u32[]{:S(2)}, u32[]{:S(2)}) %collective-permute-start) | collective-permute-done | bytes 401440 | tf_op jit(solution)/shard_map/ppermute | solution.py:359
  29.8 3.2 %tick_1_turn_2.1 = (f32[784,128]{1,0:T(8,128)S(1)}, f32[2,9,128,128]{3,2,1,0:T(8,128)S(1)}) custom-call(s32[3]{0:T(128)S(1)} %pad_add_fusion.refs_0_.info, f32[784,128]{1,0:T(8,128)S(1)} %collective-permute-done.refs_1_, f32[2,4,784,128]{3,2,1,0:T(8,128)S(1)} %bitcast.11, bf16[4,3,384,256]{3,2,1,0:T(8,128)(2,1)S(1)} %get-tuple-element.47.refs_3_, ...), custom_call_target="tpu_custom_call" | custom-call | flops 1 | bytes 1 | tf_op jit(solution)/shard_map/tick_1_turn_2/pallas_call | solution.py:267
  33.1 3.0 %collective-permute-start.4 = (f32[784,128]{1,0:T(8,128)S(1)}, f32[784,128]{1,0:T(8,128)S(1)}, u32[]{:S(2)}, u32[]{:S(2)}) collective-permute-start(f32[784,128]{1,0:T(8,128)S(1)} %get-tuple-element.52.refs_3_), channel_id=1, source_target_pairs={{8,0},{16,8},{24,16},{9,1},{17,9},{25,17},{10,2},{18,10},{26,18},{... | collective-permute-start | bytes 1204232 | tf_op jit(solution)/shard_map/ppermute | solution.py:359
  36.1 1.9 %collective-permute-start.3 = (f32[784,128]{1,0:T(8,128)S(1)}, f32[784,128]{1,0:T(8,128)S(1)}, u32[]{:S(2)}, u32[]{:S(2)}) collective-permute-start(f32[784,128]{1,0:T(8,128)S(1)} %get-tuple-element.45.refs_3_), channel_id=1, source_target_pairs={{8,0},{16,8},{24,16},{9,1},{17,9},{25,17},{10,2},{18,10},{26,18},{... | collective-permute-start | bytes 1204232 | tf_op jit(solution)/shard_map/ppermute | solution.py:359
  38.0 3.6 %tick_0_turn_0.1 = (f32[784,128]{1,0:T(8,128)}, bf16[4,3,384,256]{3,2,1,0:T(8,128)(2,1)S(1)}, f32[2,9,128,128]{3,2,1,0:T(8,128)S(1)}) custom-call(s32[3]{0:T(128)S(1)} %pad_add_fusion.refs_0_.info, f32[4,784,128]{2,1,0:T(8,128)S(1)} %get-tuple-element.42.refs_1_, f32[2,9,512,128]{3,2,1,0:T(8,128)S(1)} %get-tuple-element.43.refs_2_, ...), custom_call_target="tpu_custom_call" | custom-call | flops 1000000000 | bytes 1 | tf_op jit(solution)/shard_map/tick_0_turn_0/pallas_call | solution.py:267
  41.6 0.0 collective-permute-done.5.refs_1_
  41.6 3.4 %tick_2_turn_3.1 = (f32[784,128]{1,0:T(8,128)S(1)}, f32[2,9,64,128]{3,2,1,0:T(8,128)S(1)}, f32[9,64,128]{2,1,0:T(8,128)S(1)}, f32[9,64,128]{2,1,0:T(8,128)S(1)}) custom-call(s32[3]{0:T(128)S(1)} %pad_add_fusion.refs_0_.info, f32[784,128]{1,0:T(8,128)S(1)} %collective-permute-done.5.refs_1_, f32[2,4,784,128]{3,2,1,0:T(8,128)S(1)} %bitcast.12, ...), custom_call_target="tpu_custom_call" | custom-call | flops 1 | bytes 1 | tf_op jit(solution)/shard_map/tick_2_turn_3/pallas_call | solution.py:267
  45.1 0.1 collective-permute-start.6
  45.1 0.5 collective-permute-start.7
  45.6 1.9 %collective-permute-start.2 = (f32[784,128]{1,0:T(8,128)}, f32[784,128]{1,0:T(8,128)}, u32[]{:S(2)}, u32[]{:S(2)}) collective-permute-start(f32[784,128]{1,0:T(8,128)} %get-tuple-element.53.refs_5_), channel_id=1, source_target_pairs={{8,0},{16,8},{24,16},{9,1},{17,9},{25,17},{10,2},{18,10},{26,18},{... | collective-permute-start | bytes 1204232 | tf_op jit(solution)/shard_map/ppermute | solution.py:359
  47.6 0.1 add_turn_3.1.refs_5_.refs_0_
  47.7 1.3 %collective-permute-start.11 = (f32[2,9,64,128]{3,2,1,0:T(8,128)S(1)}, f32[2,9,64,128]{3,2,1,0:T(8,128)S(1)}, u32[]{:S(2)}, u32[]{:S(2)}) collective-permute-start(f32[2,9,64,128]{3,2,1,0:T(8,128)S(1)} %add_turn_3.1.refs_5_.refs_0_), channel_id=1, source_target_pairs={{0,2},{1,3},{6,4},{7,5},{8,10},{9,11},{14,12},{15,13},{16,18},{17,... | collective-permute-start | bytes 1769480 | tf_op jit(solution)/shard_map/ppermute | solution.py:338
  49.0 3.4 %tick_2_turn_2.1 = (f32[784,128]{1,0:T(8,128)S(1)}, f32[2,9,64,128]{3,2,1,0:T(8,128)S(1)}, f32[2,9,64,128]{3,2,1,0:T(8,128)S(1)}) custom-call(s32[3]{0:T(128)S(1)} %pad_add_fusion.refs_0_.info, f32[784,128]{1,0:T(8,128)S(1)} %collective-permute-done.4.refs_1_, f32[2,4,784,128]{3,2,1,0:T(8,128)S(1)} %bitcast.13, ...), custom_call_target="tpu_custom_call" | custom-call | flops 1000000000 | bytes 1 | tf_op jit(solution)/shard_map/tick_2_turn_2/pallas_call | solution.py:267
  52.4 0.2 collective-permute-start.10
  52.5 3.2 %collective-permute-done.3.refs_1_ = f32[784,128]{1,0:T(8,128)S(1)} collective-permute-done((f32[784,128]{1,0:T(8,128)S(1)}, f32[784,128]{1,0:T(8,128)S(1)}, u32[]{:S(2)}, u32[]{:S(2)}) %collective-permute-start.3) | collective-permute-done | bytes 401440 | tf_op jit(solution)/shard_map/ppermute | solution.py:359
  55.8 3.2 %tick_1_turn_1.1 = (f32[784,128]{1,0:T(8,128)S(1)}, f32[2,9,128,128]{3,2,1,0:T(8,128)S(1)}) custom-call(s32[3]{0:T(128)S(1)} %pad_add_fusion.refs_0_.info, f32[784,128]{1,0:T(8,128)S(1)} %collective-permute-done.3.refs_1_, f32[2,4,784,128]{3,2,1,0:T(8,128)S(1)} %bitcast.14, bf16[4,3,384,256]{3,2,1,0:T(8,128)(2,1)S(1)} %get-tuple-element.56.refs_3_, ...), custom_call_target="tpu_custom_call" | custom-call | flops 99999997952 | bytes 1 | tf_op jit(solution)/shard_map/tick_1_turn_1/pallas_call | solution.py:267
  59.0 3.9 %collective-permute-start.9 = (f32[784,128]{1,0:T(8,128)S(1)}, f32[784,128]{1,0:T(8,128)S(1)}, u32[]{:S(2)}, u32[]{:S(2)}) collective-permute-start(f32[784,128]{1,0:T(8,128)S(1)} %get-tuple-element.65.refs_5_), channel_id=1, source_target_pairs={{8,0},{16,8},{24,16},{9,1},{17,9},{25,17},{10,2},{18,10},{26,18},{... | collective-permute-start | bytes 1204232 | tf_op jit(solution)/shard_map/ppermute | solution.py:359
  63.0 1.9 %collective-permute-done.11.refs_2_ = f32[2,9,64,128]{3,2,1,0:T(8,128)S(1)} collective-permute-done((f32[2,9,64,128]{3,2,1,0:T(8,128)S(1)}, f32[2,9,64,128]{3,2,1,0:T(8,128)S(1)}, u32[]{:S(2)}, u32[]{:S(2)}) %collective-permute-start.11) | collective-permute-done | bytes 589856 | tf_op jit(solution)/shard_map/ppermute | solution.py:338
  64.9 0.1 add_turn_2.1.refs_5_
  65.0 0.3 collective-permute-start.15
  65.3 3.7 %tick_1_turn_0.1 = (f32[784,128]{1,0:T(8,128)S(1)}, f32[2,9,128,128]{3,2,1,0:T(8,128)S(1)}) custom-call(s32[3]{0:T(128)S(1)} %pad_add_fusion.refs_0_.info, f32[784,128]{1,0:T(8,128)} %collective-permute-done.2.refs_1_, f32[2,4,784,128]{3,2,1,0:T(8,128)S(1)} %bitcast.15, bf16[4,3,384,256]{3,2,1,0:T(8,128)(2,1)S(1)} %get-tuple-element.54.refs_3_, ...), custom_call_target="tpu_custom_call" | custom-call | flops 1 | bytes 1 | tf_op jit(solution)/shard_map/tick_1_turn_0/pallas_call | solution.py:267
  69.0 2.4 %collective-permute-done.9.refs_1_ = f32[784,128]{1,0:T(8,128)S(1)} collective-permute-done((f32[784,128]{1,0:T(8,128)S(1)}, f32[784,128]{1,0:T(8,128)S(1)}, u32[]{:S(2)}, u32[]{:S(2)}) %collective-permute-start.9) | collective-permute-done | bytes 401440 | tf_op jit(solution)/shard_map/ppermute | solution.py:359
  71.4 3.4 %tick_2_turn_1.1 = (f32[784,128]{1,0:T(8,128)S(1)}, f32[2,9,64,128]{3,2,1,0:T(8,128)S(1)}, f32[9,64,128]{2,1,0:T(8,128)S(1)}, f32[9,64,128]{2,1,0:T(8,128)S(1)}) custom-call(s32[3]{0:T(128)S(1)} %pad_add_fusion.refs_0_.info, f32[784,128]{1,0:T(8,128)S(1)} %collective-permute-done.9.refs_1_, f32[2,4,784,128]{3,2,1,0:T(8,128)S(1)} %bitcast.16, ...), custom_call_target="tpu_custom_call" | custom-call | flops 1 | bytes 1 | tf_op jit(solution)/shard_map/tick_2_turn_1/pallas_call | solution.py:267
  74.8 0.1 collective-permute-start.12
  74.9 0.5 collective-permute-start.13
  75.4 3.3 %collective-permute-start.8 = (f32[784,128]{1,0:T(8,128)S(1)}, f32[784,128]{1,0:T(8,128)S(1)}, u32[]{:S(2)}, u32[]{:S(2)}) collective-permute-start(f32[784,128]{1,0:T(8,128)S(1)} %get-tuple-element.66.refs_6_), channel_id=1, source_target_pairs={{8,0},{16,8},{24,16},{9,1},{17,9},{25,17},{10,2},{18,10},{26,18},{... | collective-permute-start | bytes 1204232 | tf_op jit(solution)/shard_map/ppermute | solution.py:359
  78.7 0.1 add_turn_1.1.refs_8_
  78.8 1.6 %collective-permute-start.14 = (f32[2,9,64,128]{3,2,1,0:T(8,128)S(1)}, f32[2,9,64,128]{3,2,1,0:T(8,128)S(1)}, u32[]{:S(2)}, u32[]{:S(2)}) collective-permute-start(f32[2,9,64,128]{3,2,1,0:T(8,128)S(1)} %add_turn_1.1.refs_8_), channel_id=1, source_target_pairs={{0,2},{1,3},{2,0},{3,1},{4,6},{5,7},{6,4},{7,5},{8,10},{9,11},{10,... | collective-permute-start | bytes 1769480 | tf_op jit(solution)/shard_map/ppermute | solution.py:338
  80.5 0.1 add_relay.1
  80.6 1.9 %collective-permute-start.16 = (f32[2,9,64,128]{3,2,1,0:T(8,128)S(1)}, f32[2,9,64,128]{3,2,1,0:T(8,128)S(1)}, u32[]{:S(2)}, u32[]{:S(2)}) collective-permute-start(f32[2,9,64,128]{3,2,1,0:T(8,128)S(1)} %add_relay.1), channel_id=1, source_target_pairs={{2,4},{3,5},{4,2},{5,3},{10,12},{11,13},{12,10},{13,11},{18,20},{1... | collective-permute-start | bytes 1769480 | tf_op jit(solution)/shard_map/ppermute | solution.py:338
  82.5 6.1 %collective-permute-done.8.refs_1_ = f32[784,128]{1,0:T(8,128)S(1)} collective-permute-done((f32[784,128]{1,0:T(8,128)S(1)}, f32[784,128]{1,0:T(8,128)S(1)}, u32[]{:S(2)}, u32[]{:S(2)}) %collective-permute-start.8) | collective-permute-done | bytes 401440 | tf_op jit(solution)/shard_map/ppermute | solution.py:359
  88.5 3.7 %tick_2_turn_0.1 = (f32[4,784,128]{2,1,0:T(8,128)}, f32[2,9,64,128]{3,2,1,0:T(8,128)S(1)}, f32[9,64,128]{2,1,0:T(8,128)S(1)}, f32[9,64,128]{2,1,0:T(8,128)S(1)}) custom-call(s32[3]{0:T(128)S(1)} %pad_add_fusion.refs_0_.info, f32[784,128]{1,0:T(8,128)S(1)} %collective-permute-done.8.refs_1_, f32[2,4,784,128]{3,2,1,0:T(8,128)S(1)} %bitcast.17, ...), custom_call_target="tpu_custom_call" | custom-call | flops 1 | bytes 1 | tf_op jit(solution)/shard_map/tick_2_turn_0/pallas_call | solution.py:267
  92.2 0.1 collective-permute-start.17
  92.3 0.5 collective-permute-start.18
  92.8 1.1 %collective-permute-done.17.refs_0_ = f32[9,64,128]{2,1,0:T(8,128)S(1)} collective-permute-done((f32[9,64,128]{2,1,0:T(8,128)S(1)}, f32[9,64,128]{2,1,0:T(8,128)S(1)}, u32[]{:S(2)}, u32[]{:S(2)}) %collective-permute-start.17) | collective-permute-done | bytes 294944 | tf_op jit(solution)/shard_map/ppermute | solution.py:335
  93.9 0.4 collective-permute-done.18.refs_1_
  94.3 2.9 %collective-permute-done.16.relayed = f32[2,9,64,128]{3,2,1,0:T(8,128)S(1)} collective-permute-done((f32[2,9,64,128]{3,2,1,0:T(8,128)S(1)}, f32[2,9,64,128]{3,2,1,0:T(8,128)S(1)}, u32[]{:S(2)}, u32[]{:S(2)}) %collective-permute-start.16) | collective-permute-done | bytes 589856 | tf_op jit(solution)/shard_map/ppermute | solution.py:338
  97.2 1.5 %add_last.1 = (f32[9,64,128]{2,1,0:T(8,128)}, f32[9,64,128]{2,1,0:T(8,128)}) custom-call(s32[3]{0:T(128)S(1)} %pad_add_fusion.refs_0_.info, f32[2,9,64,128]{3,2,1,0:T(8,128)S(1)} %get-tuple-element.76.mine, f32[2,9,64,128]{3,2,1,0:T(8,128)S(1)} %collective-permute-done.14.beside, f32[2,9,64,128]{3,2,1,0:T(8,128)S(1)} %collective-permute-done.16.relayed, ...), custom_call_target="tpu_custom_call" | custom-call | flops 1 | bytes 1 | tf_op jit(solution)/shard_map/add_last/pallas_call | solution.py:393
  (14 shorter events, 0.0 us)
Async XLA Ops:
  5.7 12.9 %collective-permute-start.1 = (f32[784,128]{1,0:T(8,128)S(1)}, f32[784,128]{1,0:T(8,128)S(1)}, u32[]{:S(2)}, u32[]{:S(2)}) collective-permute-start(f32[784,128]{1,0:T(8,128)S(1)} %get-tuple-element.44.refs_3_), channel_id=1, source_target_pairs={{8,0},{16,8},{24,16},{9,1},{17,9},{25,17},{10,2},{18,10},{26,18},{... | collective-permute-start | bytes 1204232 | tf_op jit(solution)/shard_map/ppermute | solution.py:359
  12.4 6.3 %copy-start = (f32[2,4,1,196,512]{4,2,3,1,0:T(1,128)S(1)}, f32[2,4,1,196,512]{4,2,3,1,0:T(1,128)}, u32[]{:S(2)}) copy-start(f32[2,4,1,196,512]{4,2,3,1,0:T(1,128)} %param.5) | copy-start | bytes 9633796
  15.7 14.1 %collective-permute-start = (f32[784,128]{1,0:T(8,128)S(1)}, f32[784,128]{1,0:T(8,128)S(1)}, u32[]{:S(2)}, u32[]{:S(2)}) collective-permute-start(f32[784,128]{1,0:T(8,128)S(1)} %get-tuple-element.46.refs_5_), channel_id=1, source_target_pairs={{8,0},{16,8},{24,16},{9,1},{17,9},{25,17},{10,2},{18,10},{26,18},{... | collective-permute-start | bytes 1204232 | tf_op jit(solution)/shard_map/ppermute | solution.py:359
  21.9 19.7 %collective-permute-start.5 = (f32[784,128]{1,0:T(8,128)S(1)}, f32[784,128]{1,0:T(8,128)S(1)}, u32[]{:S(2)}, u32[]{:S(2)}) collective-permute-start(f32[784,128]{1,0:T(8,128)S(1)} %get-tuple-element.51.refs_5_), channel_id=1, source_target_pairs={{8,0},{16,8},{24,16},{9,1},{17,9},{25,17},{10,2},{18,10},{26,18},{... | collective-permute-start | bytes 1204232 | tf_op jit(solution)/shard_map/ppermute | solution.py:359
  33.1 15.9 %collective-permute-start.4 = (f32[784,128]{1,0:T(8,128)S(1)}, f32[784,128]{1,0:T(8,128)S(1)}, u32[]{:S(2)}, u32[]{:S(2)}) collective-permute-start(f32[784,128]{1,0:T(8,128)S(1)} %get-tuple-element.52.refs_3_), channel_id=1, source_target_pairs={{8,0},{16,8},{24,16},{9,1},{17,9},{25,17},{10,2},{18,10},{26,18},{... | collective-permute-start | bytes 1204232 | tf_op jit(solution)/shard_map/ppermute | solution.py:359
  36.1 19.7 %collective-permute-start.3 = (f32[784,128]{1,0:T(8,128)S(1)}, f32[784,128]{1,0:T(8,128)S(1)}, u32[]{:S(2)}, u32[]{:S(2)}) collective-permute-start(f32[784,128]{1,0:T(8,128)S(1)} %get-tuple-element.45.refs_3_), channel_id=1, source_target_pairs={{8,0},{16,8},{24,16},{9,1},{17,9},{25,17},{10,2},{18,10},{26,18},{... | collective-permute-start | bytes 1204232 | tf_op jit(solution)/shard_map/ppermute | solution.py:359
  45.1 7.3 %copy-start.1 = (f32[784,128]{1,0:T(8,128)}, f32[784,128]{1,0:T(8,128)S(1)}, u32[]{:S(2)}) copy-start(f32[784,128]{1,0:T(8,128)S(1)} %get-tuple-element.63.refs_6_.refs_5_) | copy-start | bytes 1204228
  45.1 2.5 %collective-permute-start.6 = (f32[9,64,128]{2,1,0:T(8,128)S(1)}, f32[9,64,128]{2,1,0:T(8,128)S(1)}, u32[]{:S(2)}, u32[]{:S(2)}) collective-permute-start(f32[9,64,128]{2,1,0:T(8,128)S(1)} %get-tuple-element.61), channel_id=1, source_target_pairs={{0,1},{1,0},{2,3},{3,2},{4,5},{5,4},{6,7},{7,6},{8,9},{9,8},{10,11... | collective-permute-start | bytes 884744 | tf_op jit(solution)/shard_map/ppermute | solution.py:335
  45.1 2.4 %collective-permute-start.7 = (f32[9,64,128]{2,1,0:T(8,128)S(1)}, f32[9,64,128]{2,1,0:T(8,128)S(1)}, u32[]{:S(2)}, u32[]{:S(2)}) collective-permute-start(f32[9,64,128]{2,1,0:T(8,128)S(1)} %get-tuple-element.62), channel_id=1, source_target_pairs={{0,1},{1,0},{2,3},{3,2},{4,5},{5,4},{6,7},{7,6},{8,9},{9,8},{10,11... | collective-permute-start | bytes 884744 | tf_op jit(solution)/shard_map/ppermute | solution.py:335
  45.6 19.6 %collective-permute-start.2 = (f32[784,128]{1,0:T(8,128)}, f32[784,128]{1,0:T(8,128)}, u32[]{:S(2)}, u32[]{:S(2)}) collective-permute-start(f32[784,128]{1,0:T(8,128)} %get-tuple-element.53.refs_5_), channel_id=1, source_target_pairs={{8,0},{16,8},{24,16},{9,1},{17,9},{25,17},{10,2},{18,10},{26,18},{... | collective-permute-start | bytes 1204232 | tf_op jit(solution)/shard_map/ppermute | solution.py:359
  47.7 17.2 %collective-permute-start.11 = (f32[2,9,64,128]{3,2,1,0:T(8,128)S(1)}, f32[2,9,64,128]{3,2,1,0:T(8,128)S(1)}, u32[]{:S(2)}, u32[]{:S(2)}) collective-permute-start(f32[2,9,64,128]{3,2,1,0:T(8,128)S(1)} %add_turn_3.1.refs_5_.refs_0_), channel_id=1, source_target_pairs={{0,2},{1,3},{6,4},{7,5},{8,10},{9,11},{14,12},{15,13},{16,18},{17,... | collective-permute-start | bytes 1769480 | tf_op jit(solution)/shard_map/ppermute | solution.py:338
  52.4 10.6 %collective-permute-start.10 = (f32[2,9,64,128]{3,2,1,0:T(8,128)S(1)}, f32[2,9,64,128]{3,2,1,0:T(8,128)S(1)}, u32[]{:S(2)}, u32[]{:S(2)}) collective-permute-start(f32[2,9,64,128]{3,2,1,0:T(8,128)S(1)} %get-tuple-element.70), channel_id=1, source_target_pairs={{0,1},{1,0},{2,3},{3,2},{4,5},{5,4},{6,7},{7,6},{8,9},{9,8},{10,11... | collective-permute-start | bytes 1769480 | tf_op jit(solution)/shard_map/ppermute | solution.py:335
  59.0 12.4 %collective-permute-start.9 = (f32[784,128]{1,0:T(8,128)S(1)}, f32[784,128]{1,0:T(8,128)S(1)}, u32[]{:S(2)}, u32[]{:S(2)}) collective-permute-start(f32[784,128]{1,0:T(8,128)S(1)} %get-tuple-element.65.refs_5_), channel_id=1, source_target_pairs={{8,0},{16,8},{24,16},{9,1},{17,9},{25,17},{10,2},{18,10},{26,18},{... | collective-permute-start | bytes 1204232 | tf_op jit(solution)/shard_map/ppermute | solution.py:359
  65.0 15.5 %collective-permute-start.15 = (f32[2,9,64,128]{3,2,1,0:T(8,128)S(1)}, f32[2,9,64,128]{3,2,1,0:T(8,128)S(1)}, u32[]{:S(2)}, u32[]{:S(2)}) collective-permute-start(f32[2,9,64,128]{3,2,1,0:T(8,128)S(1)} %add_turn_2.1.refs_5_), channel_id=1, source_target_pairs={{0,2},{1,3},{6,4},{7,5},{2,6},{3,7},{4,0},{5,1},{8,10},{9,11},{14,... | collective-permute-start | bytes 1769480 | tf_op jit(solution)/shard_map/ppermute | solution.py:338
  74.8 3.9 %collective-permute-start.12 = (f32[9,64,128]{2,1,0:T(8,128)S(1)}, f32[9,64,128]{2,1,0:T(8,128)S(1)}, u32[]{:S(2)}, u32[]{:S(2)}) collective-permute-start(f32[9,64,128]{2,1,0:T(8,128)S(1)} %get-tuple-element.73), channel_id=1, source_target_pairs={{0,1},{1,0},{2,3},{3,2},{4,5},{5,4},{6,7},{7,6},{8,9},{9,8},{10,11... | collective-permute-start | bytes 884744 | tf_op jit(solution)/shard_map/ppermute | solution.py:335
  74.9 3.8 %collective-permute-start.13 = (f32[9,64,128]{2,1,0:T(8,128)S(1)}, f32[9,64,128]{2,1,0:T(8,128)S(1)}, u32[]{:S(2)}, u32[]{:S(2)}) collective-permute-start(f32[9,64,128]{2,1,0:T(8,128)S(1)} %get-tuple-element.74), channel_id=1, source_target_pairs={{0,1},{1,0},{2,3},{3,2},{4,5},{5,4},{6,7},{7,6},{8,9},{9,8},{10,11... | collective-permute-start | bytes 884744 | tf_op jit(solution)/shard_map/ppermute | solution.py:335
  75.4 13.2 %collective-permute-start.8 = (f32[784,128]{1,0:T(8,128)S(1)}, f32[784,128]{1,0:T(8,128)S(1)}, u32[]{:S(2)}, u32[]{:S(2)}) collective-permute-start(f32[784,128]{1,0:T(8,128)S(1)} %get-tuple-element.66.refs_6_), channel_id=1, source_target_pairs={{8,0},{16,8},{24,16},{9,1},{17,9},{25,17},{10,2},{18,10},{26,18},{... | collective-permute-start | bytes 1204232 | tf_op jit(solution)/shard_map/ppermute | solution.py:359
  78.8 9.7 %copy-start.2 = (f32[784,128]{1,0:T(8,128)S(1)}, f32[784,128]{1,0:T(8,128)}, u32[]{:S(2)}) copy-start(f32[784,128]{1,0:T(8,128)} %copy-done.1) | copy-start | bytes 1204228
  78.8 15.5 %collective-permute-start.14 = (f32[2,9,64,128]{3,2,1,0:T(8,128)S(1)}, f32[2,9,64,128]{3,2,1,0:T(8,128)S(1)}, u32[]{:S(2)}, u32[]{:S(2)}) collective-permute-start(f32[2,9,64,128]{3,2,1,0:T(8,128)S(1)} %add_turn_1.1.refs_8_), channel_id=1, source_target_pairs={{0,2},{1,3},{2,0},{3,1},{4,6},{5,7},{6,4},{7,5},{8,10},{9,11},{10,... | collective-permute-start | bytes 1769480 | tf_op jit(solution)/shard_map/ppermute | solution.py:338
  80.6 16.6 %collective-permute-start.16 = (f32[2,9,64,128]{3,2,1,0:T(8,128)S(1)}, f32[2,9,64,128]{3,2,1,0:T(8,128)S(1)}, u32[]{:S(2)}, u32[]{:S(2)}) collective-permute-start(f32[2,9,64,128]{3,2,1,0:T(8,128)S(1)} %add_relay.1), channel_id=1, source_target_pairs={{2,4},{3,5},{4,2},{5,3},{10,12},{11,13},{12,10},{13,11},{18,20},{1... | collective-permute-start | bytes 1769480 | tf_op jit(solution)/shard_map/ppermute | solution.py:338
  92.2 1.6 %collective-permute-start.17 = (f32[9,64,128]{2,1,0:T(8,128)S(1)}, f32[9,64,128]{2,1,0:T(8,128)S(1)}, u32[]{:S(2)}, u32[]{:S(2)}) collective-permute-start(f32[9,64,128]{2,1,0:T(8,128)S(1)} %get-tuple-element.77), channel_id=1, source_target_pairs={{0,1},{1,0},{2,3},{3,2},{4,5},{5,4},{6,7},{7,6},{8,9},{9,8},{10,11... | collective-permute-start | bytes 884744 | tf_op jit(solution)/shard_map/ppermute | solution.py:335
  92.3 2.0 %collective-permute-start.18 = (f32[9,64,128]{2,1,0:T(8,128)S(1)}, f32[9,64,128]{2,1,0:T(8,128)S(1)}, u32[]{:S(2)}, u32[]{:S(2)}) collective-permute-start(f32[9,64,128]{2,1,0:T(8,128)S(1)} %get-tuple-element.78), channel_id=1, source_target_pairs={{0,1},{1,0},{2,3},{3,2},{4,5},{5,4},{6,7},{7,6},{8,9},{9,8},{10,11... | collective-permute-start | bytes 884744 | tf_op jit(solution)/shard_map/ppermute | solution.py:335

commit v5 on v4

--- a/solution.py
+++ b/solution.py
@@ -150,13 +150,14 @@
 
     def filter_grads(k, change, taps):
         turned = turn(change, depth)
-        for a in range(3):
-            high = taps[a * pitch : a * pitch + depth, : 3 * width]
-            low = taps[a * pitch : a * pitch + depth, 3 * width :]
-            grad = jnp.dot(turned, jnp.concatenate([high, low, high], axis=0), preferred_element_type=F32)
-            for b in range(3):
-                tap = grad[:, b * width : (b + 1) * width]
-                sums[k, 3 * a + b] = tap if first else tap + sums_in[k, 3 * a + b]
+        high, low = (
+            jnp.concatenate([taps[a * pitch : a * pitch + depth, 3 * width * h : 3 * width * (h + 1)] for a in range(3)], axis=1)
+            for h in range(2)
+        )
+        grad = jnp.dot(turned, jnp.concatenate([high, low, high], axis=0), preferred_element_type=F32)
+        for t in range(9):
+            tap = grad[:, t * width : (t + 1) * width]
+            sums[k, t] = tap if first else tap + sums_in[k, t]
 
     spread(taps_one, plane[0], pitch, shifted)
     if first:

time: 99.1 us -> 98.7 us (level)
  transfers between devices with their start and end apart: 19 -> 19, of which waited for: 9 -> 9; matrix products, arithmetic and copies ran while one was open for 0% -> 0% of each run, Pallas kernels for 38% -> 39%
where the time goes in v5:
time: 98.7 us; the launch traced here: 98.3 us
  Pallas kernels  44.3 us (45%)
  starting transfers between devices  31.3 us (32%)
  waiting for transfers between devices  21.7 us (22%)
    pallas_call x12, Pallas kernels, step(): pl.pallas_call(functools.partial(step_kernel, dims, k_turn, tick, last, l...  42.4 us
    ppermute x8, starting transfers between devices, on_device(): moved[p] = lax.ppermute(out, 'section', down)  24.3 us
    ppermute x8, waiting for transfers between devices, on_device(): moved[p] = lax.ppermute(out, 'section', down)  15.3 us
    ppermute x4, starting transfers between devices, between(): lax.ppermute(total, 'rep', [(a * shares + n, b * shares + n) for a, b in...  5.19 us
    ppermute x4, waiting for transfers between devices, between(): lax.ppermute(total, 'rep', [(a * shares + n, b * shares + n) for a, b in...  4.88 us
  transfers between devices with their start and end apart: 19, of which 9 were waited for; matrix products, arithmetic and copies ran while one was open for 0% of the time, Pallas kernels for 39%

profile of v5, /device:TPU:20, one launch (start us, length us, event | category | flops | bytes accessed | tf_op | source)
XLA Modules:
  0.0 98.3 jit_solution(11119768246446098863)
XLA Ops:
  0.7 0.1 pad_add_fusion.refs_0_.info
  0.7 4.9 %tick_0_turn_3.1 = (f32[784,128]{1,0:T(8,128)S(1)}, bf16[4,3,384,256]{3,2,1,0:T(8,128)(2,1)S(1)}, f32[2,9,512,128]{3,2,1,0:T(8,128)S(1)}, f32[4,784,128]{2,1,0:T(8,128)S(1)}, f32[2,9,128,128]{3,2,1,0:T(8,128)S(1)}) custom-call(s32[3]{0:T(128)S(1)} %pad_add_fusion.refs_0_.info, f32[4,784,128]{2,1,0:T(8,128)} %bitcast.20, f32[9,512,128]{2,1,0:T(8,128)} %bitcast.18, ...), custom_call_target="tpu_custom_call" | custom-call | flops 10000000000 | bytes 1 | tf_op jit(solution)/shard_map/tick_0_turn_3/pallas_call | solution.py:268
  5.6 3.3 %collective-permute-start.1 = (f32[784,128]{1,0:T(8,128)S(1)}, f32[784,128]{1,0:T(8,128)S(1)}, u32[]{:S(2)}, u32[]{:S(2)}) collective-permute-start(f32[784,128]{1,0:T(8,128)S(1)} %get-tuple-element.44.refs_3_), channel_id=1, source_target_pairs={{8,0},{16,8},{24,16},{9,1},{17,9},{25,17},{10,2},{18,10},{26,18},{... | collective-permute-start | bytes 1204232 | tf_op jit(solution)/shard_map/ppermute | solution.py:360
  8.9 3.2 %tick_0_turn_1.1 = (f32[784,128]{1,0:T(8,128)S(1)}, bf16[4,3,384,256]{3,2,1,0:T(8,128)(2,1)S(1)}, f32[2,9,128,128]{3,2,1,0:T(8,128)S(1)}) custom-call(s32[3]{0:T(128)S(1)} %pad_add_fusion.refs_0_.info, f32[4,784,128]{2,1,0:T(8,128)S(1)} %get-tuple-element.42.refs_1_, f32[2,9,512,128]{3,2,1,0:T(8,128)S(1)} %get-tuple-element.43.refs_2_, ...), custom_call_target="tpu_custom_call" | custom-call | flops 1000000000 | bytes 1 | tf_op jit(solution)/shard_map/tick_0_turn_1/pallas_call | solution.py:268
  12.1 0.0 copy-start
  12.1 3.2 %tick_0_turn_2.1 = (f32[784,128]{1,0:T(8,128)S(1)}, bf16[4,3,384,256]{3,2,1,0:T(8,128)(2,1)S(1)}, f32[2,9,128,128]{3,2,1,0:T(8,128)S(1)}) custom-call(s32[3]{0:T(128)S(1)} %pad_add_fusion.refs_0_.info, f32[4,784,128]{2,1,0:T(8,128)S(1)} %get-tuple-element.42.refs_1_, f32[2,9,512,128]{3,2,1,0:T(8,128)S(1)} %get-tuple-element.43.refs_2_, ...), custom_call_target="tpu_custom_call" | custom-call | flops 1 | bytes 1 | tf_op jit(solution)/shard_map/tick_0_turn_2/pallas_call | solution.py:268
  15.3 2.4 %collective-permute-start = (f32[784,128]{1,0:T(8,128)S(1)}, f32[784,128]{1,0:T(8,128)S(1)}, u32[]{:S(2)}, u32[]{:S(2)}) collective-permute-start(f32[784,128]{1,0:T(8,128)S(1)} %get-tuple-element.46.refs_5_), channel_id=1, source_target_pairs={{8,0},{16,8},{24,16},{9,1},{17,9},{25,17},{10,2},{18,10},{26,18},{... | collective-permute-start | bytes 1204232 | tf_op jit(solution)/shard_map/ppermute | solution.py:360
  17.8 0.7 collective-permute-done.1.refs_1_
  18.5 3.1 %tick_1_turn_3.1 = (f32[784,128]{1,0:T(8,128)S(1)}, f32[2,9,128,128]{3,2,1,0:T(8,128)S(1)}) custom-call(s32[3]{0:T(128)S(1)} %pad_add_fusion.refs_0_.info, f32[784,128]{1,0:T(8,128)S(1)} %collective-permute-done.1.refs_1_, f32[2,4,784,128]{3,2,1,0:T(8,128)S(1)} %bitcast.10, bf16[4,3,384,256]{3,2,1,0:T(8,128)(2,1)S(1)} %get-tuple-element.49.refs_3_, ...), custom_call_target="tpu_custom_call" | custom-call | flops 1 | bytes 1 | tf_op jit(solution)/shard_map/tick_1_turn_3/pallas_call | solution.py:268
  21.6 4.2 %collective-permute-start.5 = (f32[784,128]{1,0:T(8,128)S(1)}, f32[784,128]{1,0:T(8,128)S(1)}, u32[]{:S(2)}, u32[]{:S(2)}) collective-permute-start(f32[784,128]{1,0:T(8,128)S(1)} %get-tuple-element.51.refs_5_), channel_id=1, source_target_pairs={{8,0},{16,8},{24,16},{9,1},{17,9},{25,17},{10,2},{18,10},{26,18},{... | collective-permute-start | bytes 1204232 | tf_op jit(solution)/shard_map/ppermute | solution.py:360
  25.9 3.6 %collective-permute-done.refs_1_ = f32[784,128]{1,0:T(8,128)S(1)} collective-permute-done((f32[784,128]{1,0:T(8,128)S(1)}, f32[784,128]{1,0:T(8,128)S(1)}, u32[]{:S(2)}, u32[]{:S(2)}) %collective-permute-start) | collective-permute-done | bytes 401440 | tf_op jit(solution)/shard_map/ppermute | solution.py:360
  29.4 3.1 %tick_1_turn_2.1 = (f32[784,128]{1,0:T(8,128)S(1)}, f32[2,9,128,128]{3,2,1,0:T(8,128)S(1)}) custom-call(s32[3]{0:T(128)S(1)} %pad_add_fusion.refs_0_.info, f32[784,128]{1,0:T(8,128)S(1)} %collective-permute-done.refs_1_, f32[2,4,784,128]{3,2,1,0:T(8,128)S(1)} %bitcast.11, bf16[4,3,384,256]{3,2,1,0:T(8,128)(2,1)S(1)} %get-tuple-element.47.refs_3_, ...), custom_call_target="tpu_custom_call" | custom-call | flops 1 | bytes 1 | tf_op jit(solution)/shard_map/tick_1_turn_2/pallas_call | solution.py:268
  32.5 3.0 %collective-permute-start.4 = (f32[784,128]{1,0:T(8,128)S(1)}, f32[784,128]{1,0:T(8,128)S(1)}, u32[]{:S(2)}, u32[]{:S(2)}) collective-permute-start(f32[784,128]{1,0:T(8,128)S(1)} %get-tuple-element.52.refs_3_), channel_id=1, source_target_pairs={{8,0},{16,8},{24,16},{9,1},{17,9},{25,17},{10,2},{18,10},{26,18},{... | collective-permute-start | bytes 1204232 | tf_op jit(solution)/shard_map/ppermute | solution.py:360
  35.5 2.1 %collective-permute-start.3 = (f32[784,128]{1,0:T(8,128)S(1)}, f32[784,128]{1,0:T(8,128)S(1)}, u32[]{:S(2)}, u32[]{:S(2)}) collective-permute-start(f32[784,128]{1,0:T(8,128)S(1)} %get-tuple-element.45.refs_3_), channel_id=1, source_target_pairs={{8,0},{16,8},{24,16},{9,1},{17,9},{25,17},{10,2},{18,10},{26,18},{... | collective-permute-start | bytes 1204232 | tf_op jit(solution)/shard_map/ppermute | solution.py:360
  37.6 3.9 %tick_0_turn_0.1 = (f32[784,128]{1,0:T(8,128)}, bf16[4,3,384,256]{3,2,1,0:T(8,128)(2,1)S(1)}, f32[2,9,128,128]{3,2,1,0:T(8,128)S(1)}) custom-call(s32[3]{0:T(128)S(1)} %pad_add_fusion.refs_0_.info, f32[4,784,128]{2,1,0:T(8,128)S(1)} %get-tuple-element.42.refs_1_, f32[2,9,512,128]{3,2,1,0:T(8,128)S(1)} %get-tuple-element.43.refs_2_, ...), custom_call_target="tpu_custom_call" | custom-call | flops 1000000000 | bytes 1 | tf_op jit(solution)/shard_map/tick_0_turn_0/pallas_call | solution.py:268
  41.6 0.0 collective-permute-done.5.refs_1_
  41.6 3.4 %tick_2_turn_3.1 = (f32[784,128]{1,0:T(8,128)S(1)}, f32[2,9,64,128]{3,2,1,0:T(8,128)S(1)}, f32[9,64,128]{2,1,0:T(8,128)S(1)}, f32[9,64,128]{2,1,0:T(8,128)S(1)}) custom-call(s32[3]{0:T(128)S(1)} %pad_add_fusion.refs_0_.info, f32[784,128]{1,0:T(8,128)S(1)} %collective-permute-done.5.refs_1_, f32[2,4,784,128]{3,2,1,0:T(8,128)S(1)} %bitcast.12, ...), custom_call_target="tpu_custom_call" | custom-call | flops 1 | bytes 1 | tf_op jit(solution)/shard_map/tick_2_turn_3/pallas_call | solution.py:268
  45.0 0.1 collective-permute-start.6
  45.1 0.5 collective-permute-start.7
  45.6 1.9 %collective-permute-start.2 = (f32[784,128]{1,0:T(8,128)}, f32[784,128]{1,0:T(8,128)}, u32[]{:S(2)}, u32[]{:S(2)}) collective-permute-start(f32[784,128]{1,0:T(8,128)} %get-tuple-element.53.refs_5_), channel_id=1, source_target_pairs={{8,0},{16,8},{24,16},{9,1},{17,9},{25,17},{10,2},{18,10},{26,18},{... | collective-permute-start | bytes 1204232 | tf_op jit(solution)/shard_map/ppermute | solution.py:360
  47.5 0.1 add_turn_3.1.refs_5_.refs_0_
  47.6 1.3 %collective-permute-start.11 = (f32[2,9,64,128]{3,2,1,0:T(8,128)S(1)}, f32[2,9,64,128]{3,2,1,0:T(8,128)S(1)}, u32[]{:S(2)}, u32[]{:S(2)}) collective-permute-start(f32[2,9,64,128]{3,2,1,0:T(8,128)S(1)} %add_turn_3.1.refs_5_.refs_0_), channel_id=1, source_target_pairs={{0,2},{1,3},{6,4},{7,5},{8,10},{9,11},{14,12},{15,13},{16,18},{17,... | collective-permute-start | bytes 1769480 | tf_op jit(solution)/shard_map/ppermute | solution.py:339
  48.9 3.4 %tick_2_turn_2.1 = (f32[784,128]{1,0:T(8,128)S(1)}, f32[2,9,64,128]{3,2,1,0:T(8,128)S(1)}, f32[2,9,64,128]{3,2,1,0:T(8,128)S(1)}) custom-call(s32[3]{0:T(128)S(1)} %pad_add_fusion.refs_0_.info, f32[784,128]{1,0:T(8,128)S(1)} %collective-permute-done.4.refs_1_, f32[2,4,784,128]{3,2,1,0:T(8,128)S(1)} %bitcast.13, ...), custom_call_target="tpu_custom_call" | custom-call | flops 1000000000 | bytes 1 | tf_op jit(solution)/shard_map/tick_2_turn_2/pallas_call | solution.py:268
  52.3 0.1 collective-permute-start.10
  52.4 2.8 %collective-permute-done.3.refs_1_ = f32[784,128]{1,0:T(8,128)S(1)} collective-permute-done((f32[784,128]{1,0:T(8,128)S(1)}, f32[784,128]{1,0:T(8,128)S(1)}, u32[]{:S(2)}, u32[]{:S(2)}) %collective-permute-start.3) | collective-permute-done | bytes 401440 | tf_op jit(solution)/shard_map/ppermute | solution.py:360
  55.3 3.1 %tick_1_turn_1.1 = (f32[784,128]{1,0:T(8,128)S(1)}, f32[2,9,128,128]{3,2,1,0:T(8,128)S(1)}) custom-call(s32[3]{0:T(128)S(1)} %pad_add_fusion.refs_0_.info, f32[784,128]{1,0:T(8,128)S(1)} %collective-permute-done.3.refs_1_, f32[2,4,784,128]{3,2,1,0:T(8,128)S(1)} %bitcast.14, bf16[4,3,384,256]{3,2,1,0:T(8,128)(2,1)S(1)} %get-tuple-element.56.refs_3_, ...), custom_call_target="tpu_custom_call" | custom-call | flops 99999997952 | bytes 1 | tf_op jit(solution)/shard_map/tick_1_turn_1/pallas_call | solution.py:268
  58.4 3.9 %collective-permute-start.9 = (f32[784,128]{1,0:T(8,128)S(1)}, f32[784,128]{1,0:T(8,128)S(1)}, u32[]{:S(2)}, u32[]{:S(2)}) collective-permute-start(f32[784,128]{1,0:T(8,128)S(1)} %get-tuple-element.65.refs_5_), channel_id=1, source_target_pairs={{8,0},{16,8},{24,16},{9,1},{17,9},{25,17},{10,2},{18,10},{26,18},{... | collective-permute-start | bytes 1204232 | tf_op jit(solution)/shard_map/ppermute | solution.py:360
  62.3 2.5 %collective-permute-done.11.refs_2_ = f32[2,9,64,128]{3,2,1,0:T(8,128)S(1)} collective-permute-done((f32[2,9,64,128]{3,2,1,0:T(8,128)S(1)}, f32[2,9,64,128]{3,2,1,0:T(8,128)S(1)}, u32[]{:S(2)}, u32[]{:S(2)}) %collective-permute-start.11) | collective-permute-done | bytes 589856 | tf_op jit(solution)/shard_map/ppermute | solution.py:339
  64.8 0.1 add_turn_2.1.refs_5_
  64.9 0.3 collective-permute-start.15
  65.2 3.6 %tick_1_turn_0.1 = (f32[784,128]{1,0:T(8,128)S(1)}, f32[2,9,128,128]{3,2,1,0:T(8,128)S(1)}) custom-call(s32[3]{0:T(128)S(1)} %pad_add_fusion.refs_0_.info, f32[784,128]{1,0:T(8,128)} %collective-permute-done.2.refs_1_, f32[2,4,784,128]{3,2,1,0:T(8,128)S(1)} %bitcast.15, bf16[4,3,384,256]{3,2,1,0:T(8,128)(2,1)S(1)} %get-tuple-element.54.refs_3_, ...), custom_call_target="tpu_custom_call" | custom-call | flops 1 | bytes 1 | tf_op jit(solution)/shard_map/tick_1_turn_0/pallas_call | solution.py:268
  68.8 2.2 %collective-permute-done.9.refs_1_ = f32[784,128]{1,0:T(8,128)S(1)} collective-permute-done((f32[784,128]{1,0:T(8,128)S(1)}, f32[784,128]{1,0:T(8,128)S(1)}, u32[]{:S(2)}, u32[]{:S(2)}) %collective-permute-start.9) | collective-permute-done | bytes 401440 | tf_op jit(solution)/shard_map/ppermute | solution.py:360
  71.0 3.4 %tick_2_turn_1.1 = (f32[784,128]{1,0:T(8,128)S(1)}, f32[2,9,64,128]{3,2,1,0:T(8,128)S(1)}, f32[9,64,128]{2,1,0:T(8,128)S(1)}, f32[9,64,128]{2,1,0:T(8,128)S(1)}) custom-call(s32[3]{0:T(128)S(1)} %pad_add_fusion.refs_0_.info, f32[784,128]{1,0:T(8,128)S(1)} %collective-permute-done.9.refs_1_, f32[2,4,784,128]{3,2,1,0:T(8,128)S(1)} %bitcast.16, ...), custom_call_target="tpu_custom_call" | custom-call | flops 1 | bytes 1 | tf_op jit(solution)/shard_map/tick_2_turn_1/pallas_call | solution.py:268
  74.4 0.1 collective-permute-start.12
  74.4 0.5 collective-permute-start.13
  74.9 3.4 %collective-permute-start.8 = (f32[784,128]{1,0:T(8,128)S(1)}, f32[784,128]{1,0:T(8,128)S(1)}, u32[]{:S(2)}, u32[]{:S(2)}) collective-permute-start(f32[784,128]{1,0:T(8,128)S(1)} %get-tuple-element.66.refs_6_), channel_id=1, source_target_pairs={{8,0},{16,8},{24,16},{9,1},{17,9},{25,17},{10,2},{18,10},{26,18},{... | collective-permute-start | bytes 1204232 | tf_op jit(solution)/shard_map/ppermute | solution.py:360
  78.3 0.1 add_turn_1.1.refs_8_
  78.4 1.6 %collective-permute-start.14 = (f32[2,9,64,128]{3,2,1,0:T(8,128)S(1)}, f32[2,9,64,128]{3,2,1,0:T(8,128)S(1)}, u32[]{:S(2)}, u32[]{:S(2)}) collective-permute-start(f32[2,9,64,128]{3,2,1,0:T(8,128)S(1)} %add_turn_1.1.refs_8_), channel_id=1, source_target_pairs={{0,2},{1,3},{2,0},{3,1},{4,6},{5,7},{6,4},{7,5},{8,10},{9,11},{10,... | collective-permute-start | bytes 1769480 | tf_op jit(solution)/shard_map/ppermute | solution.py:339
  80.1 0.1 add_relay.1
  80.1 2.0 %collective-permute-start.16 = (f32[2,9,64,128]{3,2,1,0:T(8,128)S(1)}, f32[2,9,64,128]{3,2,1,0:T(8,128)S(1)}, u32[]{:S(2)}, u32[]{:S(2)}) collective-permute-start(f32[2,9,64,128]{3,2,1,0:T(8,128)S(1)} %add_relay.1), channel_id=1, source_target_pairs={{2,4},{3,5},{4,2},{5,3},{10,12},{11,13},{12,10},{13,11},{18,20},{1... | collective-permute-start | bytes 1769480 | tf_op jit(solution)/shard_map/ppermute | solution.py:339
  82.1 6.0 %collective-permute-done.8.refs_1_ = f32[784,128]{1,0:T(8,128)S(1)} collective-permute-done((f32[784,128]{1,0:T(8,128)S(1)}, f32[784,128]{1,0:T(8,128)S(1)}, u32[]{:S(2)}, u32[]{:S(2)}) %collective-permute-start.8) | collective-permute-done | bytes 401440 | tf_op jit(solution)/shard_map/ppermute | solution.py:360
  88.1 4.2 %tick_2_turn_0.1 = (f32[4,784,128]{2,1,0:T(8,128)}, f32[2,9,64,128]{3,2,1,0:T(8,128)S(1)}, f32[9,64,128]{2,1,0:T(8,128)S(1)}, f32[9,64,128]{2,1,0:T(8,128)S(1)}) custom-call(s32[3]{0:T(128)S(1)} %pad_add_fusion.refs_0_.info, f32[784,128]{1,0:T(8,128)S(1)} %collective-permute-done.8.refs_1_, f32[2,4,784,128]{3,2,1,0:T(8,128)S(1)} %bitcast.17, ...), custom_call_target="tpu_custom_call" | custom-call | flops 1 | bytes 1 | tf_op jit(solution)/shard_map/tick_2_turn_0/pallas_call | solution.py:268
  92.4 0.1 collective-permute-start.17
  92.4 0.5 collective-permute-start.18
  92.9 1.1 %collective-permute-done.17.refs_0_ = f32[9,64,128]{2,1,0:T(8,128)S(1)} collective-permute-done((f32[9,64,128]{2,1,0:T(8,128)S(1)}, f32[9,64,128]{2,1,0:T(8,128)S(1)}, u32[]{:S(2)}, u32[]{:S(2)}) %collective-permute-start.17) | collective-permute-done | bytes 294944 | tf_op jit(solution)/shard_map/ppermute | solution.py:336
  94.0 0.4 collective-permute-done.18.refs_1_
  94.4 2.4 %collective-permute-done.16.relayed = f32[2,9,64,128]{3,2,1,0:T(8,128)S(1)} collective-permute-done((f32[2,9,64,128]{3,2,1,0:T(8,128)S(1)}, f32[2,9,64,128]{3,2,1,0:T(8,128)S(1)}, u32[]{:S(2)}, u32[]{:S(2)}) %collective-permute-start.16) | collective-permute-done | bytes 589856 | tf_op jit(solution)/shard_map/ppermute | solution.py:339
  96.8 1.5 %add_last.1 = (f32[9,64,128]{2,1,0:T(8,128)}, f32[9,64,128]{2,1,0:T(8,128)}) custom-call(s32[3]{0:T(128)S(1)} %pad_add_fusion.refs_0_.info, f32[2,9,64,128]{3,2,1,0:T(8,128)S(1)} %get-tuple-element.76.mine, f32[2,9,64,128]{3,2,1,0:T(8,128)S(1)} %collective-permute-done.14.beside, f32[2,9,64,128]{3,2,1,0:T(8,128)S(1)} %collective-permute-done.16.relayed, ...), custom_call_target="tpu_custom_call" | custom-call | flops 1 | bytes 1 | tf_op jit(solution)/shard_map/add_last/pallas_call | solution.py:394
  (14 shorter events, 0.0 us)
Async XLA Ops:
  5.6 12.9 %collective-permute-start.1 = (f32[784,128]{1,0:T(8,128)S(1)}, f32[784,128]{1,0:T(8,128)S(1)}, u32[]{:S(2)}, u32[]{:S(2)}) collective-permute-start(f32[784,128]{1,0:T(8,128)S(1)} %get-tuple-element.44.refs_3_), channel_id=1, source_target_pairs={{8,0},{16,8},{24,16},{9,1},{17,9},{25,17},{10,2},{18,10},{26,18},{... | collective-permute-start | bytes 1204232 | tf_op jit(solution)/shard_map/ppermute | solution.py:360
  12.1 6.4 %copy-start = (f32[2,4,1,196,512]{4,2,3,1,0:T(1,128)S(1)}, f32[2,4,1,196,512]{4,2,3,1,0:T(1,128)}, u32[]{:S(2)}) copy-start(f32[2,4,1,196,512]{4,2,3,1,0:T(1,128)} %param.5) | copy-start | bytes 9633796
  15.3 14.1 %collective-permute-start = (f32[784,128]{1,0:T(8,128)S(1)}, f32[784,128]{1,0:T(8,128)S(1)}, u32[]{:S(2)}, u32[]{:S(2)}) collective-permute-start(f32[784,128]{1,0:T(8,128)S(1)} %get-tuple-element.46.refs_5_), channel_id=1, source_target_pairs={{8,0},{16,8},{24,16},{9,1},{17,9},{25,17},{10,2},{18,10},{26,18},{... | collective-permute-start | bytes 1204232 | tf_op jit(solution)/shard_map/ppermute | solution.py:360
  21.6 19.9 %collective-permute-start.5 = (f32[784,128]{1,0:T(8,128)S(1)}, f32[784,128]{1,0:T(8,128)S(1)}, u32[]{:S(2)}, u32[]{:S(2)}) collective-permute-start(f32[784,128]{1,0:T(8,128)S(1)} %get-tuple-element.51.refs_5_), channel_id=1, source_target_pairs={{8,0},{16,8},{24,16},{9,1},{17,9},{25,17},{10,2},{18,10},{26,18},{... | collective-permute-start | bytes 1204232 | tf_op jit(solution)/shard_map/ppermute | solution.py:360
  32.5 16.4 %collective-permute-start.4 = (f32[784,128]{1,0:T(8,128)S(1)}, f32[784,128]{1,0:T(8,128)S(1)}, u32[]{:S(2)}, u32[]{:S(2)}) collective-permute-start(f32[784,128]{1,0:T(8,128)S(1)} %get-tuple-element.52.refs_3_), channel_id=1, source_target_pairs={{8,0},{16,8},{24,16},{9,1},{17,9},{25,17},{10,2},{18,10},{26,18},{... | collective-permute-start | bytes 1204232 | tf_op jit(solution)/shard_map/ppermute | solution.py:360
  35.5 19.7 %collective-permute-start.3 = (f32[784,128]{1,0:T(8,128)S(1)}, f32[784,128]{1,0:T(8,128)S(1)}, u32[]{:S(2)}, u32[]{:S(2)}) collective-permute-start(f32[784,128]{1,0:T(8,128)S(1)} %get-tuple-element.45.refs_3_), channel_id=1, source_target_pairs={{8,0},{16,8},{24,16},{9,1},{17,9},{25,17},{10,2},{18,10},{26,18},{... | collective-permute-start | bytes 1204232 | tf_op jit(solution)/shard_map/ppermute | solution.py:360
  45.0 7.3 %copy-start.1 = (f32[784,128]{1,0:T(8,128)}, f32[784,128]{1,0:T(8,128)S(1)}, u32[]{:S(2)}) copy-start(f32[784,128]{1,0:T(8,128)S(1)} %get-tuple-element.63.refs_6_.refs_5_) | copy-start | bytes 1204228
  45.0 2.5 %collective-permute-start.6 = (f32[9,64,128]{2,1,0:T(8,128)S(1)}, f32[9,64,128]{2,1,0:T(8,128)S(1)}, u32[]{:S(2)}, u32[]{:S(2)}) collective-permute-start(f32[9,64,128]{2,1,0:T(8,128)S(1)} %get-tuple-element.61), channel_id=1, source_target_pairs={{0,1},{1,0},{2,3},{3,2},{4,5},{5,4},{6,7},{7,6},{8,9},{9,8},{10,11... | collective-permute-start | bytes 884744 | tf_op jit(solution)/shard_map/ppermute | solution.py:336
  45.1 2.4 %collective-permute-start.7 = (f32[9,64,128]{2,1,0:T(8,128)S(1)}, f32[9,64,128]{2,1,0:T(8,128)S(1)}, u32[]{:S(2)}, u32[]{:S(2)}) collective-permute-start(f32[9,64,128]{2,1,0:T(8,128)S(1)} %get-tuple-element.62), channel_id=1, source_target_pairs={{0,1},{1,0},{2,3},{3,2},{4,5},{5,4},{6,7},{7,6},{8,9},{9,8},{10,11... | collective-permute-start | bytes 884744 | tf_op jit(solution)/shard_map/ppermute | solution.py:336
  45.6 19.6 %collective-permute-start.2 = (f32[784,128]{1,0:T(8,128)}, f32[784,128]{1,0:T(8,128)}, u32[]{:S(2)}, u32[]{:S(2)}) collective-permute-start(f32[784,128]{1,0:T(8,128)} %get-tuple-element.53.refs_5_), channel_id=1, source_target_pairs={{8,0},{16,8},{24,16},{9,1},{17,9},{25,17},{10,2},{18,10},{26,18},{... | collective-permute-start | bytes 1204232 | tf_op jit(solution)/shard_map/ppermute | solution.py:360
  47.6 17.2 %collective-permute-start.11 = (f32[2,9,64,128]{3,2,1,0:T(8,128)S(1)}, f32[2,9,64,128]{3,2,1,0:T(8,128)S(1)}, u32[]{:S(2)}, u32[]{:S(2)}) collective-permute-start(f32[2,9,64,128]{3,2,1,0:T(8,128)S(1)} %add_turn_3.1.refs_5_.refs_0_), channel_id=1, source_target_pairs={{0,2},{1,3},{6,4},{7,5},{8,10},{9,11},{14,12},{15,13},{16,18},{17,... | collective-permute-start | bytes 1769480 | tf_op jit(solution)/shard_map/ppermute | solution.py:339
  52.3 10.0 %collective-permute-start.10 = (f32[2,9,64,128]{3,2,1,0:T(8,128)S(1)}, f32[2,9,64,128]{3,2,1,0:T(8,128)S(1)}, u32[]{:S(2)}, u32[]{:S(2)}) collective-permute-start(f32[2,9,64,128]{3,2,1,0:T(8,128)S(1)} %get-tuple-element.70), channel_id=1, source_target_pairs={{0,1},{1,0},{2,3},{3,2},{4,5},{5,4},{6,7},{7,6},{8,9},{9,8},{10,11... | collective-permute-start | bytes 1769480 | tf_op jit(solution)/shard_map/ppermute | solution.py:336
  58.4 12.6 %collective-permute-start.9 = (f32[784,128]{1,0:T(8,128)S(1)}, f32[784,128]{1,0:T(8,128)S(1)}, u32[]{:S(2)}, u32[]{:S(2)}) collective-permute-start(f32[784,128]{1,0:T(8,128)S(1)} %get-tuple-element.65.refs_5_), channel_id=1, source_target_pairs={{8,0},{16,8},{24,16},{9,1},{17,9},{25,17},{10,2},{18,10},{26,18},{... | collective-permute-start | bytes 1204232 | tf_op jit(solution)/shard_map/ppermute | solution.py:360
  64.9 15.2 %collective-permute-start.15 = (f32[2,9,64,128]{3,2,1,0:T(8,128)S(1)}, f32[2,9,64,128]{3,2,1,0:T(8,128)S(1)}, u32[]{:S(2)}, u32[]{:S(2)}) collective-permute-start(f32[2,9,64,128]{3,2,1,0:T(8,128)S(1)} %add_turn_2.1.refs_5_), channel_id=1, source_target_pairs={{0,2},{1,3},{6,4},{7,5},{2,6},{3,7},{4,0},{5,1},{8,10},{9,11},{14,... | collective-permute-start | bytes 1769480 | tf_op jit(solution)/shard_map/ppermute | solution.py:339
  74.4 4.0 %collective-permute-start.12 = (f32[9,64,128]{2,1,0:T(8,128)S(1)}, f32[9,64,128]{2,1,0:T(8,128)S(1)}, u32[]{:S(2)}, u32[]{:S(2)}) collective-permute-start(f32[9,64,128]{2,1,0:T(8,128)S(1)} %get-tuple-element.73), channel_id=1, source_target_pairs={{0,1},{1,0},{2,3},{3,2},{4,5},{5,4},{6,7},{7,6},{8,9},{9,8},{10,11... | collective-permute-start | bytes 884744 | tf_op jit(solution)/shard_map/ppermute | solution.py:336
  74.4 3.9 %collective-permute-start.13 = (f32[9,64,128]{2,1,0:T(8,128)S(1)}, f32[9,64,128]{2,1,0:T(8,128)S(1)}, u32[]{:S(2)}, u32[]{:S(2)}) collective-permute-start(f32[9,64,128]{2,1,0:T(8,128)S(1)} %get-tuple-element.74), channel_id=1, source_target_pairs={{0,1},{1,0},{2,3},{3,2},{4,5},{5,4},{6,7},{7,6},{8,9},{9,8},{10,11... | collective-permute-start | bytes 884744 | tf_op jit(solution)/shard_map/ppermute | solution.py:336
  74.9 13.2 %collective-permute-start.8 = (f32[784,128]{1,0:T(8,128)S(1)}, f32[784,128]{1,0:T(8,128)S(1)}, u32[]{:S(2)}, u32[]{:S(2)}) collective-permute-start(f32[784,128]{1,0:T(8,128)S(1)} %get-tuple-element.66.refs_6_), channel_id=1, source_target_pairs={{8,0},{16,8},{24,16},{9,1},{17,9},{25,17},{10,2},{18,10},{26,18},{... | collective-permute-start | bytes 1204232 | tf_op jit(solution)/shard_map/ppermute | solution.py:360
  78.4 9.7 %copy-start.2 = (f32[784,128]{1,0:T(8,128)S(1)}, f32[784,128]{1,0:T(8,128)}, u32[]{:S(2)}) copy-start(f32[784,128]{1,0:T(8,128)} %copy-done.1) | copy-start | bytes 1204228
  78.4 16.0 %collective-permute-start.14 = (f32[2,9,64,128]{3,2,1,0:T(8,128)S(1)}, f32[2,9,64,128]{3,2,1,0:T(8,128)S(1)}, u32[]{:S(2)}, u32[]{:S(2)}) collective-permute-start(f32[2,9,64,128]{3,2,1,0:T(8,128)S(1)} %add_turn_1.1.refs_8_), channel_id=1, source_target_pairs={{0,2},{1,3},{2,0},{3,1},{4,6},{5,7},{6,4},{7,5},{8,10},{9,11},{10,... | collective-permute-start | bytes 1769480 | tf_op jit(solution)/shard_map/ppermute | solution.py:339
  80.1 16.6 %collective-permute-start.16 = (f32[2,9,64,128]{3,2,1,0:T(8,128)S(1)}, f32[2,9,64,128]{3,2,1,0:T(8,128)S(1)}, u32[]{:S(2)}, u32[]{:S(2)}) collective-permute-start(f32[2,9,64,128]{3,2,1,0:T(8,128)S(1)} %add_relay.1), channel_id=1, source_target_pairs={{2,4},{3,5},{4,2},{5,3},{10,12},{11,13},{12,10},{13,11},{18,20},{1... | collective-permute-start | bytes 1769480 | tf_op jit(solution)/shard_map/ppermute | solution.py:339
  92.4 1.6 %collective-permute-start.17 = (f32[9,64,128]{2,1,0:T(8,128)S(1)}, f32[9,64,128]{2,1,0:T(8,128)S(1)}, u32[]{:S(2)}, u32[]{:S(2)}) collective-permute-start(f32[9,64,128]{2,1,0:T(8,128)S(1)} %get-tuple-element.77), channel_id=1, source_target_pairs={{0,1},{1,0},{2,3},{3,2},{4,5},{5,4},{6,7},{7,6},{8,9},{9,8},{10,11... | collective-permute-start | bytes 884744 | tf_op jit(solution)/shard_map/ppermute | solution.py:336
  92.4 2.0 %collective-permute-start.18 = (f32[9,64,128]{2,1,0:T(8,128)S(1)}, f32[9,64,128]{2,1,0:T(8,128)S(1)}, u32[]{:S(2)}, u32[]{:S(2)}) collective-permute-start(f32[9,64,128]{2,1,0:T(8,128)S(1)} %get-tuple-element.78), channel_id=1, source_target_pairs={{0,1},{1,0},{2,3},{3,2},{4,5},{5,4},{6,7},{7,6},{8,9},{9,8},{10,11... | collective-permute-start | bytes 884744 | tf_op jit(solution)/shard_map/ppermute | solution.py:336
